TPU v7x, 128 devices: a whole 4x4x4 slice. The times are simulated.
128 devices in a mesh: ctx: 8 (over y, z_hi), shard: 16 (over x, z_lo, core).
Axes of the slice: x: 4, y: 4, z: 4 (z_hi: 2, z_lo: 2; z = z_hi * 2 + z_lo), core: 2. Of those that a mesh axis runs over, the one named last changes fastest.
Arguments:
- tokens: bfloat16 [16, 1024, 2048], P('shard', 'ctx'), may hold values from -6 to 6
- cotangent: bfloat16 [16, 1024, 2048], P('shard', 'ctx'), may hold values from -6 to 6
- lengths: int32 [16], P('shard'), may hold values from 512 to 1024, as said below
- routes: int32 [16, 1024, 4], P('shard', 'ctx'), may hold values from 0 to 5, all different within a row; in each aligned block of 128 rows (0 to 127, 128 to 255, ..., all dimensions but the last counted through in order) at most 112 rows name the same one
- block_order: int32 [16], replicated, may hold values from 0 to 15, as said below
- norm_gains: bfloat16 [2, 2048], P(None, 'shard'), may hold values from 0.5 to 1.5
- qkv_weight: bfloat16 [2048, 6144], P('shard'), may hold values from -0.125 to 0.125
- qkv_bias: bfloat16 [6144], P('shard'), may hold values from -3 to 3
- out_weight: bfloat16 [2048, 2048], P('shard'), may hold values from -0.5 to 0.5
- router: bfloat16 [2048, 6], P('shard'), may hold values from -0.0625 to 0.0625
- shared_gate: bfloat16 [2048], P('shard'), may hold values from -0.125 to 0.125
- ffn_in: bfloat16 [2048, 28160], P('shard'), may hold values from -0.125 to 0.125
- ffn_out: bfloat16 [2048, 14080], P('shard'), may hold values from -0.3125 to 0.3125
Outputs:
- output: bfloat16 [16, 1024, 2048], P('shard', 'ctx')
- input_grad: float32 [16, 1024, 2048], P('shard', 'ctx')
- grad_gains: float32 [2, 2048], P(None, 'shard')
- grad_qkv: float32 [2048, 6144], P('shard')
- grad_bias: float32 [6144], P('shard')
- grad_out: float32 [2048, 2048], P('shard')
- grad_router: float32 [2048, 6], P('shard')
- grad_shared_gate: float32 [2048], P('shard')
- grad_ffn_in: float32 [2048, 28160], P('shard')
- grad_ffn_out: float32 [2048, 14080], P('shard')
Inputs may be any that keep to these rules, and one draw needn't show every extreme that they name: `lengths`: A row is valid when its position is below its sequence's length. `routes`: each token names 4 different experts; among the 128 rows held by one device (aligned blocks of rows) no expert is named by more than 112 tokens. `block_order`: A permutation of 0 to 15; entries 2c and 2c + 1 are some i and 15 - i in either order.
All inputs are finite; a program needn't handle non-finite values.
Results may differ from a plain program's by a relative error of at most 0.03.
Values may be sent and summed in bfloat16 or wider, within the bound.
A program may use at most 704 MiB of HBM per device.

v0:
```python
import jax
import jax.numpy as jnp
from jax import lax
from jax.sharding import PartitionSpec as P

HEAD = 128
HE = 1408
FS = 5632
EXPERTS = 6


highest = lax.Precision.HIGHEST
epsilon = 1e-06
rope_base = 1000000.0


def contract_last(left, right):
    return lax.dot_general(
        left, right, (((1,), (1,)), ((), ())), preferred_element_type=jnp.float32
    )


def contract_first(left, right):
    return lax.dot_general(
        left, right, (((0,), (0,)), ((), ())), preferred_element_type=jnp.float32
    )


def rope_tables(positions):
    half = HEAD // 2
    freqs = rope_base ** (-jnp.arange(half, dtype=jnp.float32) * 2.0 / HEAD)
    phase = positions.astype(jnp.float32)[:, None] * freqs[None, :]
    phase = jnp.concatenate([phase, phase], axis=1)
    return (jnp.cos(phase)[:, None, :], jnp.sin(phase)[:, None, :])


def rotate(values, cosines, sines):
    half = values.shape[-1] // 2
    turned = jnp.concatenate([-values[..., half:], values[..., :half]], axis=-1)
    return values * cosines + turned * sines


def swish(gate):
    return gate * jax.nn.sigmoid(gate)


def swiglu_back(gate_up, grad_act, half):
    gate = gate_up[..., :half]
    upward = gate_up[..., half:]
    squashed = jax.nn.sigmoid(gate)
    grad_gate = grad_act * upward * squashed * (1.0 + gate * (1.0 - squashed))
    grad_up = grad_act * gate * squashed
    return jnp.concatenate([grad_gate, grad_up], axis=-1).astype(jnp.bfloat16)


def normalize(values):
    factor = lax.rsqrt(jnp.mean(values * values, axis=-1, keepdims=True) + epsilon)
    return (values * factor, factor)


def norm_back(grad_normed, normalized, factor, gain):
    scaled = grad_normed * gain
    return factor * (scaled - normalized * jnp.mean(scaled * normalized, axis=-1, keepdims=True))


def local(
    tokens,
    cotangent,
    lengths,
    routes,
    block_order,
    norm_gains,
    qkv_weight,
    qkv_bias,
    out_weight,
    router,
    shared_gate,
    ffn_in,
    ffn_out,
):
    n_ctx = lax.axis_size("ctx")
    n_shard = lax.axis_size("shard")
    rows_dev = tokens.shape[1]
    width = tokens.shape[2]
    seq_len = rows_dev * n_ctx
    block = rows_dev // 2
    heads = width // HEAD
    capacity = rows_dev * 7 // 8
    n_blocks = block_order.shape[0]
    scale = HEAD ** (-0.5)
    place = lax.axis_index("ctx")
    every = jnp.arange(seq_len, dtype=jnp.int32)
    block_ids = every // block
    matches = block_ids[:, None] == jnp.arange(n_blocks, dtype=jnp.int32)[None, :]
    key_pos = jnp.sum(jnp.where(matches, block_order[None, :], 0), axis=1) * block + every % block
    query_pos = lax.dynamic_slice_in_dim(key_pos, place * rows_dev, rows_dev)
    length = lengths[0]
    valid_keys = key_pos < length
    valid_rows = (query_pos < length).astype(jnp.float32)[:, None]
    all_gains, all_qkv, all_bias, all_out, all_router, all_gate = (
        lax.all_gather(norm_gains, "shard", axis=1, tiled=True),
        lax.all_gather(qkv_weight, "shard", axis=0, tiled=True),
        lax.all_gather(qkv_bias, "shard", axis=0, tiled=True),
        lax.all_gather(out_weight, "shard", axis=0, tiled=True),
        lax.all_gather(router, "shard", axis=0, tiled=True),
        lax.all_gather(shared_gate, "shard", axis=0, tiled=True),
    )
    first_gain = all_gains[0].astype(jnp.float32)
    second_gain = all_gains[1].astype(jnp.float32)
    inputs = tokens[0].astype(jnp.float32)
    first_normed, first_factor = normalize(inputs)
    first_low = (first_normed * first_gain).astype(jnp.bfloat16)
    projected = jnp.dot(first_low, all_qkv, preferred_element_type=jnp.float32) + all_bias.astype(
        jnp.float32
    )
    cosines, sines = rope_tables(query_pos)
    query_lin = projected[:, :width].reshape(rows_dev, heads, HEAD)
    key_lin = projected[:, width : 2 * width].reshape(rows_dev, heads, HEAD)
    query_low = rotate(query_lin, cosines, sines).astype(jnp.bfloat16)
    key_low = rotate(key_lin, cosines, sines).astype(jnp.bfloat16)
    value_low = projected[:, 2 * width :].astype(jnp.bfloat16)
    key_all, value_all = (
        lax.all_gather(key_low.reshape(rows_dev, width), "ctx", axis=0, tiled=True),
        lax.all_gather(value_low, "ctx", axis=0, tiled=True),
    )
    key_heads = key_all.reshape(seq_len, heads, HEAD)
    value_heads = value_all.reshape(seq_len, heads, HEAD)
    allowed = ((key_pos[None, :] <= query_pos[:, None]) & valid_keys[None, :])[None]
    scores = (
        jnp.einsum("qhd,khd->hqk", query_low, key_heads, preferred_element_type=jnp.float32) * scale
    )
    masked = jnp.where(allowed, scores, -1e30)
    peak = jnp.max(masked, axis=-1, keepdims=True)
    summed = jnp.sum(jnp.exp(masked - peak), axis=-1, keepdims=True)
    log_total = peak + jnp.log(summed)
    probs = jnp.exp(masked - log_total)
    probs_low = probs.astype(jnp.bfloat16)
    mixed = jnp.einsum("hqk,khd->qhd", probs_low, value_heads, preferred_element_type=jnp.float32)
    mixed_low = mixed.reshape(rows_dev, width).astype(jnp.bfloat16)
    attended = contract_last(mixed_low, all_out)
    residual = inputs + attended
    second_normed, second_factor = normalize(residual)
    second_low = (second_normed * second_gain).astype(jnp.bfloat16)
    second_full = second_low.astype(jnp.float32)
    logits = jnp.dot(second_low, all_router, preferred_element_type=jnp.float32)
    route_ids = routes[0]
    expert_ids = jnp.arange(EXPERTS, dtype=jnp.int32)
    picks = route_ids[:, :, None] == expert_ids[None, None, :]
    picked = picks.astype(jnp.float32)
    chosen = jnp.sum(logits[:, None, :] * picked, axis=-1)
    gates = jax.nn.softmax(chosen, axis=-1)
    weights = jnp.sum(gates[:, :, None] * picked, axis=1)
    sigma = jax.nn.sigmoid(jnp.dot(second_low, all_gate, preferred_element_type=jnp.float32))
    assigned = jnp.sum(picks.astype(jnp.int32), axis=1)
    ranking = jnp.cumsum(assigned, axis=0) - 1
    slot_ids = jnp.arange(capacity, dtype=jnp.int32)
    placing = (assigned.T[:, None, :] == 1) & (ranking.T[:, None, :] == slot_ids[None, :, None])
    dispatch = placing.astype(jnp.float32)
    expert_rows = jnp.einsum(
        "ect,td->ecd", placing.astype(jnp.bfloat16), second_low, preferred_element_type=jnp.float32
    ).astype(jnp.bfloat16)
    piece = lax.all_gather(ffn_in, "shard", axis=0, tiled=True)
    count = piece.shape[0]
    columns = second_low
    expert_columns = expert_rows
    shared_acc = jnp.dot(columns, piece[:, : 2 * FS], preferred_element_type=jnp.float32)
    expert_piece = piece[:, 2 * FS :].reshape(count, EXPERTS, 2 * HE)
    expert_acc = jnp.einsum(
        "ecn,nef->ecf", expert_columns, expert_piece, preferred_element_type=jnp.float32
    )
    shared_gu = shared_acc
    expert_gu = expert_acc
    shared_act = (swish(shared_gu[:, :FS]) * shared_gu[:, FS:]).astype(jnp.bfloat16)
    expert_act = (swish(expert_gu[..., :HE]) * expert_gu[..., HE:]).astype(jnp.bfloat16)
    piece = lax.all_gather(ffn_out, "shard", axis=0, tiled=True)
    count = piece.shape[0]
    shared_part = contract_last(shared_act, piece[:, :FS])
    expert_piece = piece[:, FS:].reshape(count, EXPERTS, HE)
    expert_part = jnp.einsum(
        "ech,neh->ecn", expert_act, expert_piece, preferred_element_type=jnp.float32
    )
    expert_out = expert_part
    combine = dispatch * weights.T[:, None, :]
    routed = jnp.einsum(
        "ect,ecd->td", combine, expert_out, precision=highest, preferred_element_type=jnp.float32
    )
    total = residual + sigma[:, None] * shared_part + routed
    output = (total * valid_rows).astype(jnp.bfloat16)[None]
    grad_y = cotangent[0].astype(jnp.float32) * valid_rows
    grad_sigma = jnp.sum(grad_y * shared_part, axis=-1) * sigma * (1.0 - sigma)
    grad_shared = (grad_y * sigma[:, None]).astype(jnp.bfloat16)
    grad_slots = jnp.einsum(
        "ect,td->ecd", dispatch, grad_y, precision=highest, preferred_element_type=jnp.float32
    )
    slot_weights = jnp.einsum(
        "ect,te->ec", dispatch, weights, precision=highest, preferred_element_type=jnp.float32
    )
    grad_expert = (slot_weights[:, :, None] * grad_slots).astype(jnp.bfloat16)
    slot_dots = jnp.sum(grad_slots * expert_out, axis=-1)
    grad_weights = jnp.einsum(
        "ect,ec->te", dispatch, slot_dots, precision=highest, preferred_element_type=jnp.float32
    )
    grad_gates = jnp.sum(picked * grad_weights[:, None, :], axis=-1)
    grad_chosen = gates * (grad_gates - jnp.sum(gates * grad_gates, axis=-1, keepdims=True))
    grad_logits = jnp.sum(picked * grad_chosen[:, :, None], axis=1)
    piece = lax.all_gather(ffn_out, "shard", axis=0, tiled=True)
    count = piece.shape[0]
    columns = grad_shared
    expert_columns = grad_expert
    shared_acc = jnp.dot(columns, piece[:, :FS], preferred_element_type=jnp.float32)
    expert_piece = piece[:, FS:].reshape(count, EXPERTS, HE)
    expert_acc = jnp.einsum(
        "ecn,neh->ech", expert_columns, expert_piece, preferred_element_type=jnp.float32
    )
    grad_shared_gu = swiglu_back(shared_gu, shared_acc, FS)
    grad_expert_gu = swiglu_back(expert_gu, expert_acc, HE)
    piece = lax.all_gather(ffn_in, "shard", axis=0, tiled=True)
    count = piece.shape[0]
    part = contract_last(grad_shared_gu, piece[:, : 2 * FS])
    expert_piece = piece[:, 2 * FS :].reshape(count, EXPERTS, 2 * HE)
    expert_part = jnp.einsum(
        "ecf,nef->ecn", grad_expert_gu, expert_piece, preferred_element_type=jnp.float32
    )
    part = part + jnp.einsum(
        "ect,ecn->tn", dispatch, expert_part, precision=highest, preferred_element_type=jnp.float32
    )
    grad_second = part
    grad_second = grad_second + jnp.dot(
        grad_logits,
        all_router.astype(jnp.float32).T,
        precision=highest,
        preferred_element_type=jnp.float32,
    )
    grad_second = grad_second + grad_sigma[:, None] * all_gate.astype(jnp.float32)[None, :]
    grad_second_gain = jnp.sum(grad_second * second_normed, axis=0)
    grad_residual = grad_y + norm_back(grad_second, second_normed, second_factor, second_gain)
    grad_attended = grad_residual.astype(jnp.bfloat16)
    grad_mixed = jnp.dot(grad_attended, all_out, preferred_element_type=jnp.float32).astype(
        jnp.bfloat16
    )
    grad_mixed_heads = grad_mixed.reshape(rows_dev, heads, HEAD)
    grad_probs = jnp.einsum(
        "qhd,khd->hqk", grad_mixed_heads, value_heads, preferred_element_type=jnp.float32
    )
    scores_again = (
        jnp.einsum("qhd,khd->hqk", query_low, key_heads, preferred_element_type=jnp.float32) * scale
    )
    probs_again = jnp.exp(jnp.where(allowed, scores_again, -1e30) - log_total)
    centre = jnp.sum(probs_again * grad_probs, axis=-1, keepdims=True)
    grad_scores = (probs_again * (grad_probs - centre)).astype(jnp.bfloat16)
    grad_query = (
        jnp.einsum("hqk,khd->qhd", grad_scores, key_heads, preferred_element_type=jnp.float32)
        * scale
    )
    grad_key_all = (
        jnp.einsum("hqk,qhd->khd", grad_scores, query_low, preferred_element_type=jnp.float32)
        * scale
    )
    grad_value_all = jnp.einsum(
        "hqk,qhd->khd",
        probs_again.astype(jnp.bfloat16),
        grad_mixed_heads,
        preferred_element_type=jnp.float32,
    )
    grad_key, grad_value = (
        lax.psum_scatter(
            grad_key_all.reshape(seq_len, width).astype(jnp.bfloat16),
            "ctx",
            scatter_dimension=0,
            tiled=True,
        ).astype(jnp.float32),
        lax.psum_scatter(
            grad_value_all.reshape(seq_len, width).astype(jnp.bfloat16),
            "ctx",
            scatter_dimension=0,
            tiled=True,
        ).astype(jnp.float32),
    )

    def rope_both(query_part, key_part):
        return (rotate(query_part, cosines, sines), rotate(key_part, cosines, sines))

    unused, rope_pullback = jax.vjp(rope_both, query_lin, key_lin)
    grad_query_lin, grad_key_lin = rope_pullback(
        (grad_query, grad_key.reshape(rows_dev, heads, HEAD))
    )
    grad_projected = jnp.concatenate(
        [
            grad_query_lin.reshape(rows_dev, width),
            grad_key_lin.reshape(rows_dev, width),
            grad_value,
        ],
        axis=1,
    ).astype(jnp.bfloat16)
    grad_bias_local = jnp.sum(grad_projected.astype(jnp.float32), axis=0)
    grad_first = contract_last(grad_projected, all_qkv)
    grad_first_gain = jnp.sum(grad_first * first_normed, axis=0)
    input_grad = (grad_residual + norm_back(grad_first, first_normed, first_factor, first_gain))[
        None
    ]
    owned = width // n_shard
    left_rows = jnp.stack([first_low, grad_attended, second_low, grad_shared], axis=0)
    left_slots = jnp.stack([expert_rows, grad_expert], axis=0).reshape(2 * EXPERTS, capacity, width)
    owned_rows, owned_slots = (
        lax.all_to_all(left_rows, "shard", split_axis=2, concat_axis=1, tiled=True),
        lax.all_to_all(left_slots, "shard", split_axis=2, concat_axis=1, tiled=True),
    )
    expert_gu_major = jnp.transpose(grad_expert_gu, (1, 0, 2))
    expert_act_major = jnp.transpose(expert_act, (1, 0, 2))
    proj_piece = lax.all_gather(grad_projected, "shard", axis=0, tiled=True)
    mixed_piece = lax.all_gather(mixed_low, "shard", axis=0, tiled=True)
    shared_gu_piece = lax.all_gather(grad_shared_gu, "shard", axis=0, tiled=True)
    shared_act_piece = lax.all_gather(shared_act, "shard", axis=0, tiled=True)
    expert_gu_piece = lax.all_gather(expert_gu_major, "shard", axis=0, tiled=True)
    expert_act_piece = lax.all_gather(expert_act_major, "shard", axis=0, tiled=True)
    slot_count = expert_gu_piece.shape[0]
    slot_cols = owned_slots
    slot_cols = slot_cols.reshape(2, EXPERTS, slot_count, owned)
    qkv_acc = contract_first(owned_rows[0], proj_piece)
    out_acc = contract_first(owned_rows[1], mixed_piece)
    in_shared_acc = contract_first(owned_rows[2], shared_gu_piece)
    in_expert_acc = jnp.einsum(
        "ecn,cef->nef", slot_cols[0], expert_gu_piece, preferred_element_type=jnp.float32
    )
    out_shared_acc = contract_first(owned_rows[3], shared_act_piece)
    out_expert_acc = jnp.einsum(
        "ecn,ceh->neh", slot_cols[1], expert_act_piece, preferred_element_type=jnp.float32
    )
    grad_share = jnp.concatenate(
        [
            qkv_acc,
            out_acc,
            in_shared_acc,
            in_expert_acc.reshape(owned, EXPERTS * 2 * HE),
            out_shared_acc,
            out_expert_acc.reshape(owned, EXPERTS * HE),
        ],
        axis=1,
    )
    grad_gains_local = jnp.stack([grad_first_gain, grad_second_gain], axis=0)
    grad_router_local = lax.dot_general(
        second_full,
        grad_logits,
        (((0,), (0,)), ((), ())),
        precision=highest,
        preferred_element_type=jnp.float32,
    )
    grad_gate_local = jnp.dot(
        grad_sigma, second_full, precision=highest, preferred_element_type=jnp.float32
    )
    small_gains, small_bias, small_router, small_gate = (
        lax.psum_scatter(
            grad_gains_local.astype(jnp.bfloat16), "shard", scatter_dimension=1, tiled=True
        ).astype(jnp.float32),
        lax.psum_scatter(
            grad_bias_local.astype(jnp.bfloat16), "shard", scatter_dimension=0, tiled=True
        ).astype(jnp.float32),
        lax.psum_scatter(
            grad_router_local.astype(jnp.bfloat16), "shard", scatter_dimension=0, tiled=True
        ).astype(jnp.float32),
        lax.psum_scatter(
            grad_gate_local.astype(jnp.bfloat16), "shard", scatter_dimension=0, tiled=True
        ).astype(jnp.float32),
    )
    summed_share, grad_gains, grad_bias, grad_router, grad_shared_gate = lax.psum(
        (grad_share, small_gains, small_bias, small_router, small_gate), "ctx"
    )
    fin = ffn_in.shape[1]
    grad_qkv = summed_share[:, : 3 * width]
    grad_out = summed_share[:, 3 * width : 4 * width]
    grad_ffn_in = summed_share[:, 4 * width : 4 * width + fin]
    grad_ffn_out = summed_share[:, 4 * width + fin :]
    return (
        output,
        input_grad,
        grad_gains,
        grad_qkv,
        grad_bias,
        grad_out,
        grad_router,
        grad_shared_gate,
        grad_ffn_in,
        grad_ffn_out,
    )


def solution(mesh):
    placed = (
        P("shard", "ctx", None),
        P("shard", "ctx", None),
        P("shard"),
        P("shard", "ctx", None),
        P(),
        P(None, "shard"),
        P("shard", None),
        P("shard"),
        P("shard", None),
        P("shard", None),
        P("shard"),
        P("shard", None),
        P("shard", None),
    )
    return jax.shard_map(
        local,
        mesh=mesh,
        in_specs=placed,
        out_specs=(
            P("shard", "ctx", None),
            P("shard", "ctx", None),
            P(None, "shard"),
            P("shard", None),
            P("shard"),
            P("shard", None),
            P("shard", None),
            P("shard"),
            P("shard", None),
            P("shard", None),
        ),
        check_vma=False,
    )
```

profile of v0, /device:TPU:2, one launch (start us, length us, event | category | flops | bytes accessed | tf_op | source)
XLA Modules:
  0.0 3965.2 jit_solution(1785046656018731678)
XLA Ops:
  9.3 17.9 all-gather
  47.8 95.2 %all-gather.15.cloned.1.call-done = bf16[2048,6144]{1,0:T(8,128)(2,1)} async-done(((bf16[128,6144]{1,0:T(8,128)(2,1)}), bf16[2048,6144]{1,0:T(8,128)(2,1)}) %all-gather.15.cloned.1.call-update) | async-done | bytes 25165840 | tf_op jit(solution)/shard_map/all_gather | solution.py:102
  196.6 16.7 all_gather.59
  214.7 18.3 all-gather.19.cloned.1.call-done
  249.2 56.1 %all-gather.17.cloned.1.call-done = bf16[1024,2048]{1,0:T(8,128)(2,1)} async-done(((bf16[128,2048]{1,0:T(8,128)(2,1)}), bf16[1024,2048]{1,0:T(8,128)(2,1)}) %all-gather.17.cloned.1.call-update) | async-done | bytes 4194320 | tf_op jit(solution)/shard_map/all_gather | solution.py:124
  312.8 43.8 %all-gather.21.cloned.1.call-done = bf16[2048,2048]{1,0:T(8,128)(2,1)} async-done(((bf16[128,2048]{1,0:T(8,128)(2,1)}), bf16[2048,2048]{1,0:T(8,128)(2,1)}) %all-gather.21.cloned.1.call-update) | async-done | bytes 8388624 | tf_op jit(solution)/shard_map/all_gather | solution.py:104
  365.1 288.5 %all-gather.25.cloned.1.call-done = bf16[2048,14080]{0,1:T(8,128)(2,1)} async-done(((bf16[128,14080]{0,1:T(8,128)(2,1)}), bf16[2048,14080]{0,1:T(8,128)(2,1)}) %all-gather.25.cloned.1.call-update) | async-done | bytes 57671696 | tf_op jit(solution)/shard_map/all_gather | solution.py:175
  653.5 24.5 slice.139
  678.0 548.2 %all-gather.23.cloned.1.call-done = bf16[2048,28160]{0,1:T(8,128)(2,1)} async-done(((bf16[128,28160]{0,1:T(8,128)(2,1)}), bf16[2048,28160]{0,1:T(8,128)(2,1)}) %all-gather.23.cloned.1.call-update) | async-done | bytes 115343376 | tf_op jit(solution)/shard_map/all_gather | solution.py:162
  1226.3 45.3 %slice.136 = bf16[2048,16896]{0,1:T(8,128)(2,1)} slice(bf16[2048,28160]{0,1:T(8,128)(2,1)} %all-gather.23.cloned.1.call-done), slice={[0:2048], [11264:28160]} | slice | bytes 138412032 | tf_op jit(solution)/shard_map/slice | solution.py:167
  1271.6 32.0 fusion.133
  1303.6 18.5 fusion.134
  1330.3 22.7 fusion.2
  1379.1 20.9 multiply_convert_fusion.4
  1400.0 27.5 fusion.21
  1432.4 17.3 fusion.17
  1498.2 65.2 %reduce-scatter.13.cloned.1.call-done = bf16[128,2048]{1,0:T(8,128)(2,1)} async-done(((bf16[1024,2048]{1,0:T(8,128)(2,1)}), bf16[128,2048]{1,0:T(8,128)(2,1)}) %reduce-scatter.13.cloned.1.call-update) | async-done | bytes 524304
  1567.5 84.0 %reduce-scatter.15.cloned.1.call-done = bf16[128,2048]{1,0:T(8,128)(2,1)} async-done(((bf16[1024,2048]{1,0:T(8,128)(2,1)}), bf16[128,2048]{1,0:T(8,128)(2,1)}) %reduce-scatter.15.cloned.1.call-update) | async-done | bytes 524304
  1697.5 24.5 all-to-all-done
  1734.7 140.4 %all-to-all-done.1 = bf16[12,112,2048]{1,0,2:T(8,128)(2,1)} async-done(((bf16[12,112,2048]{1,0,2:T(8,128)(2,1)}), bf16[12,112,2048]{1,0,2:T(8,128)(2,1)}, u32[]{:S(2)}, u32[]{:S(2)}) %all-to-all-start.1) | async-done | bytes 5505056 | tf_op jit(solution)/shard_map/all_to_all | solution.py:306
  1928.1 58.2 %all-gather.29.cloned.1.call-done = bf16[2048,2048]{0,1:T(8,128)(2,1)} async-done(((bf16[128,2048]{0,1:T(8,128)(2,1)}), bf16[2048,2048]{0,1:T(8,128)(2,1)}) %all-gather.29.cloned.1.call-update) | async-done | bytes 8388624 | tf_op jit(solution)/shard_map/all_gather | solution.py:311
  1993.6 148.5 %all-gather.37.cloned.1.call-done = bf16[1792,6,1408]{2,0,1:T(8,128)(2,1)} async-done(((bf16[112,6,1408]{2,0,1:T(8,128)(2,1)}), bf16[1792,6,1408]{2,0,1:T(8,128)(2,1)}) %all-gather.37.cloned.1.call-update) | async-done | bytes 30277648 | tf_op jit(solution)/shard_map/all_gather | solution.py:315
  2142.1 17.3 fusion.136
  2165.1 209.6 %all-gather.31.cloned.1.call-done = bf16[2048,11264]{1,0:T(8,128)(2,1)} async-done(((bf16[128,11264]{1,0:T(8,128)(2,1)}), bf16[2048,11264]{1,0:T(8,128)(2,1)}) %all-gather.31.cloned.1.call-update) | async-done | bytes 46137360 | tf_op jit(solution)/shard_map/all_gather | solution.py:312
  2374.7 21.9 convolution_dynamic-update-slice_fusion
  2396.6 278.2 %all-gather.33.cloned.1.call-done = bf16[1792,6,2816]{2,0,1:T(8,128)(2,1)} async-done(((bf16[112,6,2816]{2,0,1:T(8,128)(2,1)}), bf16[1792,6,2816]{2,0,1:T(8,128)(2,1)}) %all-gather.33.cloned.1.call-update) | async-done | bytes 60555280 | tf_op jit(solution)/shard_map/all_gather | solution.py:314
  2674.7 29.8 fusion.135
  2721.7 77.0 %all-gather.35.cloned.1.call-done = bf16[2048,5632]{1,0:T(8,128)(2,1)} async-done(((bf16[128,5632]{1,0:T(8,128)(2,1)}), bf16[2048,5632]{1,0:T(8,128)(2,1)}) %all-gather.35.cloned.1.call-update) | async-done | bytes 23068688 | tf_op jit(solution)/shard_map/all_gather | solution.py:313
  2823.6 32.1 reduce-scatter.19.cloned.1.call-done
  2856.5 53.3 %all-reduce.7 = (bf16[6144]{0:T(1024)(128)(2,1)S(1)}, bf16[2048]{0:T(1024)(128)(2,1)S(1)}) all-reduce(bf16[6144]{0:T(1024)(128)(2,1)S(1)} %get-tuple-element.26, bf16[2048]{0:T(1024)(128)(2,1)S(1)} %convert_element_type.186), channel_id=5, replica_groups=mesh['ctx'=8,'shard'=16] {'shard'}, use_global_device_ids=true, to_apply=%region_27.28.clone | all-reduce | flops 8192 | bytes 32768
  2918.1 25.1 all-reduce.6
  2943.2 990.8 %all-reduce.10.cloned.1.call-done = f32[128,50432]{1,0:T(8,128)} async-done(((f32[128,50432]{1,0:T(8,128)}), f32[128,50432]{1,0:T(8,128)}) %all-reduce.10.cloned.1.call-update) | async-done | bytes 25821200 | tf_op jit(solution)/shard_map/psum | solution.py:365
  (297 shorter events, 398.4 us)
Async XLA Ops:
  7.2 135.8 %all-gather.15.cloned.1.call-start = ((), (), s32[]{:S(2)}) async-start(), calls=%async_computation.6 | async-start | bytes 26738688 | tf_op jit(solution)/shard_map/all_gather | solution.py:102
  7.9 225.1 %all-gather.19.cloned.1.call-start = ((), (), s32[]{:S(2)}) async-start(), calls=%async_computation.8 | async-start | bytes 4718592 | tf_op jit(solution)/shard_map/all_gather | solution.py:123
  29.6 184.9 %copy-start.24 = (f32[128,128]{0,1:T(8,128)}, f32[128,128]{0,1:T(8,128)S(1)}, u32[]{:S(2)}) copy-start(f32[128,128]{0,1:T(8,128)S(1)} %get-tuple-element.56) | copy-start | bytes 196612
  29.6 184.9 %copy-start.26 = (f32[128,128]{0,1:T(8,128)}, f32[128,128]{0,1:T(8,128)S(1)}, u32[]{:S(2)}) copy-start(f32[128,128]{0,1:T(8,128)S(1)} %get-tuple-element.55) | copy-start | bytes 196612
  47.7 105.3 %copy-start.46 = (f32[128]{0:T(128)}, f32[128]{0:T(128)S(1)}, u32[]{:S(2)}) copy-start(f32[128]{0:T(128)S(1)} %add_rsqrt_fusion.1) | copy-start | bytes 1540
  47.8 105.3 %copy-start.30 = (f32[1,2048]{1,0:T(1,128)}, f32[1,2048]{1,0:T(1,128)S(1)}, u32[]{:S(2)}) copy-start(f32[1,2048]{1,0:T(1,128)S(1)} %get-tuple-element.58) | copy-start | bytes 24580
  47.8 315.2 %copy-start.34 = (f32[1,2048]{1,0:T(1,128)}, f32[1,2048]{1,0:T(1,128)S(1)}, u32[]{:S(2)}) copy-start(f32[1,2048]{1,0:T(1,128)S(1)} %get-tuple-element.57) | copy-start | bytes 24580
  159.9 145.4 %all-gather.17.cloned.1.call-start = ((), (), s32[]{:S(2)}) async-start(), calls=%async_computation.7 | async-start | bytes 4718592 | tf_op jit(solution)/shard_map/all_gather | solution.py:124
  162.1 194.5 %all-gather.21.cloned.1.call-start = ((), (), s32[]{:S(2)}) async-start(), calls=%async_computation.9 | async-start | bytes 8912896 | tf_op jit(solution)/shard_map/all_gather | solution.py:104
  162.7 490.9 %all-gather.25.cloned.1.call-start = ((), (), s32[]{:S(2)}) async-start(), calls=%async_computation.11 | async-start | bytes 61276160 | tf_op jit(solution)/shard_map/all_gather | solution.py:175
  168.6 1057.7 %all-gather.23.cloned.1.call-start = ((), (), s32[]{:S(2)}) async-start(), calls=%async_computation.10 | async-start | bytes 122552320 | tf_op jit(solution)/shard_map/all_gather | solution.py:162
  178.9 1384.5 %reduce-scatter.13.cloned.1.call-start = ((), (), s32[]{:S(2)}) async-start(), calls=%async_computation.19 | async-start | bytes 4718592
  179.9 1247.6 %copy-start.38 = (s32[6,128]{1,0:T(8,128)}, s32[6,128]{1,0:T(8,128)S(1)}, u32[]{:S(2)}) copy-start(s32[6,128]{1,0:T(8,128)S(1)} %copy.147) | copy-start | bytes 9220
  213.3 150.1 %copy-start.28 = (bf16[2048,6]{0,1:T(8,128)(2,1)}, bf16[2048,6]{0,1:T(8,128)(2,1)S(1)}, u32[]{:S(2)}) copy-start(bf16[2048,6]{0,1:T(8,128)(2,1)S(1)} %all_gather.59) | copy-start | bytes 73732
  213.3 1214.2 %copy-start.41 = (pred[6,128]{1,0:T(8,128)(4,1)}, pred[6,128]{1,0:T(8,128)(4,1)S(1)}, u32[]{:S(2)}) copy-start(pred[6,128]{1,0:T(8,128)(4,1)S(1)} %compare_bitcast_fusion) | copy-start | bytes 2308
  214.1 91.2 %copy-start.14 = (pred[128,1024]{1,0:T(8,128)(4,1)}, pred[128,1024]{1,0:T(8,128)(4,1)S(1)}, u32[]{:S(2)}) copy-start(pred[128,1024]{1,0:T(8,128)(4,1)S(1)} %compare_and_fusion) | copy-start | bytes 393220
  363.2 967.1 %copy-start.10 = (bf16[128,2048]{1,0:T(8,128)(2,1)}, bf16[128,2048]{1,0:T(8,128)(2,1)S(1)}, u32[]{:S(2)}) copy-start(bf16[128,2048]{1,0:T(8,128)(2,1)S(1)} %multiply_convert_fusion.9) | copy-start | bytes 1572868
  365.0 906.6 %copy-start.1 = (bf16[6,112,2048]{2,1,0:T(8,128)(2,1)}, bf16[6,112,2048]{2,1,0:T(8,128)(2,1)S(1)}, u32[]{:S(2)}) copy-start(bf16[6,112,2048]{2,1,0:T(8,128)(2,1)S(1)} %convolution_convert_fusion) | copy-start | bytes 8257540
  1477.6 173.9 %reduce-scatter.15.cloned.1.call-start = ((), (), s32[]{:S(2)}) async-start(), calls=%async_computation.20 | async-start | bytes 4718592
  1492.3 421.4 %all-gather.27.cloned.1.call-start = ((), (), s32[]{:S(2)}) async-start(), calls=%async_computation.12 | async-start | bytes 26738688 | tf_op jit(solution)/shard_map/all_gather | solution.py:310
  1655.7 330.6 %all-gather.29.cloned.1.call-start = ((), (), s32[]{:S(2)}) async-start(), calls=%async_computation.13 | async-start | bytes 8912896 | tf_op jit(solution)/shard_map/all_gather | solution.py:311
  1656.2 485.9 %all-gather.37.cloned.1.call-start = ((), (), s32[]{:S(2)}) async-start(), calls=%async_computation.17 | async-start | bytes 32169984 | tf_op jit(solution)/shard_map/all_gather | solution.py:315
  1661.9 712.8 %all-gather.31.cloned.1.call-start = ((), (), s32[]{:S(2)}) async-start(), calls=%async_computation.14 | async-start | bytes 49020928 | tf_op jit(solution)/shard_map/all_gather | solution.py:312
  1665.6 1009.1 %all-gather.33.cloned.1.call-start = ((), (), s32[]{:S(2)}) async-start(), calls=%async_computation.15 | async-start | bytes 64339968 | tf_op jit(solution)/shard_map/all_gather | solution.py:314
  1670.1 1128.6 %all-gather.35.cloned.1.call-start = ((), (), s32[]{:S(2)}) async-start(), calls=%async_computation.16 | async-start | bytes 24510464 | tf_op jit(solution)/shard_map/all_gather | solution.py:313
  1674.2 47.8 %all-to-all-start = ((bf16[4,128,2048]{1,0,2:T(4,128)(2,1)}), bf16[4,128,2048]{1,0,2:T(4,128)(2,1)}, u32[]{:S(2)}, u32[]{:S(2)}) async-start(bf16[4,128,2048]{1,0,2:T(4,128)(2,1)} %copy.156), calls=%async_computation | async-start | bytes 4194304 | tf_op jit(solution)/shard_map/all_to_all | solution.py:305
  1722.0 153.1 %all-to-all-start.1 = ((bf16[12,112,2048]{1,0,2:T(8,128)(2,1)}), bf16[12,112,2048]{1,0,2:T(8,128)(2,1)}, u32[]{:S(2)}, u32[]{:S(2)}) async-start(bf16[12,112,2048]{1,0,2:T(8,128)(2,1)} %copy.161), calls=%async_computation.1 | async-start | bytes 16777216 | tf_op jit(solution)/shard_map/all_to_all | solution.py:306
  1727.7 1128.0 %reduce-scatter.19.cloned.1.call-start = ((), (), s32[]{:S(2)}) async-start(), calls=%async_computation.22 | async-start | bytes 557056
  1729.3 1188.0 %reduce-scatter.17.cloned.1.call-start = ((), (), s32[]{:S(2)}) async-start(), calls=%async_computation.21 | async-start | bytes 557056
  1909.3 2024.6 %all-reduce.10.cloned.1.call-start = ((), (), s32[]{:S(2)}) async-start(), calls=%async_computation.18 | async-start | bytes 51642368 | tf_op jit(solution)/shard_map/psum | solution.py:365
  2714.0 84.7 %copy-start.19 = (bf16[1,16,128,128]{3,2,1,0:T(8,128)(2,1)S(1)}, bf16[1,16,128,128]{3,2,1,0:T(8,128)(2,1)}, u32[]{:S(2)}) copy-start(bf16[1,16,128,128]{3,2,1,0:T(8,128)(2,1)} %copy.163) | copy-start | bytes 1572868
  2714.0 97.4 %slice-start.4 = ((s8[4325376]{0:T(1024)(128)(4,1)}), s8[131072]{0:T(1024)(128)(4,1)S(1)}, s32[]{:S(2)}) async-start(s8[4325376]{0:T(1024)(128)(4,1)} %bitcast.253), calls=%async_computation.27 | async-start | bytes 262144
  (49 other events, 908.3 us)
Sparse Core Ops, SparseCore 0:
  9.7 133.1 all-gather.14
  160.0 72.9 all-gather.18
  235.9 69.3 all-gather.16
  306.9 49.6 all-gather.20
  358.1 295.4 all-gather.24
  655.6 570.6 all-gather.22
  1477.7 85.6 reduce-scatter.12
  1567.8 83.5 reduce-scatter.14
  1655.8 257.8 all-gather.26
  1915.1 71.0 all-gather.28
  1987.9 154.1 all-gather.36
  2144.2 230.4 all-gather.30
  2376.4 298.3 all-gather.32
  2676.3 122.3 all-gather.34
  2800.9 54.7 reduce-scatter.18
  2858.0 59.2 reduce-scatter.16
  2919.8 1014.0 all-reduce.9
where the time goes:
time: 3970 us
  waiting for transfers between devices  3170 us (80%)
  matrix products  360 us (9%)
  local copies, waits for them, and re-layouts  216 us (5%)
  blocking collectives  146 us (4%)
  other arithmetic  43.6 us (1%)
    psum x1, waiting for transfers between devices, local(): lax.psum((grad_share, small_gains, small_bias, small_router, small_gate),...  991 us
    all_gather x1, waiting for transfers between devices, local(): piece = lax.all_gather(ffn_in, 'shard', axis=0, tiled=True)  548 us
    all_gather x1, waiting for transfers between devices, local(): piece = lax.all_gather(ffn_out, 'shard', axis=0, tiled=True)  288 us
    all_gather x1, waiting for transfers between devices, local(): lax.all_gather(expert_gu_major, 'shard', axis=0, tiled=True)  278 us
    all_gather x1, waiting for transfers between devices, local(): lax.all_gather(grad_shared_gu, 'shard', axis=0, tiled=True)  210 us
    unnamed x21, waiting for transfers between devices  188 us
    all_gather x1, waiting for transfers between devices, local(): lax.all_gather(expert_act_major, 'shard', axis=0, tiled=True)  149 us
    all_to_all x1, waiting for transfers between devices, local(): lax.all_to_all(left_slots, 'shard', split_axis=2, concat_axis=1, tiled=True)  140 us
  transfers between devices with their start and end apart: 19, of which 19 were waited for; matrix products, arithmetic and copies ran while one was open for 8% of the time, Pallas kernels for 0%

commit v1 on v0

v1 whole, which is shorter than its diff:
```python
import jax
import jax.numpy as jnp
import numpy as np
from jax import lax
from jax.sharding import PartitionSpec as P

D = 2048
HEAD = 128
HE = 1408
FS = 5632
EXPERTS = 6
FIN = 28160
FOUT = 14080
LANE = 128
SHARED_BLOCKS = FS // LANE
EXPERT_BLOCKS = HE // LANE
HIDDEN_BLOCKS = SHARED_BLOCKS + EXPERTS * EXPERT_BLOCKS

highest = lax.Precision.HIGHEST
epsilon = 1e-06
rope_base = 1000000.0


def contract_last(left, right):
    return lax.dot_general(
        left, right, (((1,), (1,)), ((), ())), preferred_element_type=jnp.float32
    )


def contract_first(left, right):
    return lax.dot_general(
        left, right, (((0,), (0,)), ((), ())), preferred_element_type=jnp.float32
    )


def dot(left, right):
    return jnp.dot(left, right, preferred_element_type=jnp.float32)


def rope_tables(positions):
    half = HEAD // 2
    freqs = rope_base ** (-jnp.arange(half, dtype=jnp.float32) * 2.0 / HEAD)
    phase = positions.astype(jnp.float32)[:, None] * freqs[None, :]
    phase = jnp.concatenate([phase, phase], axis=1)
    return (jnp.cos(phase)[:, None, :], jnp.sin(phase)[:, None, :])


def rotate(values, cosines, sines):
    half = values.shape[-1] // 2
    turned = jnp.concatenate([-values[..., half:], values[..., :half]], axis=-1)
    return values * cosines + turned * sines


def rotate_back(values, cosines, sines):
    half = values.shape[-1] // 2
    scaled = values * sines
    turned = jnp.concatenate([scaled[..., half:], -scaled[..., :half]], axis=-1)
    return values * cosines + turned


def normalize(values):
    factor = lax.rsqrt(jnp.mean(values * values, axis=-1, keepdims=True) + epsilon)
    return (values * factor, factor)


def norm_back(grad_normed, normalized, factor, gain):
    scaled = grad_normed * gain
    return factor * (scaled - normalized * jnp.mean(scaled * normalized, axis=-1, keepdims=True))


def gate_start(block):
    routed = block >= SHARED_BLOCKS
    expert = (block - SHARED_BLOCKS) // EXPERT_BLOCKS
    rest = (block - SHARED_BLOCKS) % EXPERT_BLOCKS
    start = jnp.where(routed, 2 * FS + 2 * HE * expert + LANE * rest, LANE * block)
    return start, jnp.where(routed, HE, FS)


def columns_at(array, starts):
    return jnp.concatenate(
        [lax.dynamic_slice_in_dim(array, start, LANE, axis=1) for start in starts], axis=1
    )


def ag_ctx(value):
    return lax.all_gather(value, "ctx", axis=0, tiled=True)


def rs_ctx(value):
    return lax.psum_scatter(value, "ctx", scatter_dimension=0, tiled=True)


def ag_shard(value):
    return lax.all_gather(value, "shard", axis=0, tiled=True)


def rs_shard(value):
    return lax.psum_scatter(value, "shard", scatter_dimension=0, tiled=True)


def local(
    tokens,
    cotangent,
    lengths,
    routes,
    block_order,
    norm_gains,
    qkv_weight,
    qkv_bias,
    out_weight,
    router,
    shared_gate,
    ffn_in,
    ffn_out,
):
    bf16, f32 = jnp.bfloat16, jnp.float32
    n_ctx = lax.axis_size("ctx")
    n_shard = lax.axis_size("shard")
    rows_dev = tokens.shape[1]
    seq_len = rows_dev * n_ctx
    n_blocks = block_order.shape[0]
    block = seq_len // n_blocks
    heads = D // HEAD // n_ctx
    width = heads * HEAD
    hidden_blocks = -(-HIDDEN_BLOCKS // n_ctx)
    hidden = hidden_blocks * LANE
    scale = HEAD ** (-0.5)
    place = lax.axis_index("ctx")
    owner = lax.axis_index("shard")

    every = jnp.arange(seq_len, dtype=jnp.int32)
    matches = (every // block)[:, None] == jnp.arange(n_blocks, dtype=jnp.int32)[None, :]
    pos = jnp.sum(jnp.where(matches, block_order[None, :], 0), axis=1) * block + every % block
    valid = pos < lengths[0]
    valid_rows = valid.astype(f32)[:, None]
    own_valid = lax.dynamic_slice_in_dim(valid_rows, place * rows_dev, rows_dev)

    inputs = tokens[0].astype(f32)
    picks = routes[0][:, :, None] == jnp.arange(EXPERTS, dtype=jnp.int32)[None, None, :]
    own_assigned = jnp.sum(picks.astype(f32), axis=1)
    x_all = ag_ctx(tokens[0])
    assigned = ag_ctx(own_assigned.astype(bf16)).astype(f32)

    small = jnp.concatenate(
        [
            norm_gains.reshape(-1),
            router.T.reshape(-1),
            shared_gate.reshape(-1),
            qkv_bias.reshape(-1),
        ]
    ).reshape(1, -1)
    small_all = ag_shard(small)
    gains = small_all[:, : 2 * LANE].reshape(n_shard, 2, LANE).transpose(1, 0, 2).reshape(2, D)
    first_gain, second_gain = gains[0].astype(f32), gains[1].astype(f32)
    logit_weights = (
        small_all[:, 2 * LANE : 9 * LANE]
        .reshape(n_shard, EXPERTS + 1, LANE)
        .transpose(0, 2, 1)
        .reshape(D, EXPERTS + 1)
    )
    bias = small_all[:, 9 * LANE :].reshape(3 * D)
    own_bias = jnp.concatenate(
        [lax.dynamic_slice_in_dim(bias, D * i + width * place, width) for i in range(3)]
    ).astype(f32)
    attn_weights = ag_shard(
        jnp.concatenate(
            [
                lax.dynamic_slice_in_dim(qkv_weight, D * i + width * place, width, axis=1)
                for i in range(3)
            ]
            + [lax.dynamic_slice_in_dim(out_weight, width * place, width, axis=1)],
            axis=1,
        )
    )
    w_qkv, w_out = attn_weights[:, : 3 * width], attn_weights[:, 3 * width :]
    blocks = [hidden_blocks * place + j for j in range(hidden_blocks)]
    safe = [jnp.minimum(b, HIDDEN_BLOCKS - 1) for b in blocks]
    starts = [gate_start(b) for b in safe]
    w_in = ag_shard(columns_at(ffn_in, [s for s, _ in starts] + [s + u for s, u in starts]))
    w_down = ag_shard(columns_at(ffn_out, [LANE * b for b in safe]))
    g_all = ag_ctx(cotangent[0])
    g_all = jnp.where(valid_rows > 0, g_all, 0).astype(bf16)

    first_normed_all, _ = normalize(x_all.astype(f32))
    first_all = (first_normed_all * first_gain).astype(bf16)
    projected = dot(first_all, w_qkv) + own_bias
    cosines, sines = rope_tables(pos)
    query = rotate(projected[:, :width].reshape(seq_len, heads, HEAD), cosines, sines).astype(bf16)
    key = rotate(
        projected[:, width : 2 * width].reshape(seq_len, heads, HEAD), cosines, sines
    ).astype(bf16)
    value = projected[:, 2 * width :].astype(bf16).reshape(seq_len, heads, HEAD)
    allowed = ((pos[None, :] <= pos[:, None]) & valid[None, :])[None]
    scores = jnp.einsum("qhd,khd->hqk", query, key, preferred_element_type=f32) * scale
    masked = jnp.where(allowed, scores, -1e30)
    peak = jnp.max(masked, axis=-1, keepdims=True)
    log_total = peak + jnp.log(jnp.sum(jnp.exp(masked - peak), axis=-1, keepdims=True))
    probs = jnp.exp(masked - log_total)
    probs_low = probs.astype(bf16)
    mixed = jnp.einsum("hqk,khd->qhd", probs_low, value, preferred_element_type=f32)
    mixed = mixed.reshape(seq_len, width).astype(bf16)
    attended = rs_ctx(contract_last(mixed, w_out).astype(bf16)).astype(f32)

    residual = inputs + attended
    second_normed, second_factor = normalize(residual)
    second = (second_normed * second_gain).astype(bf16)
    second_all = ag_ctx(second)

    logits = dot(second_all, logit_weights)
    chosen = jnp.where(assigned > 0, logits[:, :EXPERTS], -jnp.inf)
    raised = jnp.exp(chosen - jnp.max(chosen, axis=-1, keepdims=True))
    gates = raised / jnp.sum(raised, axis=-1, keepdims=True)
    sigma = jax.nn.sigmoid(logits[:, EXPERTS:])
    branch_weights = jnp.concatenate([gates, sigma], axis=1)
    block_ids = jnp.stack(blocks)
    branch_of = jnp.where(
        block_ids < SHARED_BLOCKS, EXPERTS, (block_ids - SHARED_BLOCKS) // EXPERT_BLOCKS
    )
    member = (
        (branch_of[None, :] == jnp.arange(EXPERTS + 1, dtype=jnp.int32)[:, None])
        & (block_ids < HIDDEN_BLOCKS)[None, :]
    ).astype(f32)
    block_weights = jnp.dot(branch_weights, member, precision=highest)
    spread = jnp.broadcast_to(block_weights[:, :, None], (seq_len, hidden_blocks, LANE))
    spread = spread.reshape(seq_len, hidden)

    gate = dot(second_all, w_in[:, :hidden])
    upward = dot(second_all, w_in[:, hidden:])
    squashed = jax.nn.sigmoid(gate)
    act = gate * squashed * upward
    act_low = (act * spread).astype(bf16)
    ffn = rs_ctx(contract_last(act_low, w_down).astype(bf16)).astype(f32)
    output = ((residual + ffn) * own_valid).astype(bf16)[None]
    grad_raw = dot(g_all, w_down)
    block_dots = jnp.sum((grad_raw * act).reshape(seq_len, hidden_blocks, LANE), axis=-1)
    branch_dots = rs_ctx(jnp.dot(block_dots, member.T, precision=highest))
    grad_act = grad_raw * spread
    grad_gate = grad_act * upward * squashed * (1.0 + gate * (1.0 - squashed))
    grad_up = grad_act * gate * squashed
    grad_gu = jnp.concatenate([grad_gate, grad_up], axis=1).astype(bf16)
    grad_second = rs_ctx(contract_last(grad_gu, w_in).astype(bf16)).astype(f32)

    own_weights = lax.dynamic_slice_in_dim(branch_weights, place * rows_dev, rows_dev)
    own_gates, own_sigma = own_weights[:, :EXPERTS], own_weights[:, EXPERTS:]
    dots = branch_dots[:, :EXPERTS]
    grad_logits = own_gates * (dots - jnp.sum(own_gates * dots, axis=-1, keepdims=True))
    grad_sigma = branch_dots[:, EXPERTS:] * own_sigma * (1.0 - own_sigma)
    grad_both = jnp.concatenate([grad_logits, grad_sigma], axis=1)
    grad_second = grad_second + lax.dot_general(
        grad_both,
        logit_weights.astype(f32),
        (((1,), (1,)), ((), ())),
        precision=highest,
        preferred_element_type=f32,
    )
    grad_second_gain = jnp.sum(grad_second * second_normed, axis=0)
    own_g = cotangent[0].astype(f32) * own_valid
    grad_residual = own_g + norm_back(grad_second, second_normed, second_factor, second_gain)
    grad_attended = ag_ctx(grad_residual.astype(bf16))

    ffn_share = jnp.concatenate(
        [
            contract_first(second_all, grad_gu).astype(bf16),
            contract_first(g_all, act_low).astype(bf16),
        ],
        axis=1,
    )
    ffn_grads = lax.all_gather(rs_shard(ffn_share), "ctx", axis=0)

    grad_mixed = dot(grad_attended, w_out).astype(bf16).reshape(seq_len, heads, HEAD)
    grad_probs = jnp.einsum("qhd,khd->hqk", grad_mixed, value, preferred_element_type=f32)
    centre = jnp.sum(probs * grad_probs, axis=-1, keepdims=True)
    grad_scores = (probs * (grad_probs - centre)).astype(bf16)
    grad_query = jnp.einsum("hqk,khd->qhd", grad_scores, key, preferred_element_type=f32) * scale
    grad_key = jnp.einsum("hqk,qhd->khd", grad_scores, query, preferred_element_type=f32) * scale
    grad_value = jnp.einsum("hqk,qhd->khd", probs_low, grad_mixed, preferred_element_type=f32)
    grad_projected = jnp.concatenate(
        [
            rotate_back(grad_query, cosines, sines).reshape(seq_len, width),
            rotate_back(grad_key, cosines, sines).reshape(seq_len, width),
            grad_value.reshape(seq_len, width),
        ],
        axis=1,
    ).astype(bf16)
    grad_first = rs_ctx(contract_last(grad_projected, w_qkv).astype(bf16)).astype(f32)
    first_normed, first_factor = normalize(inputs)
    grad_first_gain = jnp.sum(grad_first * first_normed, axis=0)
    input_grad = grad_residual + norm_back(grad_first, first_normed, first_factor, first_gain)
    attn_share = jnp.concatenate(
        [
            contract_first(first_all, grad_projected).astype(bf16),
            contract_first(grad_attended, mixed).astype(bf16),
        ],
        axis=1,
    )
    attn_grads = lax.all_gather(rs_shard(attn_share), "ctx", axis=0)

    grad_bias_own = jnp.sum(grad_projected.astype(f32), axis=0).reshape(3, width)
    grad_bias = lax.dynamic_update_slice(
        jnp.zeros((3, D), f32), grad_bias_own, (0, width * place)
    ).reshape(3 * D)
    second_full = second.astype(f32)
    grad_logit_weights = lax.dot_general(
        grad_both,
        second_full,
        (((0,), (0,)), ((), ())),
        precision=highest,
        preferred_element_type=f32,
    )
    small_grads = jnp.concatenate(
        [
            jnp.stack([grad_first_gain, grad_second_gain])
            .reshape(2, n_shard, LANE)
            .transpose(1, 0, 2)
            .reshape(n_shard, -1),
            grad_logit_weights.reshape(EXPERTS + 1, n_shard, LANE)
            .transpose(1, 0, 2)
            .reshape(n_shard, -1),
            grad_bias.reshape(n_shard, -1),
        ],
        axis=1,
    )
    small_sums = lax.psum(small_grads, ("ctx", "shard"))
    own_small = lax.dynamic_slice_in_dim(small_sums, owner, 1)[0]
    grad_gains = own_small[: 2 * LANE].reshape(2, LANE)
    grad_router = own_small[2 * LANE : 8 * LANE].reshape(EXPERTS, LANE).T
    grad_shared_gate = own_small[8 * LANE : 9 * LANE]
    grad_bias_out = own_small[9 * LANE :]

    grad_qkv = jnp.concatenate(
        [
            attn_grads[p, :, width * i : width * (i + 1)]
            for i in range(3)
            for p in range(n_ctx)
        ],
        axis=1,
    ).astype(f32)
    grad_out = jnp.concatenate(
        [attn_grads[p, :, 3 * width :] for p in range(n_ctx)], axis=1
    ).astype(f32)

    def piece(first, count, offset):
        parts = []
        while count:
            p, j = first // hidden_blocks, first % hidden_blocks
            take = min(count, hidden_blocks - j)
            start = offset + LANE * j
            parts.append(ffn_grads[p, :, start : start + LANE * take])
            first, count = first + take, count - take
        return parts

    spans = [(0, SHARED_BLOCKS)] + [
        (SHARED_BLOCKS + EXPERT_BLOCKS * e, EXPERT_BLOCKS) for e in range(EXPERTS)
    ]
    grad_ffn_in = jnp.concatenate(
        [part for f, n in spans for half in (0, hidden) for part in piece(f, n, half)], axis=1
    ).astype(f32)
    grad_ffn_out = jnp.concatenate(
        [part for f, n in spans for part in piece(f, n, 2 * hidden)], axis=1
    ).astype(f32)
    return (
        output,
        input_grad[None],
        grad_gains,
        grad_qkv,
        grad_bias_out,
        grad_out,
        grad_router,
        grad_shared_gate,
        grad_ffn_in,
        grad_ffn_out,
    )


def solution(mesh):
    placed = (
        P("shard", "ctx", None),
        P("shard", "ctx", None),
        P("shard"),
        P("shard", "ctx", None),
        P(),
        P(None, "shard"),
        P("shard", None),
        P("shard"),
        P("shard", None),
        P("shard", None),
        P("shard"),
        P("shard", None),
        P("shard", None),
    )
    return jax.shard_map(
        local,
        mesh=mesh,
        in_specs=placed,
        out_specs=(
            P("shard", "ctx", None),
            P("shard", "ctx", None),
            P(None, "shard"),
            P("shard", None),
            P("shard"),
            P("shard", None),
            P("shard", None),
            P("shard"),
            P("shard", None),
            P("shard", None),
        ),
        check_vma=False,
    )
```

time: 3970 us -> 1670 us (0.42)
  waiting for transfers between devices: 3170 us -> 1220 us
  matrix products: 360 us -> 168 us
  blocking collectives: 146 us -> 48 us
  local copies, waits for them, and re-layouts: 216 us -> 130 us
    all_gather x12 -> x9, waiting for transfers between devices: 1830 us -> 482 us  [the longest x4 177 us: ag_ctx(): return lax.all_gather(value, 'ctx', axis=0, tiled=True)]
    psum x1, waiting for transfers between devices: 991 us -> 139 us  [local(): small_sums = lax.psum(small_grads, ('ctx', 'shard'))]
    reduce_scatter x0 -> x6, waiting for transfers between devices: none -> 543 us  [the longest x5 310 us: rs_ctx(): return lax.psum_scatter(value, 'ctx', scatter_dimension=0, tiled=True)]
    dot_general x27 -> x16, matrix products: 254 us -> 81.1 us  [the longest x6 60 us: dot(): return jnp.dot(left, right, preferred_element_type=jnp.float32)]
    all_to_all x2 -> x0, waiting for transfers between devices: 165 us -> none  [the longest x1 140 us: local(): lax.all_to_all(left_slots, 'shard', split_axis=2, concat_axis=1, tiled=True)]
    unnamed x21 -> x18, waiting for transfers between devices: 188 us -> 56.5 us
    slice x14 -> x9, local copies, waits for them, and re-layouts: 106 us -> 5.53 us  [the longest x1 1.41 us: local(): grad_router = own_small[2 * LANE:8 * LANE].reshape(EXPERTS, LANE).T]
    unnamed x1 -> x0, blocking collectives: 53.3 us -> none
  transfers between devices with their start and end apart: 19 -> 17, of which waited for: 19 -> 16; matrix products, arithmetic and copies ran while one was open for 8% -> 14% of each run, Pallas kernels for 0% -> 0%
where the time goes in v1:
time: 1670 us; the launch traced here: 1650 us
  waiting for transfers between devices  1220 us (73%)
  matrix products  168 us (10%)
  local copies, waits for them, and re-layouts  130 us (8%)
  other arithmetic  68.5 us (4%)
  blocking collectives  48 us (3%)
  between operations  16.7 us (1%)
    reduce_scatter x5, waiting for transfers between devices, rs_ctx(): return lax.psum_scatter(value, 'ctx', scatter_dimension=0, tiled=True)  310 us
    reduce_scatter x1, waiting for transfers between devices, rs_shard(): return lax.psum_scatter(value, 'shard', scatter_dimension=0, tiled=True)  233 us
    all_gather x4, waiting for transfers between devices, ag_ctx(): return lax.all_gather(value, 'ctx', axis=0, tiled=True)  177 us
    all_gather x3, waiting for transfers between devices, ag_shard(): return lax.all_gather(value, 'shard', axis=0, tiled=True)  146 us
    psum x1, waiting for transfers between devices, local(): small_sums = lax.psum(small_grads, ('ctx', 'shard'))  139 us
    all_gather x1, waiting for transfers between devices, local(): ffn_grads = lax.all_gather(rs_shard(ffn_share), 'ctx', axis=0)  106 us
    unnamed x158, local copies, waits for them, and re-layouts  94.3 us
    dot_general x6, matrix products, dot(): return jnp.dot(left, right, preferred_element_type=jnp.float32)  60 us
  transfers between devices with their start and end apart: 17, of which 16 were waited for; matrix products, arithmetic and copies ran while one was open for 14% of the time, Pallas kernels for 0%

profile of v1, /device:TPU:2, one launch (start us, length us, event | category | flops | bytes accessed | tf_op | source)
XLA Modules:
  0.0 1652.1 jit_solution(12648174695102922056)
XLA Ops:
  10.5 18.3 %all-gather.5 = bf16[16,1,1536]{2,1,0:T(2,128)(2,1)S(1)} all-gather(bf16[1,1,1536]{2,1,0:T(2,128)(2,1)S(1)} %reshape.700), channel_id=3, replica_groups=mesh['ctx'=8,'shard'=16] {'shard'}, dimensions={0}, use_global_device_ids=true | all-gather | bytes 52224 | tf_op jit(solution)/shard_map/all_gather | solution.py:94
  34.2 50.2 %all-gather.26.cloned.1.call-done = bf16[1,1024,2048]{2,1,0:T(8,128)(2,1)} async-done(((bf16[1,128,2048]{2,1,0:T(8,128)(2,1)}), bf16[1,1024,2048]{2,1,0:T(8,128)(2,1)}) %all-gather.26.cloned.1.call-update) | async-done | bytes 4194320 | tf_op jit(solution)/shard_map/all_gather | solution.py:86
  87.5 34.2 %all-gather.16.cloned.1.call-done = bf16[2048,1024]{1,0:T(8,128)(2,1)} async-done(((bf16[128,1024]{1,0:T(8,128)(2,1)}), bf16[2048,1024]{1,0:T(8,128)(2,1)}) %all-gather.16.cloned.1.call-update) | async-done | bytes 4194320 | tf_op jit(solution)/shard_map/all_gather | solution.py:94
  121.7 6.6 fusion.15
  143.0 85.3 %reduce-scatter.10.cloned.1.call-done = bf16[128,2048]{1,0:T(8,128)(2,1)} async-done(((bf16[1024,2048]{1,0:T(8,128)(2,1)}), bf16[128,2048]{1,0:T(8,128)(2,1)}) %reduce-scatter.10.cloned.1.call-update) | async-done | bytes 524304 | tf_op jit(solution)/shard_map/reduce_scatter | solution.py:90
  267.5 29.8 %all_gather.44 = bf16[1024,6]{0,1:T(8,128)(2,1)S(1)} all-gather(bf16[128,6]{0,1:T(8,128)(2,1)S(1)} %convert_reduce_fusion.1), channel_id=1, replica_groups=mesh['ctx'=8,'shard'=16] {'ctx'}, dimensions={0}, use_global_device_ids=true | all-gather | bytes 13824 | tf_op jit(solution)/shard_map/all_gather | solution.py:86
  310.0 8.6 copy.162
  318.6 65.1 %all-gather.20.cloned.1.call-done = bf16[2048,3584]{1,0:T(8,128)(2,1)} async-done(((bf16[128,3584]{1,0:T(8,128)(2,1)}), bf16[2048,3584]{1,0:T(8,128)(2,1)}) %all-gather.20.cloned.1.call-update) | async-done | bytes 14680080 | tf_op jit(solution)/shard_map/all_gather | solution.py:94
  383.7 13.6 fusion.3
  397.4 9.9 fusion.5
  407.2 51.3 %all-gather.28.cloned.1.call-done = bf16[1,1024,2048]{2,1,0:T(8,128)(2,1)} async-done(((bf16[1,128,2048]{2,1,0:T(8,128)(2,1)}), bf16[1,1024,2048]{2,1,0:T(8,128)(2,1)}) %all-gather.28.cloned.1.call-update) | async-done | bytes 4194320 | tf_op jit(solution)/shard_map/all_gather | solution.py:86
  458.6 47.1 %all-gather.22.cloned.1.call-done = bf16[2048,1792]{1,0:T(8,128)(2,1)} async-done(((bf16[128,1792]{1,0:T(8,128)(2,1)}), bf16[2048,1792]{1,0:T(8,128)(2,1)}) %all-gather.22.cloned.1.call-update) | async-done | bytes 7340048 | tf_op jit(solution)/shard_map/all_gather | solution.py:94
  505.7 22.6 %fusion.104 = (f32[1024,1792]{1,0:T(8,128)}, bf16[1024,1792]{1,0:T(8,128)(2,1)}, bf16[1024,1792]{1,0:T(8,128)(2,1)}, bf16[1024,1792]{1,0:T(8,128)(2,1)}) fusion(f32[1024,1792]{1,0:T(8,128)} %fusion.3, f32[1024,1792]{1,0:T(8,128)} %fusion.5, f32[1024,1792]{1,0:T(8,128)} %copy.162, bf16[2048,1792]{1,0:T(8,128)(2,1)} %all-gather.22.cloned.1.call-done, ...), kind=kOutput, calls=%fused_computation.373 | convolution fusion | flops 7553155072 | bytes 51905536 | tf_op jit(solution)/shard_map/dot_general | solution.py:37
  528.3 8.4 copy.164
  541.5 21.6 %fusion.10 = bf16[1024,2048]{1,0:T(8,128)(2,1)} fusion(bf16[2048,3584]{1,0:T(8,128)(2,1)} %all-gather.20.cloned.1.call-done, bf16[1024,1792]{1,0:T(8,128)(2,1)} %get-tuple-element.20, bf16[1024,1792]{1,0:T(8,128)(2,1)} %get-tuple-element.18), kind=kOutput, calls=%fused_computation.29 | convolution fusion | flops 15049162752 | bytes 26214400 | tf_op jit(solution)/shard_map/dot_general | solution.py:25
  563.3 41.7 %reduce-scatter.16.cloned.1.call-done = f32[128,7]{0,1:T(8,128)} async-done(((f32[1024,7]{0,1:T(8,128)}), f32[128,7]{0,1:T(8,128)}) %reduce-scatter.16.cloned.1.call-update) | async-done | bytes 3600 | tf_op jit(solution)/shard_map/reduce_scatter | solution.py:90
  607.1 87.0 %reduce-scatter.14.cloned.1.call-done = bf16[128,2048]{1,0:T(8,128)(2,1)} async-done(((bf16[1024,2048]{1,0:T(8,128)(2,1)}), bf16[128,2048]{1,0:T(8,128)(2,1)}) %reduce-scatter.14.cloned.1.call-update) | async-done | bytes 524304 | tf_op jit(solution)/shard_map/reduce_scatter | solution.py:90
  698.5 70.3 %all-gather.24.cloned.1.call-done = bf16[1024,2048]{1,0:T(8,128)(2,1)} async-done(((bf16[128,2048]{1,0:T(8,128)(2,1)}), bf16[1024,2048]{1,0:T(8,128)(2,1)}) %all-gather.24.cloned.1.call-update) | async-done | bytes 4194320 | tf_op jit(solution)/shard_map/all_gather | solution.py:86
  772.8 6.9 convolution_convert_fusion.7
  791.1 5.0 convolution_convert_fusion.4
  806.8 6.4 copy.213
  813.3 13.1 convolution_convert_fusion.1
  826.3 22.6 %convolution_convert_fusion = bf16[2048,3584]{1,0:T(8,128)(2,1)} fusion(bf16[1024,2048]{1,0:T(8,128)(2,1)} %all-gather.18.cloned.1.call-done, bf16[1024,1792]{1,0:T(8,128)(2,1)} %get-tuple-element.20, bf16[1024,1792]{1,0:T(8,128)(2,1)} %get-tuple-element.18), kind=kOutput, calls=%fused_computation.1 | convolution fusion | flops 15054405632 | bytes 26214400 | tf_op jit(solution)/shard_map/dot_general | solution.py:31
  848.9 19.4 %pad_maximum_fusion = bf16[2048,5376]{1,0:T(8,128)(2,1)} fusion(bf16[2048,1792]{1,0:T(8,128)(2,1)} %convolution_convert_fusion.1, bf16[2048,3584]{1,0:T(8,128)(2,1)} %convolution_convert_fusion), kind=kLoop, calls=%fused_computation | loop fusion | flops 44040192 | bytes 44040192 | tf_op jit(solution)/shard_map/concatenate | solution.py:261
  868.4 12.8 convolution_convert_fusion.2
  886.2 55.1 %reduce-scatter.22.cloned.1.call-done = bf16[128,1024]{1,0:T(8,128)(2,1)} async-done(((bf16[2048,1024]{1,0:T(8,128)(2,1)}), bf16[128,1024]{1,0:T(8,128)(2,1)}) %reduce-scatter.22.cloned.1.call-update) | async-done | bytes 262160
  943.1 232.7 %reduce-scatter.20.cloned.1.call-done = bf16[128,5376]{1,0:T(8,128)(2,1)} async-done(((bf16[2048,5376]{1,0:T(8,128)(2,1)}), bf16[128,5376]{1,0:T(8,128)(2,1)}) %reduce-scatter.20.cloned.1.call-update) | async-done | bytes 1376272 | tf_op jit(solution)/shard_map/reduce_scatter | solution.py:98
  1175.8 96.5 %reduce-scatter.12.cloned.1.call-done = bf16[128,2048]{1,0:T(8,128)(2,1)} async-done(((bf16[1024,2048]{1,0:T(8,128)(2,1)}), bf16[128,2048]{1,0:T(8,128)(2,1)}) %reduce-scatter.12.cloned.1.call-update) | async-done | bytes 524304 | tf_op jit(solution)/shard_map/reduce_scatter | solution.py:90
  1275.9 139.3 %all-reduce.2.cloned.1.call-done = f32[16,1536]{1,0:T(8,128)} async-done(((f32[16,1536]{1,0:T(8,128)}), f32[16,1536]{1,0:T(8,128)}) %all-reduce.2.cloned.1.call-update) | async-done | bytes 98320 | tf_op jit(solution)/shard_map/psum | solution.py:323
  1420.5 52.2 %all-gather.30.cloned.1.call-done = bf16[1024,1024]{0,1:T(8,128)(2,1)} async-done(((bf16[128,1024]{0,1:T(8,128)(2,1)}), bf16[1024,1024]{0,1:T(8,128)(2,1)}) %all-gather.30.cloned.1.call-update) | async-done | bytes 2097168 | tf_op jit(solution)/shard_map/all_gather | solution.py:296
  1500.4 106.2 %all-gather.32.cloned.1.call-done = bf16[1024,5376]{1,0:T(8,128)(2,1)} async-done(((bf16[128,5376]{1,0:T(8,128)(2,1)}), bf16[1024,5376]{1,0:T(8,128)(2,1)}) %all-gather.32.cloned.1.call-update) | async-done | bytes 11010064 | tf_op jit(solution)/shard_map/all_gather | solution.py:268
  1634.9 6.8 convert_element_type.198
  (286 shorter events, 188.9 us)
Async XLA Ops:
  7.2 77.2 %all-gather.26.cloned.1.call-start = ((), (), s32[]{:S(2)}) async-start(), calls=%async_computation.19 | async-start | bytes 4718592 | tf_op jit(solution)/shard_map/all_gather | solution.py:86
  7.9 113.8 %all-gather.16.cloned.1.call-start = ((), (), s32[]{:S(2)}) async-start(), calls=%async_computation.7 | async-start | bytes 4456448 | tf_op jit(solution)/shard_map/all_gather | solution.py:94
  9.7 218.6 %reduce-scatter.10.cloned.1.call-start = ((), (), s32[]{:S(2)}) async-start(), calls=%async_computation.8 | async-start | bytes 4718592 | tf_op jit(solution)/shard_map/reduce_scatter | solution.py:90
  33.1 95.2 %copy-start.23 = (f32[1,16,128]{2,0,1:T(1,128)}, f32[1,16,128]{2,0,1:T(1,128)S(1)}, u32[]{:S(2)}) copy-start(f32[1,16,128]{2,0,1:T(1,128)S(1)} %get-tuple-element.94) | copy-start | bytes 24580
  87.5 40.9 %copy-start.25 = (f32[1024]{0:T(1024)}, f32[1024]{0:T(1024)S(1)}, u32[]{:S(2)}) copy-start(f32[1024]{0:T(1024)S(1)} %add_rsqrt_fusion) | copy-start | bytes 12292
  128.4 5.3 copy-start.14
  142.9 85.4 %copy-start.1 = (bf16[1,128,2048]{2,1,0:T(8,128)(2,1)S(1)}, bf16[1,128,2048]{2,1,0:T(8,128)(2,1)}, u32[]{:S(2)}) copy-start(bf16[1,128,2048]{2,1,0:T(8,128)(2,1)} %param.13) | copy-start | bytes 1572868
  143.0 124.5 %copy-start.27 = (s32[1,128,4]{1,2,0:T(4,128)S(1)}, s32[1,128,4]{1,2,0:T(4,128)}, u32[]{:S(2)}) copy-start(s32[1,128,4]{1,2,0:T(4,128)} %param.16) | copy-start | bytes 6148
  143.0 159.4 %all-gather.18.cloned.1.call-start = ((), (), s32[]{:S(2)}) async-start(), calls=%async_computation.9 | async-start | bytes 4718592 | tf_op jit(solution)/shard_map/all_gather | solution.py:86
  231.7 152.1 %all-gather.20.cloned.1.call-start = ((), (), s32[]{:S(2)}) async-start(), calls=%async_computation.10 | async-start | bytes 15597568 | tf_op jit(solution)/shard_map/all_gather | solution.py:94
  255.0 203.5 %all-gather.28.cloned.1.call-start = ((), (), s32[]{:S(2)}) async-start(), calls=%async_computation.20 | async-start | bytes 4718592 | tf_op jit(solution)/shard_map/all_gather | solution.py:86
  255.6 250.0 %all-gather.22.cloned.1.call-start = ((), (), s32[]{:S(2)}) async-start(), calls=%async_computation.11 | async-start | bytes 7798784 | tf_op jit(solution)/shard_map/all_gather | solution.py:94
  267.3 337.7 %reduce-scatter.16.cloned.1.call-start = ((), (), s32[]{:S(2)}) async-start(), calls=%async_computation.14 | async-start | bytes 36864 | tf_op jit(solution)/shard_map/reduce_scatter | solution.py:90
  383.7 13.7 copy-start.3
  383.7 13.7 copy-start.28
  541.4 152.6 %reduce-scatter.14.cloned.1.call-start = ((), (), s32[]{:S(2)}) async-start(), calls=%async_computation.13 | async-start | bytes 4718592 | tf_op jit(solution)/shard_map/reduce_scatter | solution.py:90
  563.0 131.0 %copy-start.2 = (bf16[128,2048]{1,0:T(8,128)(2,1)S(1)}, bf16[128,2048]{1,0:T(8,128)(2,1)}, u32[]{:S(2)}) copy-start(bf16[128,2048]{1,0:T(8,128)(2,1)} %reduce-scatter.10.cloned.1.call-done) | copy-start | bytes 1572868
  563.0 134.1 %copy-start.4 = (bf16[1,128,2048]{2,1,0:T(8,128)(2,1)S(1)}, bf16[1,128,2048]{2,1,0:T(8,128)(2,1)}, u32[]{:S(2)}) copy-start(bf16[1,128,2048]{2,1,0:T(8,128)(2,1)} %param.14) | copy-start | bytes 1572868
  563.1 205.7 %all-gather.24.cloned.1.call-start = ((), (), s32[]{:S(2)}) async-start(), calls=%async_computation.15 | async-start | bytes 4718592 | tf_op jit(solution)/shard_map/all_gather | solution.py:86
  698.4 185.6 %reduce-scatter.18.cloned.1.call-start = ((), (), s32[]{:S(2)}) async-start(), calls=%async_computation.16 | async-start | bytes 4718592 | tf_op jit(solution)/shard_map/reduce_scatter | solution.py:90
  768.8 10.9 slice-start
  772.7 6.9 slice-start.1
  772.7 6.9 copy-start.15
  796.1 4.6 copy-start.12
  796.1 4.6 copy-start.24
  796.2 4.6 copy-start.26
  796.2 145.1 %reduce-scatter.22.cloned.1.call-start = ((), (), s32[]{:S(2)}) async-start(), calls=%async_computation.23 | async-start | bytes 4456448
  813.2 362.6 %reduce-scatter.20.cloned.1.call-start = ((), (), s32[]{:S(2)}) async-start(), calls=%async_computation.18 | async-start | bytes 23396352 | tf_op jit(solution)/shard_map/reduce_scatter | solution.py:98
  868.3 404.0 %reduce-scatter.12.cloned.1.call-start = ((), (), s32[]{:S(2)}) async-start(), calls=%async_computation.12 | async-start | bytes 4718592 | tf_op jit(solution)/shard_map/reduce_scatter | solution.py:90
  881.2 533.9 %all-reduce.2.cloned.1.call-start = ((), (), s32[]{:S(2)}) async-start(), calls=%async_computation.17 | async-start | bytes 196608 | tf_op jit(solution)/shard_map/psum | solution.py:323
  886.2 586.5 %all-gather.30.cloned.1.call-start = ((), (), s32[]{:S(2)}) async-start(), calls=%async_computation.21 | async-start | bytes 2359296 | tf_op jit(solution)/shard_map/all_gather | solution.py:296
  943.1 663.4 %all-gather.32.cloned.1.call-start = ((), (), s32[]{:S(2)}) async-start(), calls=%async_computation.22 | async-start | bytes 12386304 | tf_op jit(solution)/shard_map/all_gather | solution.py:268
  (16 other events, 29.2 us)
Sparse Core Ops, SparseCore 0:
  10.4 73.9 all-gather.25
  86.7 34.9 all-gather.15
  143.1 85.1 reduce-scatter.9
  231.8 70.4 all-gather.17
  304.5 79.2 all-gather.19
  385.9 72.6 all-gather.27
  460.9 44.7 all-gather.21
  541.5 63.3 reduce-scatter.15
  609.9 84.0 reduce-scatter.13
  698.5 70.2 all-gather.23
  796.3 82.6 reduce-scatter.17
  881.4 59.8 reduce-scatter.21
  943.8 231.9 reduce-scatter.19
  1180.6 91.7 reduce-scatter.11
  1278.2 136.8 all-reduce.1
  1417.8 54.8 all-gather.29
  1474.8 131.6 all-gather.31

commit v2 on v1

v2 whole, which is shorter than its diff:
```python
import jax
import jax.numpy as jnp
from jax import lax
from jax.experimental import pallas as pl
from jax.experimental.pallas import tpu as pltpu
from jax.sharding import PartitionSpec as P

D = 2048
HEAD = 128
HE = 1408
FS = 5632
EXPERTS = 6
FIN = 28160
FOUT = 14080
LANE = 128
SHARED_BLOCKS = FS // LANE
EXPERT_BLOCKS = HE // LANE
HIDDEN_BLOCKS = SHARED_BLOCKS + EXPERTS * EXPERT_BLOCKS

highest = lax.Precision.HIGHEST
epsilon = 1e-06
rope_base = 1000000.0


def contract_last(left, right):
    return lax.dot_general(
        left, right, (((1,), (1,)), ((), ())), preferred_element_type=jnp.float32
    )


def contract_first(left, right):
    return lax.dot_general(
        left, right, (((0,), (0,)), ((), ())), preferred_element_type=jnp.float32
    )


def dot(left, right):
    return jnp.dot(left, right, preferred_element_type=jnp.float32)


def rope_tables(positions):
    half = HEAD // 2
    freqs = rope_base ** (-jnp.arange(half, dtype=jnp.float32) * 2.0 / HEAD)
    phase = positions.astype(jnp.float32)[:, None] * freqs[None, :]
    phase = jnp.concatenate([phase, phase], axis=1)
    return (jnp.cos(phase)[:, None, :], jnp.sin(phase)[:, None, :])


def rotate(values, cosines, sines):
    half = values.shape[-1] // 2
    turned = jnp.concatenate([-values[..., half:], values[..., :half]], axis=-1)
    return values * cosines + turned * sines


def rotate_back(values, cosines, sines):
    half = values.shape[-1] // 2
    scaled = values * sines
    turned = jnp.concatenate([scaled[..., half:], -scaled[..., :half]], axis=-1)
    return values * cosines + turned


def normalize(values):
    factor = lax.rsqrt(jnp.mean(values * values, axis=-1, keepdims=True) + epsilon)
    return (values * factor, factor)


def norm_back(grad_normed, normalized, factor, gain):
    scaled = grad_normed * gain
    return factor * (scaled - normalized * jnp.mean(scaled * normalized, axis=-1, keepdims=True))


def gate_start(block):
    routed = block >= SHARED_BLOCKS
    expert = (block - SHARED_BLOCKS) // EXPERT_BLOCKS
    rest = (block - SHARED_BLOCKS) % EXPERT_BLOCKS
    start = jnp.where(routed, 2 * FS + 2 * HE * expert + LANE * rest, LANE * block)
    return start, jnp.where(routed, HE, FS)


def columns_at(array, starts):
    return jnp.concatenate(
        [lax.dynamic_slice_in_dim(array, start, LANE, axis=1) for start in starts], axis=1
    )


def ag_ctx(value):
    return lax.all_gather(value, "ctx", axis=0, tiled=True)


def ag_shard(value):
    return lax.all_gather(value, "shard", axis=0, tiled=True)


MESH = pl.DeviceIdType.MESH
ANY = pl.BlockSpec(memory_space=pl.ANY)
VMEM = pl.BlockSpec(memory_space=pltpu.VMEM)
N_CTX = 8
CHIPS = 8


def params(number, limit=None):
    return pltpu.CompilerParams(
        collective_id=number, has_side_effects=True, vmem_limit_bytes=limit
    )


def greet(peers):
    semaphore = pltpu.get_barrier_semaphore()
    for peer in peers:
        pl.semaphore_signal(semaphore, inc=1, device_id=peer, device_id_type=MESH)
    pl.semaphore_wait(semaphore, len(peers))


def remote(source, target, sends, arrivals, slot, peer):
    return pltpu.make_async_remote_copy(
        src_ref=source,
        dst_ref=target,
        send_sem=sends.at[slot],
        recv_sem=arrivals.at[slot],
        device_id=peer,
        device_id_type=MESH,
    )


def places_of(axis):
    me = lax.axis_index(axis)
    if axis == "ctx":
        peer = lambda place: {"ctx": place}
    else:
        core, me = lax.rem(me, 2), me // 2
        peer = lambda place: {"shard": 2 * place + core}
    other = me + 1 - 2 * lax.rem(me, 2)
    places = [[lax.rem(base + 2 * k, N_CTX) for k in (0, 1, 3, 2)] for base in (me, other)]
    return places, peer


def by_rows(rows, body):
    step = 16

    def run(i, carry):
        body(pl.ds(pl.multiple_of(i * step, step), step))
        return carry

    lax.fori_loop(0, rows // step, run, 0)


class Gather:
    SEMAPHORES = 9

    def __init__(self, own, out, sends, arrivals):
        self.own, self.out, self.sends, self.arrivals = own, out, sends, arrivals
        self.places, _ = places_of("ctx")
        (self.me, self.up, self.down, self.far), other = self.places
        self.other = other[0]
        self.half = out.shape[1] // 2
        self.started = []

    def _send(self, slot, source, target, place):
        def copy():
            return remote(source(), target(), self.sends, self.arrivals, slot, {"ctx": place})

        copy().start()
        self.started.append(copy)

    def _await(self, slot, ref):
        remote(ref, ref, self.sends, self.arrivals, slot, {"ctx": self.other}).wait_recv()

    def begin(self):
        for slot, place in ((0, self.other), (1, self.up), (2, self.down)):
            self._send(slot, lambda: self.own, lambda: self.out.at[self.me], place)

    def pass_other(self):
        def block():
            return self.out.at[self.other]

        self._await(0, block())
        self._send(3, block, block, self.up)
        self._send(4, block, block, self.down)

    def pass_ring(self, column):
        _, up, down, _ = self.places[column]
        first = 1 + 2 * column
        low, high = pl.ds(0, self.half), pl.ds(self.half, self.half)
        self._await(first, self.out.at[down])
        lower = lambda: self.out.at[down, low]
        self._send(5 + 2 * column, lower, lower, self.up)
        self._await(first + 1, self.out.at[up])
        upper = lambda: self.out.at[up, high]
        self._send(6 + 2 * column, upper, upper, self.down)

    def end(self):
        low, high = pl.ds(0, self.half), pl.ds(self.half, self.half)
        for column in range(2):
            far = self.places[column][3]
            self._await(5 + 2 * column, self.out.at[far, low])
            self._await(6 + 2 * column, self.out.at[far, high])
        for copy in self.started:
            copy().wait_send()


class Reduce:
    SEMAPHORES = 13

    @staticmethod
    def scratch(rows, width, across=2):
        return [
            pltpu.VMEM((4, rows // 2, width), jnp.bfloat16),
            pltpu.VMEM((4, rows, width), jnp.bfloat16),
            pltpu.VMEM((across, rows, width), jnp.bfloat16),
            pltpu.SemaphoreType.DMA((Reduce.SEMAPHORES,)),
            pltpu.SemaphoreType.DMA((Reduce.SEMAPHORES,)),
        ]

    def __init__(self, parts, held, passing, near, across, sends, arrivals, axis="ctx"):
        self.parts, self.held = parts, held
        self.passing, self.near, self.across = passing, near, across
        self.sends, self.arrivals = sends, arrivals
        self.places, self.peer = places_of(axis)
        _, self.up, self.down, _ = self.places[0]
        self.other = self.places[1][0]
        self.rows, self.width = near.shape[1], near.shape[2]
        self.half = self.rows // 2
        self.started = []

    def _send(self, slot, source, target, place):
        def copy():
            return remote(source(), target(), self.sends, self.arrivals, slot, self.peer(place))

        copy().start()
        self.started.append(copy)

    def _await(self, slot, ref):
        remote(ref, ref, self.sends, self.arrivals, slot, self.peer(self.other)).wait_recv()

    def begin(self):
        self.send_far()
        self.send_near(0)
        self.send_near(1)

    def send_far(self):
        for column in (1, 0):
            self._send_far(column)

    def _send_far(self, column):
        low, high = pl.ds(0, self.half), pl.ds(self.half, self.half)
        far = self.places[column][3]
        slot, a, b = 6 * column, 2 * column, 2 * column + 1
        parts, passing = self.parts, self.passing
        self._send(slot, lambda: parts.at[far, low], lambda: passing.at[a], self.up)
        self._send(slot + 1, lambda: parts.at[far, high], lambda: passing.at[b], self.down)

    def send_near(self, side):
        for column in (1, 0):
            self._send_near(column, side)

    def _send_near(self, column, side):
        half = pl.ds((1 - side) * self.half, self.half)
        toward, place = self.places[column][1 + side], (self.up, self.down)[side]
        index, parts, near = 2 * column + side, self.parts, self.near
        self._send(
            6 * column + 2 + side,
            lambda: parts.at[toward, half],
            lambda: near.at[index, half],
            place,
        )

    def pass_side(self, side):
        for column in (1, 0):
            self._pass_side(column, side)

    def _loop(self, rows, body):
        step = 16

        def run(i, carry):
            body(pl.multiple_of(i * step, step), step)
            return carry

        lax.fori_loop(0, rows // step, run, 0)

    def pass_on(self, column):
        self._pass_side(column, 0)
        self._pass_side(column, 1)

    def _pass_side(self, column, side):
        slot, index, start = 6 * column, 2 * column + side, side * self.half
        toward, place = self.places[column][1 + side], (self.up, self.down)[side]
        passing, near, held = self.passing, self.near, self.held
        self._await(slot + side, passing.at[index])

        def add(row, step):
            there = pl.ds(row, step)
            total = passing[index, there, :].astype(jnp.float32)
            total = total + held[toward, pl.ds(start + row, step), :].astype(jnp.float32)
            passing[index, there, :] = total.astype(jnp.bfloat16)

        self._loop(self.half, add)
        target = pl.ds(start, self.half)
        self._send(
            slot + 4 + side, lambda: passing.at[index], lambda: near.at[index, target], place
        )

    def _near(self, column):
        low, high = pl.ds(0, self.half), pl.ds(self.half, self.half)
        slot = 6 * column
        self._await(slot + 2, self.near.at[2 * column, high])
        self._await(slot + 3, self.near.at[2 * column + 1, low])
        self._await(slot + 4, self.near.at[2 * column, low])
        self._await(slot + 5, self.near.at[2 * column + 1, high])

    def _sum(self, column, there):
        place = self.places[column][0]
        total = self.held[place, there, :].astype(jnp.float32)
        total = total + self.near[2 * column, there, :].astype(jnp.float32)
        return total + self.near[2 * column + 1, there, :].astype(jnp.float32)

    def cross(self):
        self._near(1)
        place, held, across = self.places[1][0], self.held, self.across
        if across.shape[0] == 1:
            kept = lambda: held.at[place]
        else:
            kept = lambda: across.at[1]

        def add(row, step):
            there = pl.ds(row, step)
            kept()[there, :] = self._sum(1, there).astype(jnp.bfloat16)

        self._loop(self.rows, add)
        self._send(12, kept, lambda: across.at[0], self.other)

    def ready(self):
        self._near(0)
        self._await(12, self.across.at[0])

    def total(self, there):
        return self._sum(0, there) + self.across[0, there, :].astype(jnp.float32)

    def end(self):
        for copy in self.started:
            copy().wait_send()


class Spread:
    SEMAPHORES = 7 + 8

    def __init__(self, own, out, sends, arrivals):
        self.own, self.out, self.sends, self.arrivals = own, out, sends, arrivals
        self.me = lax.axis_index("shard")
        self.core, self.chip = lax.rem(self.me, 2), self.me // 2
        self.mate = {"shard": self.me + 1 - 2 * self.core}
        self.started = []

    def _send(self, slot, source, target, peer):
        copy = remote(source, target, self.sends, self.arrivals, slot, peer)
        copy.start()
        self.started.append(copy)

    def _await(self, slot, ref):
        remote(ref, ref, self.sends, self.arrivals, slot, self.mate).wait_recv()

    def _from(self, k, core):
        return self.out.at[2 * lax.rem(self.chip + CHIPS - k, CHIPS) + core]

    def peers(self):
        return [self.mate] + [
            {"shard": 2 * lax.rem(self.chip + k, CHIPS) + self.core} for k in range(1, CHIPS)
        ]

    def begin(self):
        target = self.out.at[self.me]
        for k in range(1, CHIPS):
            peer = {"shard": 2 * lax.rem(self.chip + k, CHIPS) + self.core}
            self._send(k - 1, self.own, target, peer)
        self._send(7, self.own, target, self.mate)

    def hand_on(self):
        for k in range(1, CHIPS):
            block = self._from(k, self.core)
            self._await(k - 1, block)
            self._send(7 + k, block, block, self.mate)

    def end(self):
        for k in range(CHIPS):
            self._await(7 + k, self._from(k, 1 - self.core))
        for copy in self.started:
            copy.wait_send()


def front(block, qkv_weight, out_weight, small):
    rows, width = qkv_weight.shape[0], out_weight.shape[1] // N_CTX
    n_shard = out_weight.shape[1] // rows

    def kernel(
        block, qkv_weight, out_weight, small, x_all, weights, small_all, staged, loads, local, *scratch
    ):
        gather = Gather(block, x_all, *scratch[0:2])
        spread = Spread(staged, weights, *scratch[2:4])
        spread_small = Spread(small, small_all, *scratch[4:6])
        place = gather.me
        loaded = [
            pltpu.make_async_copy(
                qkv_weight.at[:, pl.ds(pl.multiple_of(width * N_CTX * i + width * place, width), width)],
                staged.at[:, width * i : width * (i + 1)],
                loads.at[i],
            )
            for i in range(3)
        ] + [
            pltpu.make_async_copy(
                out_weight.at[:, pl.ds(pl.multiple_of(width * place, width), width)],
                staged.at[:, 3 * width :],
                loads.at[3],
            )
        ]
        for copy in loaded:
            copy.start()
        greet([{"ctx": p} for p in (gather.other, gather.up, gather.down)] + spread.peers())
        gather.begin()
        spread_small.begin()
        for copy in loaded:
            copy.wait()
        spread.begin()
        kept = [
            pltpu.make_async_copy(source, target, local.at[k])
            for k, (source, target) in enumerate(
                (
                    (block, x_all.at[place]),
                    (staged, weights.at[spread.me]),
                    (small, small_all.at[spread.me]),
                )
            )
        ]
        for copy in kept:
            copy.start()
        gather.pass_other()
        spread_small.hand_on()
        gather.pass_ring(0)
        spread.hand_on()
        gather.pass_ring(1)
        for copy in kept:
            copy.wait()
        spread_small.end()
        spread.end()
        gather.end()

    bf16 = jnp.bfloat16
    return pl.pallas_call(
        kernel,
        out_shape=(
            jax.ShapeDtypeStruct((N_CTX,) + block.shape, bf16),
            jax.ShapeDtypeStruct((n_shard, rows, 4 * width), bf16),
            jax.ShapeDtypeStruct((n_shard,) + small.shape, bf16),
        ),
        in_specs=[ANY] * 4,
        out_specs=(ANY, ANY, ANY),
        scratch_shapes=[
            pltpu.VMEM((rows, 4 * width), bf16),
            pltpu.SemaphoreType.DMA((4,)),
            pltpu.SemaphoreType.DMA((3,)),
        ]
        + [pltpu.SemaphoreType.DMA((Gather.SEMAPHORES,))] * 2
        + [pltpu.SemaphoreType.DMA((Spread.SEMAPHORES,))] * 4,
        compiler_params=params(0),
        name="front",
    )(block, qkv_weight, out_weight, small)


def middle(parts, inputs, gain):
    _, rows, width = parts.shape

    def kernel(parts, inputs, gain, residual, out, own, local, *scratch):
        reduce_scratch, gather_scratch = scratch[:5], scratch[5:]
        reduce = Reduce(parts, parts, *reduce_scratch)
        gather = Gather(own, out, *gather_scratch)
        greet([{"ctx": p} for p in (gather.other, gather.up, gather.down)])
        reduce.begin()
        reduce.pass_on(1)
        reduce.pass_on(0)
        reduce.cross()
        reduce.ready()

        def norm(there):
            total = inputs[there, :].astype(jnp.float32) + reduce.total(there)
            residual[there, :] = total
            normed, _ = normalize(total)
            own[there, :] = (normed * gain[...]).astype(jnp.bfloat16)

        by_rows(rows, norm)
        gather.begin()
        copy = pltpu.make_async_copy(own, out.at[gather.me], local)
        copy.start()
        gather.pass_other()
        gather.pass_ring(0)
        gather.pass_ring(1)
        reduce.end()
        copy.wait()
        gather.end()

    return pl.pallas_call(
        kernel,
        out_shape=(
            jax.ShapeDtypeStruct((rows, width), jnp.float32),
            jax.ShapeDtypeStruct((N_CTX, rows, width), jnp.bfloat16),
        ),
        in_specs=[VMEM, VMEM, VMEM],
        out_specs=(VMEM, ANY),
        scratch_shapes=[pltpu.VMEM((rows, width), jnp.bfloat16), pltpu.SemaphoreType.DMA]
        + Reduce.scratch(rows, width)
        + [pltpu.SemaphoreType.DMA((Gather.SEMAPHORES,))] * 2,
        compiler_params=params(1, 40 << 20),
        name="middle",
    )(parts, inputs, gain)


def feed_forward(second, grad_out, assigned, w_in, w_down, logit_weights, logit_rows, member, residual, own_grad, own_valid, gain):
    _, rows, width = second.shape
    seq = rows * N_CTX
    hidden = w_down.shape[1]
    lanes = logit_weights.shape[1]
    pair = 2 * rows
    tile = 256
    f32, bf16 = jnp.float32, jnp.bfloat16

    def kernel(
        second, grad_out, assigned, w_in, w_down, logit_weights, logit_rows, member,
        residual, own_grad, own_valid, gain,
        grad_residual, output, grad_gain, grad_logits, act_out, grad_gu_out,
        second_held, grad_held, in_held, down_held, act, grad_gu, weights, dots, dots_in, gain_sum,
        back_parts, ffn_parts, dot_sends, dot_arrivals, loads, weight_loads, stores, *scratch,
    ):
        back = Reduce(back_parts, back_parts, *scratch[:5])
        ahead = Reduce(ffn_parts, ffn_parts, *scratch[5:])
        own, other = back.places
        me = own[0]
        peers = [lax.rem(me + k, N_CTX) for k in range(1, N_CTX)]
        copies = [
            pltpu.make_async_copy(source, target, loads.at[k])
            for k, (source, target) in enumerate(((second, second_held), (grad_out, grad_held)))
        ]
        for copy in copies:
            copy.start()

        def weight_copies(t):
            columns = [
                pl.ds(pl.multiple_of(start + tile * t, tile), tile) for start in (0, hidden, 0)
            ]
            return [
                pltpu.make_async_copy(
                    source.at[:, there], target.at[:, there], weight_loads.at[3 * t + k]
                )
                for k, (source, target, there) in enumerate(
                    zip((w_in, w_in, w_down), (in_held, in_held, down_held), columns)
                )
            ]

        def start_weights(t, carry):
            for copy in weight_copies(t):
                copy.start()
            return carry

        lax.fori_loop(0, hidden // tile, start_weights, 0)
        greet([{"ctx": p} for p in peers])
        for copy in copies:
            copy.wait()

        def stored(slot, start):
            there = pl.ds(start, pair)
            return [
                pltpu.make_async_copy(act.at[slot], act_out.at[there, :], stores.at[slot, 0]),
                pltpu.make_async_copy(grad_gu.at[slot], grad_gu_out.at[there, :], stores.at[slot, 1]),
            ]

        def dot_copy(slot, place):
            return remote(
                dots.at[place], dots_in.at[slot], dot_sends, dot_arrivals, slot, {"ctx": place}
            )

        def start_of(b):
            ahead = 2 - b + 3 * (b // 2) - 2 * (b // 3)
            return pl.multiple_of(lax.rem(me // 2 + ahead, N_CTX // 2) * pair, pair)

        def block(b, carry):
            start = start_of(b)
            slot = lax.rem(b, 2)
            first = pl.multiple_of(start // rows, 2)

            @pl.when(b >= 2)
            def _():
                for copy in stored(slot, start_of(b - 2)):
                    copy.wait()

            def rows_of(ref):
                return ref[pl.ds(first, 2)].reshape(pair, width)

            logits = jnp.dot(
                rows_of(second_held), logit_weights[...], preferred_element_type=f32
            )
            lane = lax.broadcasted_iota(jnp.int32, logits.shape, 1)
            named = assigned[pl.ds(start, pair), :] > 0
            raised = jnp.where(named, logits, -1e30)
            raised = jnp.exp(raised - jnp.max(raised, axis=-1, keepdims=True))
            raised = jnp.where(named, raised, 0.0)
            gates = raised / jnp.sum(raised, axis=-1, keepdims=True)
            gates = jnp.where(lane == EXPERTS, jax.nn.sigmoid(logits), gates)
            weights[pl.ds(start, pair), :] = gates
            dots[pl.ds(first, 2)] = jnp.zeros((2, rows, lanes), f32)

            def hidden_tile(t, carry):
                @pl.when(b == 0)
                def _():
                    for copy in weight_copies(t):
                        copy.wait()

                low = pl.ds(pl.multiple_of(tile * t, tile), tile)
                high = pl.ds(pl.multiple_of(hidden + tile * t, tile), tile)
                rows_in = rows_of(second_held)
                gate = jnp.dot(rows_in, in_held[:, low], preferred_element_type=f32)
                upward = jnp.dot(rows_in, in_held[:, high], preferred_element_type=f32)
                raw = jnp.dot(rows_of(grad_held), down_held[:, low], preferred_element_type=f32)
                held = jnp.dot(
                    weights[pl.ds(start, pair), :],
                    member[:, low],
                    precision=highest,
                    preferred_element_type=f32,
                )
                squashed = jax.nn.sigmoid(gate)
                swished = gate * squashed
                value = swished * upward
                act[slot, :, low] = (value * held).astype(bf16)
                part = lax.dot_general(
                    raw * value,
                    member[:, low],
                    (((1,), (1,)), ((), ())),
                    precision=highest,
                    preferred_element_type=f32,
                )
                dots[pl.ds(first, 2)] += part.reshape(2, rows, lanes)
                grad = raw * held
                grad_gu[slot, :, low] = (
                    grad * upward * squashed * (1.0 + gate * (1.0 - squashed))
                ).astype(bf16)
                grad_gu[slot, :, high] = (grad * swished).astype(bf16)
                return carry

            lax.fori_loop(0, hidden // tile, hidden_tile, 0)
            for copy in stored(slot, start):
                copy.start()

            def out_tile(t, carry):
                there = pl.ds(pl.multiple_of(512 * t, 512), 512)
                for parts, left, right in (
                    (back_parts, grad_gu, in_held),
                    (ffn_parts, act, down_held),
                ):
                    made = contract_last(left[slot], right[there, :])
                    parts[pl.ds(first, 2), :, there] = made.astype(bf16).reshape(2, rows, 512)
                return carry

            lax.fori_loop(0, width // 512, out_tile, 0)

            def far():
                back.send_far()
                ahead.send_far()
                dot_copy(0, own[3]).start()
                dot_copy(1, other[3]).start()

            def near(side):
                back.send_near(side)
                back.pass_side(side)
                ahead.send_near(side)
                ahead.pass_side(side)
                dot_copy(2 + 2 * side, own[1 + side]).start()
                dot_copy(3 + 2 * side, other[1 + side]).start()

            pl.when(b == 0)(far)
            pl.when(b == 1)(lambda: near(0))
            pl.when(b == 2)(lambda: near(1))
            return carry

        lax.fori_loop(0, 4, block, 0)
        dot_copy(6, other[0]).start()
        back.cross()
        ahead.cross()
        back.ready()
        for k in range(7):
            ref = dots_in.at[k]
            remote(ref, ref, dot_sends, dot_arrivals, k, {"ctx": other[0]}).wait_recv()
        total_dots = dots[me]
        for k in range(7):
            total_dots = total_dots + dots_in[k]
        held = weights[pl.ds(pl.multiple_of(me * rows, rows), rows), :]
        lane = lax.broadcasted_iota(jnp.int32, held.shape, 1)
        routed = lane < EXPERTS
        centre = jnp.sum(jnp.where(routed, held * total_dots, 0.0), axis=-1, keepdims=True)
        both = jnp.where(
            routed,
            held * (total_dots - centre),
            jnp.where(lane == EXPERTS, total_dots * held * (1.0 - held), 0.0),
        )
        grad_logits[...] = both
        grad_residual[...] = jnp.dot(
            both, logit_rows[...], precision=highest, preferred_element_type=f32
        )
        gain_sum[...] = jnp.zeros_like(gain_sum)

        def norm(there):
            normed, factor = normalize(residual[there, :])
            grad = back.total(there) + grad_residual[there, :]
            gain_sum[...] += grad * normed
            grad_residual[there, :] = own_grad[there, :].astype(f32) + norm_back(
                grad, normed, factor, gain[...]
            )

        by_rows(rows, norm)
        grad_gain[...] = jnp.sum(gain_sum[...], axis=0, keepdims=True)
        ahead.ready()

        def finish(there):
            total = residual[there, :] + ahead.total(there)
            output[there, :] = (total * own_valid[there, :]).astype(bf16)

        by_rows(rows, finish)
        for b in (2, 3):
            for copy in stored(b % 2, start_of(b)):
                copy.wait()
        back.end()
        ahead.end()
        for slot, place in enumerate((own[3], other[3], own[1], other[1], own[2], other[2], other[0])):
            dot_copy(slot, place).wait_send()

    return pl.pallas_call(
        kernel,
        out_shape=(
            jax.ShapeDtypeStruct((rows, width), f32),
            jax.ShapeDtypeStruct((rows, width), bf16),
            jax.ShapeDtypeStruct((1, width), f32),
            jax.ShapeDtypeStruct((rows, lanes), f32),
            jax.ShapeDtypeStruct((seq, hidden), bf16),
            jax.ShapeDtypeStruct((seq, 2 * hidden), bf16),
        ),
        in_specs=[ANY, ANY, VMEM, ANY, ANY] + [VMEM] * 7,
        out_specs=(VMEM, VMEM, VMEM, VMEM, ANY, ANY),
        scratch_shapes=[
            pltpu.VMEM(second.shape, bf16),
            pltpu.VMEM(grad_out.shape, bf16),
            pltpu.VMEM(w_in.shape, bf16),
            pltpu.VMEM(w_down.shape, bf16),
            pltpu.VMEM((2, pair, hidden), bf16),
            pltpu.VMEM((2, pair, 2 * hidden), bf16),
            pltpu.VMEM((seq, lanes), f32),
            pltpu.VMEM((N_CTX, rows, lanes), f32),
            pltpu.VMEM((N_CTX - 1, rows, lanes), f32),
            pltpu.VMEM((16, width), f32),
            pltpu.VMEM(second.shape, bf16),
            pltpu.VMEM(second.shape, bf16),
            pltpu.SemaphoreType.DMA((N_CTX - 1,)),
            pltpu.SemaphoreType.DMA((N_CTX - 1,)),
            pltpu.SemaphoreType.DMA((2,)),
            pltpu.SemaphoreType.DMA((3 * hidden // tile,)),
            pltpu.SemaphoreType.DMA((2, 2)),
        ]
        + Reduce.scratch(rows, width, 1) * 2,
        compiler_params=params(2, 64 << 20),
        name="feed_forward",
    )(second, grad_out, assigned, w_in, w_down, logit_weights, logit_rows, member, residual, own_grad, own_valid, gain)


class Exchange:
    @staticmethod
    def scratch():
        return [pltpu.SemaphoreType.DMA((CHIPS,)), pltpu.SemaphoreType.DMA((CHIPS,))]

    def __init__(self, parts, staged, sends, arrivals):
        self.parts, self.staged = parts, staged
        self.sems = (sends, arrivals)
        self.width = parts.shape[2]
        me = lax.axis_index("shard")
        self.core, self.chip = lax.rem(me, 2), me // 2
        self.mate = {"shard": me + 1 - 2 * self.core}

    def chip_at(self, step):
        base = self.chip + (1 - lax.rem(step, 2)) * (1 - 2 * lax.rem(self.chip, 2))
        b = step // 2
        ahead = 2 - b + 3 * (b // 2) - 2 * (b // 3)
        return 2 * lax.rem(base // 2 + ahead, 4) + lax.rem(base, 2)

    def _pair(self, step):
        return remote(
            self.staged.at[lax.rem(step, 2), 1 - self.core, :, pl.ds(0, self.width)],
            self.parts.at[self.chip_at(step)],
            *self.sems,
            step,
            self.mate,
        )

    def finish(self, step):
        chip, slot, width = self.chip_at(step), lax.rem(step, 2), self.width
        ref = self.parts.at[chip]
        remote(ref, ref, *self.sems, step, self.mate).wait_recv()

        def add(there):
            total = self.parts[chip, there, :].astype(jnp.float32)
            total = total + self.staged[slot, self.core, there, 0:width].astype(jnp.float32)
            self.parts[chip, there, :] = total.astype(jnp.bfloat16)

        by_rows(128, add)

    def run(self, left, right, turned, between):
        width = self.width
        tile = 896 if width % 896 == 0 else width

        def step_of(step, carry):
            @pl.when(step >= 2)
            def _():
                self._pair(step - 2).wait_send()

            slot = lax.rem(step, 2)
            columns = pl.ds(pl.multiple_of(self.chip_at(step) * 256, 256), 256)
            turned[...] = left[:, :, columns].reshape(turned.shape[1], 256).T
            for start in range(0, width, tile):
                made = jnp.dot(
                    turned[...], right(start, tile), preferred_element_type=jnp.float32
                ).astype(jnp.bfloat16)
                self.staged[slot, 0, :, start : start + tile] = made[:128]
                self.staged[slot, 1, :, start : start + tile] = made[128:]
            self._pair(step).start()

            @pl.when(step >= 1)
            def _():
                self.finish(step - 1)

            for at, events in between.items():

                @pl.when(step == at)
                def _(events=events):
                    for event in events:
                        event()

            return carry

        lax.fori_loop(0, CHIPS, step_of, 0)
        self.finish(CHIPS - 1)
        for step in (CHIPS - 2, CHIPS - 1):
            self._pair(step).wait_send()


class Share:
    @staticmethod
    def scratch(width):
        return (
            [pltpu.VMEM((CHIPS, 128, width), jnp.bfloat16), pltpu.VMEM((128, width), jnp.bfloat16)]
            + Exchange.scratch()
            + Reduce.scratch(128, width, 1)
            + [pltpu.SemaphoreType.DMA((Gather.SEMAPHORES,))] * 2
            + [pltpu.SemaphoreType.DMA]
        )

    COUNT = 2 + 2 + 5 + 2 + 1

    def __init__(self, staged, out, scratch):
        parts, self.owned = scratch[0:2]
        self.exchange = Exchange(parts, staged, *scratch[2:4])
        self.reduce = Reduce(parts, parts, *scratch[4:9], axis="shard")
        self.gather = Gather(self.owned, out, *scratch[9:11])
        self.local = scratch[11]

    def near(self, side):
        return lambda: self.reduce.send_near(side)

    def side(self, side):
        return lambda: self.reduce.pass_side(side)

    def ring(self, column):
        return lambda: self.gather.pass_ring(column)

    def own(self):
        self.reduce.ready()

        def keep(there):
            self.owned[there, :] = self.reduce.total(there).astype(jnp.bfloat16)

        by_rows(128, keep)
        self.gather.begin()
        self._kept().start()

    def _kept(self):
        return pltpu.make_async_copy(
            self.owned, self.gather.out.at[self.gather.me], self.local
        )

    def end(self):
        self._kept().wait()
        self.gather.end()
        self.reduce.end()


def backward(own, second, grad_out, grad_gu, act, qkv, mixed, weights, first, cosines, sines, key_pos, query_pos, inputs, grad_residual, gain, second_gain_grad, grad_logits):
    rows, width = own.shape
    seq = rows * N_CTX
    hidden = act.shape[1]
    heads_width = mixed.shape[1]
    heads = heads_width // HEAD
    lanes = grad_logits.shape[1]
    n_shard = width // 128
    f32, bf16 = jnp.float32, jnp.bfloat16
    scale = HEAD ** (-0.5)
    tile = 256
    half = width // 2

    def kernel(
        own, second, grad_out, grad_gu, act, qkv, mixed, weights, first, cosines, sines, key_pos,
        query_pos, inputs, grad_residual, gain, second_gain_grad, grad_logits,
        input_grad, small_out, grad_attended, out_share, gate_share, up_share, mixed_share, qkv_share,
        second_held, g_held, gu_held, act_held, turned, staged, key_sum, value_sum, gain_sum,
        small, small_in, small_kept, small_across,
        loads, local, small_sends, small_arrivals, across_sends, across_arrivals, *scratch,
    ):
        gather = Gather(own, grad_attended, *scratch[0:2])
        reduce = Reduce(g_held, g_held, *scratch[2:7])
        shares = []
        for k, out in enumerate((out_share, gate_share, up_share, mixed_share, qkv_share)):
            start = 7 + Share.COUNT * k
            shares.append(Share(staged, out, scratch[start : start + Share.COUNT]))
        a, b, c, d, e = shares
        me = gather.me
        shard = lax.axis_index("shard")
        owners = [lax.rem(shard + k, n_shard) for k in range(1, n_shard)]
        places = [lax.rem(me + k, N_CTX) for k in range(1, N_CTX)]

        def load(k, source, target):
            return pltpu.make_async_copy(source, target, loads.at[k])

        early = [
            load(0, grad_out, g_held),
            load(1, act, act_held),
            load(2, second, second_held),
            load(3, grad_gu, gu_held),
        ]
        for copy in early:
            copy.start()
        greet([{"ctx": p} for p in places] + [{"shard": s} for s in owners])
        gather.begin()
        kept = pltpu.make_async_copy(own, grad_attended.at[me], local)
        kept.start()
        early[0].wait()
        early[1].wait()
        a.exchange.run(
            g_held,
            lambda start, count: act_held[:, start : start + count],
            turned,
            {
                2: [a.reduce.send_far],
                4: [a.near(0)],
                6: [a.near(1), gather.pass_other],
                7: [a.side(0)],
            },
        )
        early[2].wait()
        early[3].wait()
        b.exchange.run(
            second_held,
            lambda start, count: gu_held[:, start : start + count],
            turned,
            {
                0: [a.side(1)],
                2: [b.reduce.send_far],
                3: [lambda: gather.pass_ring(0)],
                4: [b.near(0)],
                5: [a.reduce.cross],
                6: [b.near(1), lambda: gather.pass_ring(1)],
                7: [b.side(0)],
            },
        )
        c.exchange.run(
            second_held,
            lambda start, count: gu_held[:, hidden + start : hidden + start + count],
            turned,
            {
                0: [b.side(1)],
                2: [c.reduce.send_far],
                3: [a.own],
                4: [c.near(0)],
                5: [b.reduce.cross],
                6: [c.near(1)],
                7: [c.side(0)],
            },
        )
        logits_grad = lax.dot_general(
            grad_logits[...],
            second_held[me].astype(f32),
            (((0,), (0,)), ((), ())),
            precision=highest,
            preferred_element_type=f32,
        )
        small[...] = jnp.zeros_like(small)
        for s in range(n_shard):
            there = slice(128 * s, 128 * (s + 1))
            small[s, 1:2, :] = second_gain_grad[:, there]
            small[s, 2 : 3 + EXPERTS, :] = logits_grad[: EXPERTS + 1, there]
        kept.wait()
        gather.end()
        late = [
            load(0, grad_attended, g_held),
            load(1, weights.at[pl.ds(0, half), :], gu_held.at[:, 0:half]),
            load(2, weights.at[pl.ds(half, half), :], gu_held.at[:, half : 2 * half]),
            load(3, qkv, gu_held.at[:, 2 * half : 2 * half + 3 * heads_width]),
            load(
                4,
                mixed,
                gu_held.at[:, 2 * half + 3 * heads_width : 2 * half + 4 * heads_width],
            ),
            load(5, first, second_held),
        ]
        for copy in late:
            copy.start()
        c.side(1)()
        for copy in late:
            copy.wait()
        columns_qkv = 2 * half
        columns_mixed = columns_qkv + 3 * heads_width
        columns_grad = columns_mixed + heads_width
        w_out = [3 * heads_width, half + 3 * heads_width]

        def grad_mixed(i, carry):
            first_block = 2 * i
            there = pl.ds(pl.multiple_of(i * tile, tile), tile)
            left = g_held[pl.ds(first_block, 2)].reshape(tile, width)
            made = jnp.dot(
                left[:, :half],
                gu_held[:, w_out[0] : w_out[0] + heads_width],
                preferred_element_type=f32,
            ) + jnp.dot(
                left[:, half:],
                gu_held[:, w_out[1] : w_out[1] + heads_width],
                preferred_element_type=f32,
            )
            gu_held[there, columns_grad : columns_grad + heads_width] = made.astype(bf16)
            return carry

        lax.fori_loop(0, seq // tile, grad_mixed, 0)
        a.gather.pass_other()
        d.exchange.run(
            g_held,
            lambda start, count: gu_held[:, columns_mixed + start : columns_mixed + start + count],
            turned,
            {
                2: [d.reduce.send_far],
                4: [d.near(0), a.ring(0)],
                6: [d.near(1)],
                7: [d.side(0), b.own],
            },
        )
        events = {
            0: [c.reduce.cross, a.ring(1), d.side(1)],
            1: [b.gather.pass_other],
            2: [d.reduce.cross, b.ring(0)],
            3: [c.own],
            4: [b.ring(1), d.own],
            5: [c.gather.pass_other],
            6: [d.gather.pass_other],
            7: [c.ring(0), d.ring(0)],
        }

        def attend(n, carry):
            head, i = n // (seq // tile), lax.rem(n, seq // tile)
            there = pl.ds(pl.multiple_of(i * tile, tile), tile)

            def lanes_of(start):
                return pl.ds(pl.multiple_of(start + HEAD * head, HEAD), HEAD)

            query = gu_held[there, lanes_of(columns_qkv)]
            key = gu_held[:, lanes_of(columns_qkv + heads_width)]
            value = gu_held[:, lanes_of(columns_qkv + 2 * heads_width)]
            grad = gu_held[there, lanes_of(columns_grad)]
            scores = contract_last(key, query) * scale
            scores = jnp.where(key_pos[...] <= query_pos[:, there], scores, -1e30)
            raised = jnp.exp(scores - jnp.max(scores, axis=0, keepdims=True))
            probs = raised * (1.0 / jnp.sum(raised, axis=0, keepdims=True))
            grad_probs = contract_last(value, grad)
            centre = jnp.sum(probs * grad_probs, axis=0, keepdims=True)
            grad_scores = (probs * (grad_probs - centre)).astype(bf16)

            @pl.when(i == 0)
            def _():
                key_sum[...] = jnp.zeros_like(key_sum)
                value_sum[...] = jnp.zeros_like(value_sum)

            key_sum[...] += jnp.dot(grad_scores, query, preferred_element_type=f32)
            value_sum[...] += jnp.dot(probs.astype(bf16), grad, preferred_element_type=f32)
            grad_query = contract_first(grad_scores, key) * scale

            def turn_back(values, cosines, sines):
                return (values * cosines + pltpu.roll(values, HEAD // 2, 1) * sines).astype(bf16)

            act_held[there, lanes_of(0)] = turn_back(
                grad_query, cosines[there, :], sines[there, :]
            )

            @pl.when(i == seq // tile - 1)
            def _():
                act_held[:, lanes_of(heads_width)] = turn_back(
                    key_sum[...] * scale, cosines[...], sines[...]
                )
                act_held[:, lanes_of(2 * heads_width)] = value_sum[...].astype(bf16)

            for at, todo in events.items():

                @pl.when(n == at)
                def _(todo=todo):
                    for event in todo:
                        event()

            return carry

        lax.fori_loop(0, heads * (seq // tile), attend, 0)

        def start_of(k):
            ahead = 2 - k + 3 * (k // 2) - 2 * (k // 3)
            return lax.rem(me // 2 + ahead, N_CTX // 2) * 2

        def grad_first(k, carry):
            block = start_of(k)
            left = act_held[pl.ds(pl.multiple_of(block * rows, tile), tile), 0 : 3 * heads_width]
            for t in range(4):
                low = 512 * (t % 2)
                start = half * (t // 2)
                made = contract_last(left, gu_held[low : low + 512, start : start + 3 * heads_width])
                g_held[pl.ds(block, 2), :, 512 * t : 512 * (t + 1)] = made.astype(bf16).reshape(
                    2, rows, 512
                )
            pl.when(k == 0)(reduce.send_far)
            pl.when(k == 1)(lambda: reduce.send_near(0))
            pl.when(k == 2)(lambda: reduce.send_near(1))
            return carry

        lax.fori_loop(0, 4, grad_first, 0)
        e.exchange.run(
            second_held,
            lambda start, count: act_held[:, start : start + count],
            turned,
            {
                1: [lambda: reduce.pass_side(0)],
                2: [e.reduce.send_far, lambda: reduce.pass_side(1)],
                4: [e.near(0), c.ring(1)],
                6: [e.near(1), d.ring(1)],
                7: [e.side(0), reduce.cross],
            },
        )
        e.side(1)()
        bias = jnp.sum(act_held[:, 0 : 3 * heads_width].astype(f32), axis=0, keepdims=True)
        per = heads_width // 128
        for i in range(3):
            for j in range(per):
                block = n_shard * i + per * me + j
                there = slice(heads_width * i + 128 * j, heads_width * i + 128 * (j + 1))
                small[block // 3, pl.ds(3 + EXPERTS + lax.rem(block, 3), 1), :] = bias[:, there]
        e.reduce.cross()
        reduce.ready()
        gain_sum[...] = jnp.zeros_like(gain_sum)

        def norm(there):
            normed, factor = normalize(inputs[there, :].astype(f32))
            grad = reduce.total(there)
            gain_sum[...] += grad * normed
            input_grad[there, :] = grad_residual[there, :] + norm_back(
                grad, normed, factor, gain[...]
            )

        by_rows(rows, norm)
        first_gain_grad = jnp.sum(gain_sum[...], axis=0, keepdims=True)
        for s in range(n_shard):
            small[s, 0:1, :] = first_gain_grad[:, 128 * s : 128 * (s + 1)]
        to_owners = [
            remote(small.at[s], small_in.at[k], small_sends, small_arrivals, k, {"shard": s})
            for k, s in enumerate(owners)
        ]
        for copy in to_owners:
            copy.start()
        e.own()
        total = small[shard]
        for k, copy in enumerate(to_owners):
            copy.wait_recv()
            total = total + small_in[k]
        small_kept[...] = total
        to_places = [
            remote(small_kept, small_across.at[k], across_sends, across_arrivals, k, {"ctx": p})
            for k, p in enumerate(places)
        ]
        for copy in to_places:
            copy.start()
        e.gather.pass_other()
        e.ring(0)()
        e.ring(1)()
        for k, copy in enumerate(to_places):
            copy.wait_recv()
            total = total + small_across[k]
        small_out[...] = total
        for copy in to_owners + to_places:
            copy.wait_send()
        reduce.end()
        for share in shares:
            share.end()

    def shared(count):
        return jax.ShapeDtypeStruct((N_CTX, 128, count), bf16)

    return pl.pallas_call(
        kernel,
        out_shape=(
            jax.ShapeDtypeStruct((rows, width), f32),
            jax.ShapeDtypeStruct((16, 128), f32),
            jax.ShapeDtypeStruct((N_CTX, rows, width), bf16),
            shared(hidden),
            shared(hidden),
            shared(hidden),
            shared(heads_width),
            shared(3 * heads_width),
        ),
        in_specs=[VMEM] + [ANY] * 8 + [VMEM] * 9,
        out_specs=(VMEM, VMEM) + (ANY,) * 6,
        scratch_shapes=[
            pltpu.VMEM(second.shape, bf16),
            pltpu.VMEM(grad_out.shape, bf16),
            pltpu.VMEM(grad_gu.shape, bf16),
            pltpu.VMEM(act.shape, bf16),
            pltpu.VMEM((256, seq), bf16),
            pltpu.VMEM((2, 2, 128, hidden), bf16),
            pltpu.VMEM((seq, HEAD), f32),
            pltpu.VMEM((seq, HEAD), f32),
            pltpu.VMEM((16, width), f32),
            pltpu.VMEM((n_shard, 16, 128), f32),
            pltpu.VMEM((n_shard - 1, 16, 128), f32),
            pltpu.VMEM((16, 128), f32),
            pltpu.VMEM((N_CTX - 1, 16, 128), f32),
            pltpu.SemaphoreType.DMA((6,)),
            pltpu.SemaphoreType.DMA,
            pltpu.SemaphoreType.DMA((n_shard - 1,)),
            pltpu.SemaphoreType.DMA((n_shard - 1,)),
            pltpu.SemaphoreType.DMA((N_CTX - 1,)),
            pltpu.SemaphoreType.DMA((N_CTX - 1,)),
        ]
        + [pltpu.SemaphoreType.DMA((Gather.SEMAPHORES,))] * 2
        + Reduce.scratch(rows, width, 1)
        + Share.scratch(hidden) * 3
        + Share.scratch(heads_width)
        + Share.scratch(3 * heads_width),
        compiler_params=params(3, 64 << 20),
        name="backward",
    )(own, second, grad_out, grad_gu, act, qkv, mixed, weights, first, cosines, sines, key_pos, query_pos, inputs, grad_residual, gain, second_gain_grad, grad_logits)


def local(
    tokens,
    cotangent,
    lengths,
    routes,
    block_order,
    norm_gains,
    qkv_weight,
    qkv_bias,
    out_weight,
    router,
    shared_gate,
    ffn_in,
    ffn_out,
):
    bf16, f32 = jnp.bfloat16, jnp.float32
    n_ctx = lax.axis_size("ctx")
    n_shard = lax.axis_size("shard")
    rows_dev = tokens.shape[1]
    seq_len = rows_dev * n_ctx
    n_blocks = block_order.shape[0]
    block = seq_len // n_blocks
    heads = D // HEAD // n_ctx
    width = heads * HEAD
    hidden_blocks = -(-HIDDEN_BLOCKS // n_ctx)
    hidden = hidden_blocks * LANE
    scale = HEAD ** (-0.5)
    place = lax.axis_index("ctx")

    every = jnp.arange(seq_len, dtype=jnp.int32)
    matches = (every // block)[:, None] == jnp.arange(n_blocks, dtype=jnp.int32)[None, :]
    pos = jnp.sum(jnp.where(matches, block_order[None, :], 0), axis=1) * block + every % block
    valid = pos < lengths[0]
    valid_rows = valid.astype(f32)[:, None]

    blocked = (n_ctx, rows_dev, D)
    own_valid = lax.dynamic_slice_in_dim(valid_rows, place * rows_dev, rows_dev)
    own_grad = jnp.where(own_valid > 0, cotangent[0], 0).astype(bf16)
    g_all = ag_ctx(own_grad)
    blocks = [hidden_blocks * place + j for j in range(hidden_blocks)]
    safe = [jnp.minimum(b, HIDDEN_BLOCKS - 1) for b in blocks]
    starts = [gate_start(b) for b in safe]
    w_in = ag_shard(columns_at(ffn_in, [s for s, _ in starts] + [s + u for s, u in starts]))
    w_down = ag_shard(columns_at(ffn_out, [LANE * b for b in safe]))
    picks = routes[0][:, :, None] == jnp.arange(LANE, dtype=jnp.int32)[None, None, :]
    own_assigned = jnp.sum(picks.astype(f32), axis=1).astype(bf16)
    small = jnp.concatenate(
        [
            norm_gains.reshape(-1),
            router.T.reshape(-1),
            shared_gate.reshape(-1),
            qkv_bias.reshape(-1),
        ]
    ).reshape(-1, LANE)
    small = jnp.pad(small, ((0, 4), (0, 0)))
    x_all, attn_weights, small_all = front(
        jnp.concatenate([tokens[0], own_assigned], axis=1), qkv_weight, out_weight, small
    )
    x_all = x_all.reshape(seq_len, D + LANE)
    x_all, assigned = x_all[:, :D], x_all[:, D:]
    attn_weights = attn_weights.reshape(D, 4 * width)
    small_all = small_all.reshape(n_shard, -1)
    gains = small_all[:, : 2 * LANE].reshape(n_shard, 2, LANE).transpose(1, 0, 2).reshape(2, D)
    first_gain, second_gain = gains[0].astype(f32), gains[1].astype(f32)
    logit_weights = (
        small_all[:, 2 * LANE : 9 * LANE]
        .reshape(n_shard, EXPERTS + 1, LANE)
        .transpose(0, 2, 1)
        .reshape(D, EXPERTS + 1)
    )
    bias = small_all[:, 9 * LANE : 12 * LANE].reshape(3 * D)
    own_bias = jnp.concatenate(
        [lax.dynamic_slice_in_dim(bias, D * i + width * place, width) for i in range(3)]
    ).astype(f32)
    w_qkv, w_out = attn_weights[:, : 3 * width], attn_weights[:, 3 * width :]

    first_normed_all, _ = normalize(x_all.astype(f32))
    first_all = (first_normed_all * first_gain).astype(bf16)
    projected = dot(first_all, w_qkv) + own_bias
    cosines, sines = rope_tables(pos)
    query = rotate(projected[:, :width].reshape(seq_len, heads, HEAD), cosines, sines).astype(bf16)
    key = rotate(
        projected[:, width : 2 * width].reshape(seq_len, heads, HEAD), cosines, sines
    ).astype(bf16)
    value = projected[:, 2 * width :].astype(bf16).reshape(seq_len, heads, HEAD)
    allowed = ((pos[None, :] <= pos[:, None]) & valid[None, :])[None]
    scores = jnp.einsum("qhd,khd->hqk", query, key, preferred_element_type=f32) * scale
    masked = jnp.where(allowed, scores, -1e30)
    peak = jnp.max(masked, axis=-1, keepdims=True)
    log_total = peak + jnp.log(jnp.sum(jnp.exp(masked - peak), axis=-1, keepdims=True))
    probs = jnp.exp(masked - log_total)
    probs_low = probs.astype(bf16)
    mixed = jnp.einsum("hqk,khd->qhd", probs_low, value, preferred_element_type=f32)
    mixed = mixed.reshape(seq_len, width).astype(bf16)
    residual, second_all = middle(
        contract_last(mixed, w_out).astype(bf16).reshape(n_ctx, rows_dev, D),
        tokens[0],
        second_gain[None],
    )

    block_ids = jnp.stack(blocks)
    branch_of = jnp.where(
        block_ids < SHARED_BLOCKS, EXPERTS, (block_ids - SHARED_BLOCKS) // EXPERT_BLOCKS
    )
    member = (
        (branch_of[None, :] == jnp.arange(LANE, dtype=jnp.int32)[:, None])
        & (block_ids < HIDDEN_BLOCKS)[None, :]
    ).astype(f32)
    member = jnp.repeat(member, LANE, axis=1)
    logit_weights = jnp.pad(logit_weights, ((0, 0), (0, LANE - EXPERTS - 1)))
    grad_residual, output, grad_second_gain, grad_both, act_low, grad_gu = feed_forward(
        second_all,
        g_all.reshape(blocked),
        assigned,
        w_in,
        w_down,
        logit_weights,
        logit_weights.T.astype(f32),
        member,
        residual,
        own_grad,
        own_valid,
        second_gain[None],
    )
    lane = jnp.arange(HEAD, dtype=jnp.int32)
    turned_sines = jnp.where(lane < HEAD // 2, sines[:, 0, :], -sines[:, 0, :])
    qkv_low = jnp.concatenate(
        [part.reshape(seq_len, width) for part in (query, key, value)], axis=1
    )
    input_grad, own_small, _, out_share, gate_share, up_share, mixed_share, qkv_share = backward(
        grad_residual.astype(bf16),
        second_all,
        g_all.reshape(blocked),
        grad_gu,
        act_low,
        qkv_low,
        mixed,
        attn_weights,
        first_all.reshape(blocked),
        cosines[:, 0, :],
        turned_sines,
        jnp.where(valid, pos, 2 * seq_len)[:, None],
        pos[None],
        tokens[0],
        grad_residual,
        first_gain[None],
        grad_second_gain,
        grad_both,
    )
    own_small = own_small.reshape(-1)
    grad_gains = own_small[: 2 * LANE].reshape(2, LANE)
    grad_router = own_small[2 * LANE : 8 * LANE].reshape(EXPERTS, LANE).T
    grad_shared_gate = own_small[8 * LANE : 9 * LANE]
    grad_bias_out = own_small[9 * LANE : 12 * LANE]

    grad_qkv = jnp.concatenate(
        [
            qkv_share[p, :, width * i : width * (i + 1)]
            for i in range(3)
            for p in range(n_ctx)
        ],
        axis=1,
    ).astype(f32)
    grad_out = jnp.concatenate(
        [mixed_share[p] for p in range(n_ctx)], axis=1
    ).astype(f32)

    def piece(share, first, count):
        parts = []
        while count:
            p, j = first // hidden_blocks, first % hidden_blocks
            take = min(count, hidden_blocks - j)
            parts.append(share[p, :, LANE * j : LANE * (j + take)])
            first, count = first + take, count - take
        return parts

    spans = [(0, SHARED_BLOCKS)] + [
        (SHARED_BLOCKS + EXPERT_BLOCKS * e, EXPERT_BLOCKS) for e in range(EXPERTS)
    ]
    grad_ffn_in = jnp.concatenate(
        [part for f, n in spans for share in (gate_share, up_share) for part in piece(share, f, n)],
        axis=1,
    ).astype(f32)
    grad_ffn_out = jnp.concatenate(
        [part for f, n in spans for part in piece(out_share, f, n)], axis=1
    ).astype(f32)
    return (
        output[None],
        input_grad[None],
        grad_gains,
        grad_qkv,
        grad_bias_out,
        grad_out,
        grad_router,
        grad_shared_gate,
        grad_ffn_in,
        grad_ffn_out,
    )


def solution(mesh):
    placed = (
        P("shard", "ctx", None),
        P("shard", "ctx", None),
        P("shard"),
        P("shard", "ctx", None),
        P(),
        P(None, "shard"),
        P("shard", None),
        P("shard"),
        P("shard", None),
        P("shard", None),
        P("shard"),
        P("shard", None),
        P("shard", None),
    )
    return jax.shard_map(
        local,
        mesh=mesh,
        in_specs=placed,
        out_specs=(
            P("shard", "ctx", None),
            P("shard", "ctx", None),
            P(None, "shard"),
            P("shard", None),
            P("shard"),
            P("shard", None),
            P("shard", None),
            P("shard"),
            P("shard", None),
            P("shard", None),
        ),
        check_vma=False,
    )
```

time: 1670 us -> 701 us (0.42)
  waiting for transfers between devices: 1220 us -> 14.1 us
  Pallas kernels: 0 us -> 537 us
  matrix products: 168 us -> 12 us
  local copies, waits for them, and re-layouts: 130 us -> 72.9 us
  blocking collectives: 48 us -> 0 us
  other arithmetic: 68.5 us -> 38.8 us
    reduce_scatter x6 -> x0, waiting for transfers between devices: 543 us -> none  [the longest x5 310 us: rs_ctx(): return lax.psum_scatter(value, 'ctx', scatter_dimension=0, tiled=True)]
    pallas_call x0 -> x4, Pallas kernels: none -> 537 us  [the longest x1 243 us: backward(): pl.pallas_call(kernel, out_shape=(jax.ShapeDtypeStruct((rows, width), f32...]
    all_gather x4 -> x1, waiting for transfers between devices: 177 us -> 0.01 us  [ag_ctx(): return lax.all_gather(value, 'ctx', axis=0, tiled=True)]
    all_gather x2 -> x0, waiting for transfers between devices: 158 us -> none  [the longest x1 106 us: local(): ffn_grads = lax.all_gather(rs_shard(ffn_share), 'ctx', axis=0)]
    psum x1 -> x0, waiting for transfers between devices: 139 us -> none  [local(): small_sums = lax.psum(small_grads, ('ctx', 'shard'))]
    all_gather x3 -> x2, waiting for transfers between devices: 146 us -> 14 us  [ag_shard(): return lax.all_gather(value, 'shard', axis=0, tiled=True)]
    dot_general x12 -> x0, matrix products: 59.3 us -> none  [the longest x4 42.9 us: contract_first(): lax.dot_general(left, right, (((0,), (0,)), ((), ())), preferred_element_...]
    dot_general x6 -> x1, matrix products: 60 us -> 3.48 us  [dot(): return jnp.dot(left, right, preferred_element_type=jnp.float32)]
  transfers between devices with their start and end apart: 17 -> 3, of which waited for: 16 -> 1; matrix products, arithmetic and copies ran while one was open for 14% -> 11% of each run, Pallas kernels for 0% -> 24%
where the time goes in v2:
time: 701 us; the launch traced here: 691 us
  Pallas kernels  537 us (77%)
  local copies, waits for them, and re-layouts  72.9 us (10%)
  other arithmetic  38.8 us (6%)
  between operations  16.7 us (2%)
  waiting for transfers between devices  14.1 us (2%)
  matrix products  12 us (2%)
    pallas_call x1, Pallas kernels, backward(): pl.pallas_call(kernel, out_shape=(jax.ShapeDtypeStruct((rows, width), f32...  243 us
    pallas_call x1, Pallas kernels, feed_forward(): pl.pallas_call(kernel, out_shape=(jax.ShapeDtypeStruct((rows, width), f32...  127 us
    pallas_call x1, Pallas kernels, front(): pl.pallas_call(kernel, out_shape=(jax.ShapeDtypeStruct((N_CTX,) + block.s...  85.8 us
    pallas_call x1, Pallas kernels, middle(): pl.pallas_call(kernel, out_shape=(jax.ShapeDtypeStruct((rows, width), jnp...  80.2 us
    unnamed x181, local copies, waits for them, and re-layouts  55.1 us
    all_gather x2, waiting for transfers between devices, ag_shard(): return lax.all_gather(value, 'shard', axis=0, tiled=True)  14 us
  transfers between devices with their start and end apart: 3, of which 1 were waited for; matrix products, arithmetic and copies ran while one was open for 11% of the time, Pallas kernels for 24%

profile of v2, /device:TPU:2, one launch (start us, length us, event | category | flops | bytes accessed | tf_op | source)
XLA Modules:
  0.0 691.3 jit_solution(7639422966266647304)
XLA Ops:
  8.9 1.9 bitcast_select_fusion.own_grad
  47.6 85.8 %front.1 = (bf16[8,128,2176]{2,1,0:T(8,128)(2,1)}, bf16[16,128,1024]{2,1,0:T(8,128)(2,1)}, bf16[16,16,128]{2,1,0:T(8,128)(2,1)}) custom-call(bf16[128,2176]{1,0:T(8,128)(2,1)} %pad_maximum_fusion.1.block, bf16[128,6144]{1,0:T(8,128)(2,1)} %qkv_weight.1, bf16[128,2048]{1,0:T(8,128)(2,1)} %out_weight.1, bf16[16,128]{1,0:T(8,128)(2,1)} %pad.8.small), custom_call_target="tpu_custom_call" | custom-call | tf_op jit(solution)/shard_map/front/pallas_call | solution.py:446
  134.3 1.7 slice.403.assigned
  136.1 3.1 fusion
  139.8 3.2 fusion.2
  143.4 3.5 fusion.8
  146.9 1.7 copy-done.12
  149.9 1.3 copy.68.member
  153.5 3.0 negate_select_fusion
  158.5 2.5 fusion.3
  161.1 2.2 exponential_reduce_fusion
  163.3 3.4 fusion.11
  166.7 2.1 copy.77.mixed
  169.8 2.7 convolution_convert_fusion
  172.5 80.2 %middle.1 = (f32[128,2048]{1,0:T(8,128)S(1)}, bf16[8,128,2048]{2,1,0:T(8,128)(2,1)S(1)}) custom-call(bf16[8,128,2048]{2,1,0:T(8,128)(2,1)S(1)} %bitcast.256, bf16[128,2048]{1,0:T(8,128)(2,1)S(1)} %bitcast.259, f32[1,2048]{1,0:T(1,128)S(1)} %get-tuple-element.65.gain), custom_call_target="tpu_custom_call" | custom-call | tf_op jit(solution)/shard_map/middle/pallas_call | solution.py:498
  253.8 1.1 copy-done
  255.4 1.2 copy-done.14
  257.0 1.2 pad_maximum_fusion.qkv
  258.9 1.1 convert_bitcast_fusion.logit_rows
  260.8 14.0 %all-gather.6.cloned.1.call-done.w_in = bf16[2048,3584]{1,0:T(8,128)(2,1)} async-done(((bf16[128,3584]{1,0:T(8,128)(2,1)}), bf16[2048,3584]{1,0:T(8,128)(2,1)}) %all-gather.6.cloned.1.call-update) | async-done | bytes 14680080 | tf_op jit(solution)/shard_map/all_gather | solution.py:91
  274.8 127.3 %feed_forward.1 = (f32[128,2048]{1,0:T(8,128)}, bf16[128,2048]{1,0:T(8,128)(2,1)}, f32[1,2048]{1,0:T(1,128)}, f32[128,128]{1,0:T(8,128)}, bf16[1024,1792]{1,0:T(8,128)(2,1)}, /*index=5*/bf16[1024,3584]{1,0:T(8,128)(2,1)}) custom-call(bf16[8,128,2048]{2,1,0:T(8,128)(2,1)} %copy-done, bf16[8,128,2048]{2,1,0:T(8,128)(2,1)} %bitcast.263, ...), custom_call_target="tpu_custom_call" | custom-call | tf_op jit(solution)/shard_map/feed_forward/pallas_call | solution.py:730
  402.2 2.1 convert_element_type.137.own
  404.3 243.3 %backward.1 = (f32[128,2048]{1,0:T(8,128)}, f32[16,128]{1,0:T(8,128)}, bf16[8,128,2048]{2,1,0:T(8,128)(2,1)}, bf16[8,128,1792]{2,1,0:T(8,128)(2,1)}, bf16[8,128,...) custom-call(bf16[128,2048]{1,0:T(8,128)(2,1)} %convert_element_type., ...), custom_call_target="tpu_custom_call" | custom-call | tf_op jit(solution)/shard_map/backward/pallas_call | solution.py:1206
  647.6 1.3 slice_bitcast_fusion.3
  648.9 1.3 slice_bitcast_fusion.4
  650.1 1.2 slice.309
  651.4 1.2 slice_bitcast_fusion.5
  665.9 4.1 convert_element_type.145
  670.2 1.5 copy-done.18
  672.4 6.8 convert_element_type.144
  679.4 1.1 convert_element_type.143
  680.8 2.0 convert_element_type.142
  (234 shorter events, 64.6 us)
Async XLA Ops:
  7.2 38.7 %copy-start.32 = (bf16[2,128]{1,0:T(2,128)(2,1)S(1)}, bf16[2,128]{1,0:T(2,128)(2,1)}, u32[]{:S(2)}) copy-start(bf16[2,128]{1,0:T(2,128)(2,1)} %param.18) | copy-start | bytes 1540
  7.2 38.7 %copy-start.29 = (bf16[128,6]{0,1:T(8,128)(2,1)S(1)}, bf16[128,6]{0,1:T(8,128)(2,1)}, u32[]{:S(2)}) copy-start(bf16[128,6]{0,1:T(8,128)(2,1)} %param.22) | copy-start | bytes 4612
  7.2 38.7 %copy-start.30 = (bf16[384]{0:T(512)(128)(2,1)S(1)}, bf16[384]{0:T(512)(128)(2,1)}, u32[]{:S(2)}) copy-start(bf16[384]{0:T(512)(128)(2,1)} %param.20) | copy-start | bytes 2308
  7.2 38.7 %copy-start.31 = (bf16[128]{0:T(256)(128)(2,1)S(1)}, bf16[128]{0:T(256)(128)(2,1)}, u32[]{:S(2)}) copy-start(bf16[128]{0:T(256)(128)(2,1)} %param.23) | copy-start | bytes 772
  7.2 39.4 %copy-start.28 = (s32[1,128,4]{1,2,0:T(4,128)S(1)}, s32[1,128,4]{1,2,0:T(4,128)}, u32[]{:S(2)}) copy-start(s32[1,128,4]{1,2,0:T(4,128)} %param.16) | copy-start | bytes 6148
  7.2 39.5 %copy-start.1 = (bf16[1,128,2048]{2,1,0:T(8,128)(2,1)S(1)}, bf16[1,128,2048]{2,1,0:T(8,128)(2,1)}, u32[]{:S(2)}) copy-start(bf16[1,128,2048]{2,1,0:T(8,128)(2,1)} %param.13) | copy-start | bytes 1572868
  7.2 253.6 %all-gather.4.cloned.1.call-start = ((), (), s32[]{:S(2)}) async-start(), calls=%async_computation | async-start | bytes 4718592 | tf_op jit(solution)/shard_map/all_gather | solution.py:87
  10.8 250.0 %all-gather.8.cloned.1.call-start = ((), (), s32[]{:S(2)}) async-start(), calls=%async_computation.2 | async-start | bytes 7798784 | tf_op jit(solution)/shard_map/all_gather | solution.py:91
  22.5 252.3 %all-gather.6.cloned.1.call-start = ((), (), s32[]{:S(2)}) async-start(), calls=%async_computation.1 | async-start | bytes 15597568 | tf_op jit(solution)/shard_map/all_gather | solution.py:91
  139.8 32.8 %copy-start.3 = (f32[1,2048]{1,0:T(1,128)}, f32[1,2048]{1,0:T(1,128)S(1)}, u32[]{:S(2)}) copy-start(f32[1,2048]{1,0:T(1,128)S(1)} %get-tuple-element.65.gain) | copy-start | bytes 24580
  139.8 3.6 copy-start.15
  143.0 3.9 copy-start.4
  148.6 4.7 copy-start.16
  152.3 4.2 copy-start.13
  156.5 96.9 %copy-start.5 = (f32[1024,128]{1,0:T(8,128)}, f32[1024,128]{1,0:T(8,128)S(1)}, u32[]{:S(2)}) copy-start(f32[1024,128]{1,0:T(8,128)S(1)} %get-tuple-element.58.cosines) | copy-start | bytes 1572868
  157.5 3.5 copy-start.6
  157.5 3.5 copy-start.8
  161.0 2.2 copy-start.27
  172.5 80.3 %copy-start.7 = (f32[1024,2,64]{2,0,1:T(8,128)S(1)}, f32[1024,2,64]{2,0,1:T(8,128)}, u32[]{:S(2)}) copy-start(f32[1024,2,64]{2,0,1:T(8,128)} %copy-done.6) | copy-start | bytes 1572868
  172.5 80.3 %copy-start.9 = (f32[1024,2,64]{2,0,1:T(8,128)S(1)}, f32[1024,2,64]{2,0,1:T(8,128)}, u32[]{:S(2)}) copy-start(f32[1024,2,64]{2,0,1:T(8,128)} %copy-done.8) | copy-start | bytes 1572868
  172.5 80.3 %copy-start.11 = (f32[1024,128]{1,0:T(8,128)S(1)}, f32[1024,128]{1,0:T(8,128)}, u32[]{:S(2)}) copy-start(f32[1024,128]{1,0:T(8,128)} %copy-done.10) | copy-start | bytes 1572868
  252.8 2.1 copy-start
  252.8 2.6 copy-start.2
  252.8 3.8 copy-start.14
  253.4 3.6 copy-start.17
  257.0 2.9 copy-start.20
  665.9 4.1 copy-start.19
  665.9 5.8 copy-start.18
  672.4 6.8 copy-start.25
  672.4 8.0 %copy-start.21 = (bf16[8,128,768]{2,1,0:T(8,128)(2,1)S(1)}, bf16[8,128,768]{2,1,0:T(8,128)(2,1)}, u32[]{:S(2)}) copy-start(bf16[8,128,768]{2,1,0:T(8,128)(2,1)} %get-tuple-element.41) | copy-start | bytes 4718596
  680.5 2.3 copy-start.26
  680.6 3.0 copy-start.22
  (4 other events, 5.4 us)
Sparse Core Ops, SparseCore 0:
  11.0 116.0 all-gather.3
  128.7 44.7 all-gather.7
  175.3 99.5 all-gather.5

commit v3 on v2

--- a/solution.py
+++ b/solution.py
@@ -42,21 +42,11 @@
     half = HEAD // 2
     freqs = rope_base ** (-jnp.arange(half, dtype=jnp.float32) * 2.0 / HEAD)
     phase = positions.astype(jnp.float32)[:, None] * freqs[None, :]
-    phase = jnp.concatenate([phase, phase], axis=1)
-    return (jnp.cos(phase)[:, None, :], jnp.sin(phase)[:, None, :])
-
-
-def rotate(values, cosines, sines):
-    half = values.shape[-1] // 2
-    turned = jnp.concatenate([-values[..., half:], values[..., :half]], axis=-1)
-    return values * cosines + turned * sines
-
-
-def rotate_back(values, cosines, sines):
-    half = values.shape[-1] // 2
-    scaled = values * sines
-    turned = jnp.concatenate([scaled[..., half:], -scaled[..., :half]], axis=-1)
-    return values * cosines + turned
+    cosines, sines = jnp.cos(phase), jnp.sin(phase)
+    return (
+        jnp.concatenate([cosines, cosines], axis=1),
+        jnp.concatenate([-sines, sines], axis=1),
+    )
 
 
 def normalize(values):
@@ -67,28 +57,6 @@
 def norm_back(grad_normed, normalized, factor, gain):
     scaled = grad_normed * gain
     return factor * (scaled - normalized * jnp.mean(scaled * normalized, axis=-1, keepdims=True))
-
-
-def gate_start(block):
-    routed = block >= SHARED_BLOCKS
-    expert = (block - SHARED_BLOCKS) // EXPERT_BLOCKS
-    rest = (block - SHARED_BLOCKS) % EXPERT_BLOCKS
-    start = jnp.where(routed, 2 * FS + 2 * HE * expert + LANE * rest, LANE * block)
-    return start, jnp.where(routed, HE, FS)
-
-
-def columns_at(array, starts):
-    return jnp.concatenate(
-        [lax.dynamic_slice_in_dim(array, start, LANE, axis=1) for start in starts], axis=1
-    )
-
-
-def ag_ctx(value):
-    return lax.all_gather(value, "ctx", axis=0, tiled=True)
-
-
-def ag_shard(value):
-    return lax.all_gather(value, "shard", axis=0, tiled=True)
 
 
 MESH = pl.DeviceIdType.MESH
@@ -146,54 +114,79 @@
 
 class Gather:
     SEMAPHORES = 9
-
-    def __init__(self, own, out, sends, arrivals):
+    PAIRED = 9 + CHIPS
+
+    def __init__(self, own, out, sends, arrivals, axis="ctx"):
         self.own, self.out, self.sends, self.arrivals = own, out, sends, arrivals
-        self.places, _ = places_of("ctx")
+        self.places, self.peer = places_of(axis)
         (self.me, self.up, self.down, self.far), other = self.places
         self.other = other[0]
-        self.half = out.shape[1] // 2
+        self.half = out.shape[-2] // 2
+        self.paired = axis == "shard"
+        if self.paired:
+            shard = lax.axis_index("shard")
+            self.core = lax.rem(shard, 2)
+            self.mate = {"shard": shard + 1 - 2 * self.core}
         self.started = []
 
-    def _send(self, slot, source, target, place):
+    def at(self, place, *half):
+        if self.paired:
+            return self.out.at[(place, self.core) + half]
+        return self.out.at[(place,) + half]
+
+    def _send(self, slot, source, target, peer):
         def copy():
-            return remote(source(), target(), self.sends, self.arrivals, slot, {"ctx": place})
+            return remote(source(), target(), self.sends, self.arrivals, slot, peer())
 
         copy().start()
         self.started.append(copy)
 
     def _await(self, slot, ref):
-        remote(ref, ref, self.sends, self.arrivals, slot, {"ctx": self.other}).wait_recv()
+        remote(ref, ref, self.sends, self.arrivals, slot, self.peer(self.other)).wait_recv()
+
+    def _hand(self, number, place, source=None):
+        if self.paired:
+            block = lambda: self.at(place)
+            self._send(9 + number, source or block, block, lambda: self.mate)
 
     def begin(self):
         for slot, place in ((0, self.other), (1, self.up), (2, self.down)):
-            self._send(slot, lambda: self.own, lambda: self.out.at[self.me], place)
+            self._send(slot, lambda: self.own, lambda: self.at(self.me), lambda place=place: self.peer(place))
+        self._hand(0, self.me, lambda: self.own)
 
     def pass_other(self):
-        def block():
-            return self.out.at[self.other]
-
+        block = lambda: self.at(self.other)
         self._await(0, block())
-        self._send(3, block, block, self.up)
-        self._send(4, block, block, self.down)
+        self._send(3, block, block, lambda: self.peer(self.up))
+        self._send(4, block, block, lambda: self.peer(self.down))
+        self._hand(1, self.other)
 
     def pass_ring(self, column):
         _, up, down, _ = self.places[column]
         first = 1 + 2 * column
         low, high = pl.ds(0, self.half), pl.ds(self.half, self.half)
-        self._await(first, self.out.at[down])
-        lower = lambda: self.out.at[down, low]
-        self._send(5 + 2 * column, lower, lower, self.up)
-        self._await(first + 1, self.out.at[up])
-        upper = lambda: self.out.at[up, high]
-        self._send(6 + 2 * column, upper, upper, self.down)
+        self._await(first, self.at(down))
+        lower = lambda: self.at(down, low)
+        self._send(5 + 2 * column, lower, lower, lambda: self.peer(self.up))
+        self._await(first + 1, self.at(up))
+        upper = lambda: self.at(up, high)
+        self._send(6 + 2 * column, upper, upper, lambda: self.peer(self.down))
+        self._hand(2 + 2 * column, down)
+        self._hand(3 + 2 * column, up)
 
     def end(self):
         low, high = pl.ds(0, self.half), pl.ds(self.half, self.half)
         for column in range(2):
             far = self.places[column][3]
-            self._await(5 + 2 * column, self.out.at[far, low])
-            self._await(6 + 2 * column, self.out.at[far, high])
+            self._await(5 + 2 * column, self.at(far, low))
+            self._await(6 + 2 * column, self.at(far, high))
+            self._hand(6 + column, far)
+        if self.paired:
+            (me, up, down, far), (other, other_up, other_down, other_far) = self.places
+            for number, place in enumerate(
+                (me, other, down, up, other_down, other_up, far, other_far)
+            ):
+                self._await(9 + number, self.out.at[place, 1 - self.core])
         for copy in self.started:
             copy().wait_send()
 
@@ -386,32 +379,162 @@
             copy.wait_send()
 
 
-def front(block, qkv_weight, out_weight, small):
-    rows, width = qkv_weight.shape[0], out_weight.shape[1] // N_CTX
-    n_shard = out_weight.shape[1] // rows
+def pick_copies(ffn_in, ffn_out, picked, sems):
+    count = -(-HIDDEN_BLOCKS // N_CTX)
+    place = lax.axis_index("ctx")
+    copies = []
+    for j in range(count):
+        block = place * count + j
+        block = block - (block // HIDDEN_BLOCKS) * (block - HIDDEN_BLOCKS + 1)
+        routed = (block // SHARED_BLOCKS + 1) // 2
+        rest = block - SHARED_BLOCKS
+        expert = (rest + SHARED_BLOCKS * (1 - routed)) // EXPERT_BLOCKS * routed
+        gate = block * (1 - routed) + (2 * SHARED_BLOCKS + EXPERT_BLOCKS * expert + rest) * routed
+        up = gate + SHARED_BLOCKS * (1 - routed) + EXPERT_BLOCKS * routed
+        for k, (source, at) in enumerate(((ffn_in, gate), (ffn_in, up), (ffn_out, block))):
+            copies.append(
+                pltpu.make_async_copy(
+                    source.at[:, pl.ds(pl.multiple_of(at * LANE, LANE), LANE)],
+                    picked.at[:, LANE * (count * k + j) : LANE * (count * k + j + 1)],
+                    sems.at[3 * j + k],
+                )
+            )
+    return copies
+
+
+def assemble(out_share, gate_share, up_share, mixed_share, qkv_share):
+    rows, hidden = out_share.shape[1:]
+    width = mixed_share.shape[2]
+    count = hidden // LANE
+    spans = [(0, SHARED_BLOCKS)] + [
+        (SHARED_BLOCKS + EXPERT_BLOCKS * e, EXPERT_BLOCKS) for e in range(EXPERTS)
+    ]
+
+    def moves(place, kind):
+        result = []
+        for index, (first, size) in enumerate(spans):
+            low, high = max(first, count * place), min(first + size, count * (place + 1))
+            if low >= high:
+                continue
+            there = low if kind == 0 else first + low + (kind - 1) * size
+            result.append(((low - count * place) * LANE, there * LANE, (high - low) * LANE))
+        return result
+
+    jobs = []
+    for place in range(N_CTX):
+        for kind in range(3):
+            jobs.append((kind, place, hidden, min(kind, 1), moves(place, kind)))
+        jobs.append((3, place, width, 2, [(0, width * place, width)]))
+        jobs.append(
+            (4, place, 3 * width, 3, [(width * i, D * i + width * place, width) for i in range(3)])
+        )
+    depth = 4
+    most = max(len(job[4]) for job in jobs)
+
+    def kernel(*refs):
+        shares, outs = refs[0:5], refs[5:9]
+        low, full, loads, stores = refs[9:]
+
+        def load(n):
+            kind, place, size, _, _ = jobs[n]
+            return pltpu.make_async_copy(
+                shares[kind].at[place], low.at[n % depth, :, 0:size], loads.at[n % depth]
+            )
+
+        def store(n):
+            _, _, _, to, spans_of = jobs[n]
+            return [
+                pltpu.make_async_copy(
+                    full.at[n % depth, :, start : start + size],
+                    outs[to].at[:, there : there + size],
+                    stores.at[n % depth, k],
+                )
+                for k, (start, there, size) in enumerate(spans_of)
+            ]
+
+        for n in range(depth - 1):
+            load(n).start()
+        for n in range(len(jobs)):
+            if n + depth - 1 < len(jobs):
+                load(n + depth - 1).start()
+            load(n).wait()
+            if n >= depth:
+                for copy in store(n - depth):
+                    copy.wait()
+            slot, size = n % depth, jobs[n][2]
+
+            def widen(there, slot=slot, size=size):
+                full[slot, there, 0:size] = low[slot, there, 0:size].astype(jnp.float32)
+
+            by_rows(rows, widen)
+            for copy in store(n):
+                copy.start()
+        for n in range(len(jobs) - depth, len(jobs)):
+            for copy in store(n):
+                copy.wait()
+
+    f32 = jnp.float32
+    return pl.pallas_call(
+        kernel,
+        out_shape=(
+            jax.ShapeDtypeStruct((rows, FOUT), f32),
+            jax.ShapeDtypeStruct((rows, FIN), f32),
+            jax.ShapeDtypeStruct((rows, D), f32),
+            jax.ShapeDtypeStruct((rows, 3 * D), f32),
+        ),
+        in_specs=[ANY] * 5,
+        out_specs=(ANY,) * 4,
+        scratch_shapes=[
+            pltpu.VMEM((depth, rows, hidden), jnp.bfloat16),
+            pltpu.VMEM((depth, rows, hidden), f32),
+            pltpu.SemaphoreType.DMA((depth,)),
+            pltpu.SemaphoreType.DMA((depth, most)),
+        ],
+        compiler_params=pltpu.CompilerParams(vmem_limit_bytes=60 << 20),
+        name="assemble",
+    )(out_share, gate_share, up_share, mixed_share, qkv_share)
+
+
+def front(block, own_grad, qkv_weight, out_weight, ffn_in, ffn_out, small, cosines, sines, key_pos, query_pos):
+    rows, width = qkv_weight.shape[0], out_weight.shape[1]
+    n_shard = width // rows
+    heads_width = width // N_CTX
+    heads = heads_width // HEAD
+    seq = rows * N_CTX
+    extra = block.shape[1] - width
+    tile = 256
+    scale = HEAD ** (-0.5)
+    hidden = -(-HIDDEN_BLOCKS // N_CTX) * LANE
+    f32, bf16 = jnp.float32, jnp.bfloat16
 
     def kernel(
-        block, qkv_weight, out_weight, small, x_all, weights, small_all, staged, loads, local, *scratch
+        block, own_grad, qkv_weight, out_weight, ffn_in, ffn_out, small, cosines, sines, key_pos,
+        query_pos,
+        residual, second_all, g_all, weights_out, small_all, first_out, ffn_weights, qkv, mixed, assigned,
+        x_all, weights, first, staged, picked, params_all, parts, own, loads, picks, local, *scratch,
     ):
         gather = Gather(block, x_all, *scratch[0:2])
         spread = Spread(staged, weights, *scratch[2:4])
         spread_small = Spread(small, small_all, *scratch[4:6])
-        place = gather.me
+        gather_grad = Gather(own_grad, g_all, *scratch[6:8])
+        gather_second = Gather(own, second_all, *scratch[8:10])
+        gather_ffn = Gather(picked, ffn_weights, *scratch[10:12], axis="shard")
+        reduce = Reduce(parts, parts, *scratch[12:17])
+        me = gather.me
         loaded = [
             pltpu.make_async_copy(
-                qkv_weight.at[:, pl.ds(pl.multiple_of(width * N_CTX * i + width * place, width), width)],
-                staged.at[:, width * i : width * (i + 1)],
+                source.at[:, pl.ds(pl.multiple_of(start + heads_width * me, heads_width), heads_width)],
+                staged.at[:, heads_width * i : heads_width * (i + 1)],
                 loads.at[i],
             )
-            for i in range(3)
-        ] + [
-            pltpu.make_async_copy(
-                out_weight.at[:, pl.ds(pl.multiple_of(width * place, width), width)],
-                staged.at[:, 3 * width :],
-                loads.at[3],
+            for i, (source, start) in enumerate(
+                ((qkv_weight, 0), (qkv_weight, width), (qkv_weight, 2 * width), (out_weight, 0))
             )
         ]
         for copy in loaded:
+            copy.start()
+        picking = pick_copies(ffn_in, ffn_out, picked, picks)
+        for copy in picking:
             copy.start()
         greet([{"ctx": p} for p in (gather.other, gather.up, gather.down)] + spread.peers())
         gather.begin()
@@ -419,13 +542,18 @@
         for copy in loaded:
             copy.wait()
         spread.begin()
+        for copy in picking:
+            copy.wait()
+        gather_ffn.begin()
         kept = [
             pltpu.make_async_copy(source, target, local.at[k])
             for k, (source, target) in enumerate(
                 (
-                    (block, x_all.at[place]),
+                    (block, x_all.at[me]),
                     (staged, weights.at[spread.me]),
                     (small, small_all.at[spread.me]),
+                    (own_grad, g_all.at[me]),
+                    (picked, ffn_weights.at[spread.chip, spread.core]),
                 )
             )
         ]
@@ -436,95 +564,195 @@
         gather.pass_ring(0)
         spread.hand_on()
         gather.pass_ring(1)
-        for copy in kept:
-            copy.wait()
+        gather_grad.begin()
         spread_small.end()
         spread.end()
         gather.end()
-
-    bf16 = jnp.bfloat16
+        for copy in kept:
+            copy.wait()
+        gather_ffn.pass_other()
+        weights_kept = pltpu.make_async_copy(weights, weights_out, local.at[0])
+        weights_kept.start()
+        assigned[...] = x_all[:, :, width:].reshape(seq, extra)
+        params_all[...] = small_all[...].astype(f32)
+        gains = [
+            jnp.concatenate([params_all[s, k : k + 1, :] for s in range(n_shard)], axis=1)
+            for k in range(2)
+        ]
+        per = heads_width // 128
+
+        def bias_of(i):
+            parts_of = []
+            for j in range(per):
+                at = n_shard * i + per * me + j
+                parts_of.append(params_all[at // 3, pl.ds(3 + EXPERTS + lax.rem(at, 3), 1), :])
+            return jnp.concatenate(parts_of, axis=1)
+
+        biases = [bias_of(i) for i in range(3)]
+
+        def project(n, carry):
+            there = pl.ds(pl.multiple_of(n * tile, tile), tile)
+
+            def norm(k, inner):
+                inner_rows = pl.ds(pl.multiple_of(lax.rem(k, rows // 16) * 16, 16), 16)
+                at = 2 * n + k // (rows // 16)
+                normed, _ = normalize(x_all[at, inner_rows, 0:width].astype(f32))
+                first[at, inner_rows, :] = (normed * gains[0]).astype(bf16)
+                return inner
+
+            lax.fori_loop(0, tile // 16, norm, 0)
+            left = first[pl.ds(2 * n, 2)].reshape(tile, width)
+            for i in range(3):
+                columns = slice(heads_width * i, heads_width * (i + 1))
+                made = biases[i] + jnp.dot(
+                    left,
+                    weights[:, :, columns].reshape(width, heads_width),
+                    preferred_element_type=f32,
+                )
+                if i == 2:
+                    qkv[there, columns] = made.astype(bf16)
+                    continue
+                for h in range(heads):
+                    part = made[:, HEAD * h : HEAD * (h + 1)]
+                    turned = part * cosines[there, :] + pltpu.roll(part, HEAD // 2, 1) * sines[there, :]
+                    start = heads_width * i + HEAD * h
+                    qkv[there, start : start + HEAD] = turned.astype(bf16)
+
+            @pl.when(n == 1)
+            def _():
+                gather_grad.pass_other()
+
+            return carry
+
+        lax.fori_loop(0, seq // tile, project, 0)
+        first_kept = pltpu.make_async_copy(first, first_out, local.at[1])
+        first_kept.start()
+        events = {
+            0: lambda: gather_grad.pass_ring(0),
+            1: lambda: gather_ffn.pass_ring(0),
+            3: lambda: gather_grad.pass_ring(1),
+            7: lambda: gather_ffn.pass_ring(1),
+        }
+
+        def attend(n, carry):
+            head, i = n // (seq // tile), lax.rem(n, seq // tile)
+            there = pl.ds(pl.multiple_of(i * tile, tile), tile)
+
+            def lanes_of(start):
+                return pl.ds(pl.multiple_of(start + HEAD * head, HEAD), HEAD)
+
+            scores = scale * contract_last(qkv[:, lanes_of(heads_width)], qkv[there, lanes_of(0)])
+            scores = jnp.where(key_pos[...] <= query_pos[:, there], scores, -1e30)
+            raised = jnp.exp(scores - jnp.max(scores, axis=0, keepdims=True))
+            probs = (raised * (1.0 / jnp.sum(raised, axis=0, keepdims=True))).astype(bf16)
+            mixed[there, lanes_of(0)] = contract_first(
+                probs, qkv[:, lanes_of(2 * heads_width)]
+            ).astype(bf16)
+            for at, event in events.items():
+                pl.when(n == at)(event)
+            return carry
+
+        lax.fori_loop(0, heads * (seq // tile), attend, 0)
+
+        def attended(k, carry):
+            ahead = 2 - k + 3 * (k // 2) - 2 * (k // 3)
+            at = lax.rem(me // 2 + ahead, N_CTX // 2) * 2
+            left = mixed[pl.ds(pl.multiple_of(at * rows, tile), tile), :]
+            blocks = 512 // rows
+            for t in range(width // 512):
+                right = weights[blocks * t : blocks * (t + 1), :, 3 * heads_width :]
+                made = contract_last(left, right.reshape(512, heads_width)).astype(bf16)
+                parts[pl.ds(at, 2), :, 512 * t : 512 * (t + 1)] = made.reshape(2, rows, 512)
+            pl.when(k == 0)(reduce.send_far)
+            pl.when(k == 1)(lambda: reduce.send_near(0))
+            pl.when(k == 2)(lambda: reduce.send_near(1))
+            return carry
+
+        lax.fori_loop(0, 4, attended, 0)
+        reduce.pass_side(0)
+        reduce.pass_side(1)
+        reduce.cross()
+        reduce.ready()
+
+        def norm_second(there):
+            total = x_all[me, there, 0:width].astype(f32) + reduce.total(there)
+            residual[there, :] = total
+            normed, _ = normalize(total)
+            own[there, :] = (normed * gains[1]).astype(bf16)
+
+        by_rows(rows, norm_second)
+        gather_second.begin()
+        second_kept = pltpu.make_async_copy(own, second_all.at[me], local.at[2])
+        second_kept.start()
+        gather_second.pass_other()
+        gather_second.pass_ring(0)
+        gather_second.pass_ring(1)
+        gather_grad.end()
+        gather_ffn.end()
+        reduce.end()
+        for copy in (weights_kept, first_kept, second_kept):
+            copy.wait()
+        gather_second.end()
+
+    def shape(*dims, kind=bf16):
+        return jax.ShapeDtypeStruct(dims, kind)
+
+    pair = [pltpu.SemaphoreType.DMA((Gather.SEMAPHORES,))] * 2
+    spread_pair = [pltpu.SemaphoreType.DMA((Spread.SEMAPHORES,))] * 2
     return pl.pallas_call(
         kernel,
         out_shape=(
-            jax.ShapeDtypeStruct((N_CTX,) + block.shape, bf16),
-            jax.ShapeDtypeStruct((n_shard, rows, 4 * width), bf16),
-            jax.ShapeDtypeStruct((n_shard,) + small.shape, bf16),
+            shape(rows, width, kind=f32),
+            shape(N_CTX, rows, width),
+            shape(N_CTX, rows, width),
+            shape(n_shard, rows, 4 * heads_width),
+            shape(n_shard, 16, 128),
+            shape(N_CTX, rows, width),
+            shape(CHIPS, 2, rows, 3 * hidden),
+            shape(seq, 3 * heads_width),
+            shape(seq, heads_width),
+            shape(seq, extra),
         ),
-        in_specs=[ANY] * 4,
-        out_specs=(ANY, ANY, ANY),
+        in_specs=[ANY, VMEM] + [ANY] * 5 + [VMEM] * 4,
+        out_specs=(VMEM, ANY, ANY, ANY, VMEM, ANY, ANY, VMEM, VMEM, VMEM),
         scratch_shapes=[
-            pltpu.VMEM((rows, 4 * width), bf16),
+            pltpu.VMEM((N_CTX,) + block.shape, bf16),
+            pltpu.VMEM((n_shard, rows, 4 * heads_width), bf16),
+            pltpu.VMEM((N_CTX, rows, width), bf16),
+            pltpu.VMEM((rows, 4 * heads_width), bf16),
+            pltpu.VMEM((rows, 3 * hidden), bf16),
+            pltpu.VMEM((n_shard, 16, 128), f32),
+            pltpu.VMEM((N_CTX, rows, width), bf16),
+            pltpu.VMEM((rows, width), bf16),
             pltpu.SemaphoreType.DMA((4,)),
-            pltpu.SemaphoreType.DMA((3,)),
+            pltpu.SemaphoreType.DMA((3 * hidden // LANE,)),
+            pltpu.SemaphoreType.DMA((5,)),
         ]
-        + [pltpu.SemaphoreType.DMA((Gather.SEMAPHORES,))] * 2
-        + [pltpu.SemaphoreType.DMA((Spread.SEMAPHORES,))] * 4,
-        compiler_params=params(0),
+        + pair
+        + spread_pair * 2
+        + pair * 2
+        + [pltpu.SemaphoreType.DMA((Gather.PAIRED,))] * 2
+        + Reduce.scratch(rows, width, 1),
+        compiler_params=params(0, 56 << 20),
         name="front",
-    )(block, qkv_weight, out_weight, small)
-
-
-def middle(parts, inputs, gain):
-    _, rows, width = parts.shape
-
-    def kernel(parts, inputs, gain, residual, out, own, local, *scratch):
-        reduce_scratch, gather_scratch = scratch[:5], scratch[5:]
-        reduce = Reduce(parts, parts, *reduce_scratch)
-        gather = Gather(own, out, *gather_scratch)
-        greet([{"ctx": p} for p in (gather.other, gather.up, gather.down)])
-        reduce.begin()
-        reduce.pass_on(1)
-        reduce.pass_on(0)
-        reduce.cross()
-        reduce.ready()
-
-        def norm(there):
-            total = inputs[there, :].astype(jnp.float32) + reduce.total(there)
-            residual[there, :] = total
-            normed, _ = normalize(total)
-            own[there, :] = (normed * gain[...]).astype(jnp.bfloat16)
-
-        by_rows(rows, norm)
-        gather.begin()
-        copy = pltpu.make_async_copy(own, out.at[gather.me], local)
-        copy.start()
-        gather.pass_other()
-        gather.pass_ring(0)
-        gather.pass_ring(1)
-        reduce.end()
-        copy.wait()
-        gather.end()
-
-    return pl.pallas_call(
-        kernel,
-        out_shape=(
-            jax.ShapeDtypeStruct((rows, width), jnp.float32),
-            jax.ShapeDtypeStruct((N_CTX, rows, width), jnp.bfloat16),
-        ),
-        in_specs=[VMEM, VMEM, VMEM],
-        out_specs=(VMEM, ANY),
-        scratch_shapes=[pltpu.VMEM((rows, width), jnp.bfloat16), pltpu.SemaphoreType.DMA]
-        + Reduce.scratch(rows, width)
-        + [pltpu.SemaphoreType.DMA((Gather.SEMAPHORES,))] * 2,
-        compiler_params=params(1, 40 << 20),
-        name="middle",
-    )(parts, inputs, gain)
-
-
-def feed_forward(second, grad_out, assigned, w_in, w_down, logit_weights, logit_rows, member, residual, own_grad, own_valid, gain):
+    )(block, own_grad, qkv_weight, out_weight, ffn_in, ffn_out, small, cosines, sines, key_pos, query_pos)
+
+
+def feed_forward(second, grad_out, assigned, ffn_weights, small, member, residual, own_grad, own_valid):
     _, rows, width = second.shape
     seq = rows * N_CTX
-    hidden = w_down.shape[1]
-    lanes = logit_weights.shape[1]
+    hidden = ffn_weights.shape[1] // 3
+    lanes = 128
+    n_shard = small.shape[0]
     pair = 2 * rows
     tile = 256
     f32, bf16 = jnp.float32, jnp.bfloat16
 
     def kernel(
-        second, grad_out, assigned, w_in, w_down, logit_weights, logit_rows, member,
-        residual, own_grad, own_valid, gain,
-        grad_residual, output, grad_gain, grad_logits, act_out, grad_gu_out,
+        second, grad_out, assigned, ffn_weights, small, member, residual, own_grad, own_valid,
+        grad_residual, grad_low, output, grad_gain, grad_logits, act_out, grad_gu_out,
         second_held, grad_held, in_held, down_held, act, grad_gu, weights, dots, dots_in, gain_sum,
+        logit_rows, logit_low,
         back_parts, ffn_parts, dot_sends, dot_arrivals, loads, weight_loads, stores, *scratch,
     ):
         back = Reduce(back_parts, back_parts, *scratch[:5])
@@ -540,17 +768,14 @@
             copy.start()
 
         def weight_copies(t):
-            columns = [
-                pl.ds(pl.multiple_of(start + tile * t, tile), tile) for start in (0, hidden, 0)
-            ]
-            return [
-                pltpu.make_async_copy(
-                    source.at[:, there], target.at[:, there], weight_loads.at[3 * t + k]
-                )
-                for k, (source, target, there) in enumerate(
-                    zip((w_in, w_in, w_down), (in_held, in_held, down_held), columns)
-                )
-            ]
+            copies = []
+            for k, (target, there, here) in enumerate(
+                ((in_held, 0, 0), (in_held, hidden, hidden), (down_held, 2 * hidden, 0))
+            ):
+                source = ffn_weights.at[:, pl.ds(pl.multiple_of(there + tile * t, tile), tile)]
+                target = target.at[:, pl.ds(pl.multiple_of(here + tile * t, tile), tile)]
+                copies.append(pltpu.make_async_copy(source, target, weight_loads.at[3 * t + k]))
+            return copies
 
         def start_weights(t, carry):
             for copy in weight_copies(t):
@@ -559,6 +784,14 @@
 
         lax.fori_loop(0, hidden // tile, start_weights, 0)
         greet([{"ctx": p} for p in peers])
+        logit_rows[...] = jnp.zeros_like(logit_rows)
+        gains = []
+        for s in range(n_shard):
+            held = small[s].astype(f32)
+            gains.append(held[1:2])
+            logit_rows[0 : EXPERTS + 1, 128 * s : 128 * (s + 1)] = held[2 : 3 + EXPERTS]
+        gain = jnp.concatenate(gains, axis=1)
+        logit_low[...] = logit_rows[...].astype(bf16)
         for copy in copies:
             copy.wait()
 
@@ -591,9 +824,7 @@
             def rows_of(ref):
                 return ref[pl.ds(first, 2)].reshape(pair, width)
 
-            logits = jnp.dot(
-                rows_of(second_held), logit_weights[...], preferred_element_type=f32
-            )
+            logits = contract_last(rows_of(second_held), logit_low[...])
             lane = lax.broadcasted_iota(jnp.int32, logits.shape, 1)
             named = assigned[pl.ds(start, pair), :] > 0
             raised = jnp.where(named, logits, -1e30)
@@ -706,9 +937,9 @@
             normed, factor = normalize(residual[there, :])
             grad = back.total(there) + grad_residual[there, :]
             gain_sum[...] += grad * normed
-            grad_residual[there, :] = own_grad[there, :].astype(f32) + norm_back(
-                grad, normed, factor, gain[...]
-            )
+            grad = own_grad[there, :].astype(f32) + norm_back(grad, normed, factor, gain)
+            grad_residual[there, :] = grad
+            grad_low[there, :] = grad.astype(bf16)
 
         by_rows(rows, norm)
         grad_gain[...] = jnp.sum(gain_sum[...], axis=0, keepdims=True)
@@ -732,24 +963,27 @@
         out_shape=(
             jax.ShapeDtypeStruct((rows, width), f32),
             jax.ShapeDtypeStruct((rows, width), bf16),
+            jax.ShapeDtypeStruct((rows, width), bf16),
             jax.ShapeDtypeStruct((1, width), f32),
             jax.ShapeDtypeStruct((rows, lanes), f32),
             jax.ShapeDtypeStruct((seq, hidden), bf16),
             jax.ShapeDtypeStruct((seq, 2 * hidden), bf16),
         ),
-        in_specs=[ANY, ANY, VMEM, ANY, ANY] + [VMEM] * 7,
-        out_specs=(VMEM, VMEM, VMEM, VMEM, ANY, ANY),
+        in_specs=[ANY, ANY, VMEM, ANY] + [VMEM] * 5,
+        out_specs=(VMEM,) * 5 + (ANY, ANY),
         scratch_shapes=[
             pltpu.VMEM(second.shape, bf16),
             pltpu.VMEM(grad_out.shape, bf16),
-            pltpu.VMEM(w_in.shape, bf16),
-            pltpu.VMEM(w_down.shape, bf16),
+            pltpu.VMEM((width, 2 * hidden), bf16),
+            pltpu.VMEM((width, hidden), bf16),
             pltpu.VMEM((2, pair, hidden), bf16),
             pltpu.VMEM((2, pair, 2 * hidden), bf16),
             pltpu.VMEM((seq, lanes), f32),
             pltpu.VMEM((N_CTX, rows, lanes), f32),
             pltpu.VMEM((N_CTX - 1, rows, lanes), f32),
             pltpu.VMEM((16, width), f32),
+            pltpu.VMEM((lanes, width), f32),
+            pltpu.VMEM((lanes, width), bf16),
             pltpu.VMEM(second.shape, bf16),
             pltpu.VMEM(second.shape, bf16),
             pltpu.SemaphoreType.DMA((N_CTX - 1,)),
@@ -761,7 +995,7 @@
         + Reduce.scratch(rows, width, 1) * 2,
         compiler_params=params(2, 64 << 20),
         name="feed_forward",
-    )(second, grad_out, assigned, w_in, w_down, logit_weights, logit_rows, member, residual, own_grad, own_valid, gain)
+    )(second, grad_out, assigned, ffn_weights, small, member, residual, own_grad, own_valid)
 
 
 class Exchange:
@@ -951,7 +1185,6 @@
                 2: [a.reduce.send_far],
                 4: [a.near(0)],
                 6: [a.near(1), gather.pass_other],
-                7: [a.side(0)],
             },
         )
         early[2].wait()
@@ -961,13 +1194,12 @@
             lambda start, count: gu_held[:, start : start + count],
             turned,
             {
-                0: [a.side(1)],
+                0: [a.side(0)],
+                1: [a.side(1)],
                 2: [b.reduce.send_far],
                 3: [lambda: gather.pass_ring(0)],
                 4: [b.near(0)],
-                5: [a.reduce.cross],
                 6: [b.near(1), lambda: gather.pass_ring(1)],
-                7: [b.side(0)],
             },
         )
         c.exchange.run(
@@ -975,13 +1207,11 @@
             lambda start, count: gu_held[:, hidden + start : hidden + start + count],
             turned,
             {
-                0: [b.side(1)],
                 2: [c.reduce.send_far],
-                3: [a.own],
                 4: [c.near(0)],
-                5: [b.reduce.cross],
+                5: [a.reduce.cross],
                 6: [c.near(1)],
-                7: [c.side(0)],
+                7: [b.side(0)],
             },
         )
         logits_grad = lax.dot_general(
@@ -1012,7 +1242,8 @@
         ]
         for copy in late:
             copy.start()
-        c.side(1)()
+        b.side(1)()
+        a.own()
         for copy in late:
             copy.wait()
         columns_qkv = 2 * half
@@ -1037,27 +1268,25 @@
             return carry
 
         lax.fori_loop(0, seq // tile, grad_mixed, 0)
-        a.gather.pass_other()
         d.exchange.run(
             g_held,
             lambda start, count: gu_held[:, columns_mixed + start : columns_mixed + start + count],
             turned,
             {
                 2: [d.reduce.send_far],
-                4: [d.near(0), a.ring(0)],
+                4: [d.near(0)],
                 6: [d.near(1)],
-                7: [d.side(0), b.own],
             },
         )
         events = {
-            0: [c.reduce.cross, a.ring(1), d.side(1)],
-            1: [b.gather.pass_other],
-            2: [d.reduce.cross, b.ring(0)],
-            3: [c.own],
-            4: [b.ring(1), d.own],
-            5: [c.gather.pass_other],
-            6: [d.gather.pass_other],
-            7: [c.ring(0), d.ring(0)],
+            0: [a.gather.pass_other],
+            1: [b.reduce.cross],
+            2: [a.ring(0)],
+            3: [d.side(0), d.side(1)],
+            4: [b.own],
+            5: [a.ring(1), c.side(0)],
+            6: [c.side(1)],
+            7: [d.reduce.cross],
         }
 
         def attend(n, carry):
@@ -1089,7 +1318,7 @@
             grad_query = contract_first(grad_scores, key) * scale
 
             def turn_back(values, cosines, sines):
-                return (values * cosines + pltpu.roll(values, HEAD // 2, 1) * sines).astype(bf16)
+                return (values * cosines - pltpu.roll(values, HEAD // 2, 1) * sines).astype(bf16)
 
             act_held[there, lanes_of(0)] = turn_back(
                 grad_query, cosines[there, :], sines[there, :]
@@ -1133,6 +1362,7 @@
             return carry
 
         lax.fori_loop(0, 4, grad_first, 0)
+        b.gather.pass_other()
         e.exchange.run(
             second_held,
             lambda start, count: act_held[:, start : start + count],
@@ -1140,12 +1370,15 @@
             {
                 1: [lambda: reduce.pass_side(0)],
                 2: [e.reduce.send_far, lambda: reduce.pass_side(1)],
-                4: [e.near(0), c.ring(1)],
-                6: [e.near(1), d.ring(1)],
-                7: [e.side(0), reduce.cross],
+                3: [b.ring(0)],
+                4: [e.near(0), c.reduce.cross],
+                6: [e.near(1), c.own],
+                7: [b.ring(1), reduce.cross],
             },
         )
+        e.side(0)()
         e.side(1)()
+        d.own()
         bias = jnp.sum(act_held[:, 0 : 3 * heads_width].astype(f32), axis=0, keepdims=True)
         per = heads_width // 128
         for i in range(3):
@@ -1154,6 +1387,8 @@
                 there = slice(heads_width * i + 128 * j, heads_width * i + 128 * (j + 1))
                 small[block // 3, pl.ds(3 + EXPERTS + lax.rem(block, 3), 1), :] = bias[:, there]
         e.reduce.cross()
+        c.gather.pass_other()
+        d.gather.pass_other()
         reduce.ready()
         gain_sum[...] = jnp.zeros_like(gain_sum)
 
@@ -1176,6 +1411,8 @@
         for copy in to_owners:
             copy.start()
         e.own()
+        c.ring(0)()
+        d.ring(0)()
         total = small[shard]
         for k, copy in enumerate(to_owners):
             copy.wait_recv()
@@ -1188,6 +1425,8 @@
         for copy in to_places:
             copy.start()
         e.gather.pass_other()
+        c.ring(1)()
+        d.ring(1)()
         e.ring(0)()
         e.ring(1)()
         for k, copy in enumerate(to_places):
@@ -1270,11 +1509,7 @@
     seq_len = rows_dev * n_ctx
     n_blocks = block_order.shape[0]
     block = seq_len // n_blocks
-    heads = D // HEAD // n_ctx
-    width = heads * HEAD
     hidden_blocks = -(-HIDDEN_BLOCKS // n_ctx)
-    hidden = hidden_blocks * LANE
-    scale = HEAD ** (-0.5)
     place = lax.axis_index("ctx")
 
     every = jnp.arange(seq_len, dtype=jnp.int32)
@@ -1283,72 +1518,47 @@
     valid = pos < lengths[0]
     valid_rows = valid.astype(f32)[:, None]
 
-    blocked = (n_ctx, rows_dev, D)
     own_valid = lax.dynamic_slice_in_dim(valid_rows, place * rows_dev, rows_dev)
     own_grad = jnp.where(own_valid > 0, cotangent[0], 0).astype(bf16)
-    g_all = ag_ctx(own_grad)
-    blocks = [hidden_blocks * place + j for j in range(hidden_blocks)]
-    safe = [jnp.minimum(b, HIDDEN_BLOCKS - 1) for b in blocks]
-    starts = [gate_start(b) for b in safe]
-    w_in = ag_shard(columns_at(ffn_in, [s for s, _ in starts] + [s + u for s, u in starts]))
-    w_down = ag_shard(columns_at(ffn_out, [LANE * b for b in safe]))
     picks = routes[0][:, :, None] == jnp.arange(LANE, dtype=jnp.int32)[None, None, :]
     own_assigned = jnp.sum(picks.astype(f32), axis=1).astype(bf16)
     small = jnp.concatenate(
         [
-            norm_gains.reshape(-1),
-            router.T.reshape(-1),
-            shared_gate.reshape(-1),
-            qkv_bias.reshape(-1),
+            norm_gains,
+            router.T,
+            shared_gate.reshape(1, LANE),
+            qkv_bias.reshape(3, LANE),
+            jnp.zeros((4, LANE), bf16),
         ]
-    ).reshape(-1, LANE)
-    small = jnp.pad(small, ((0, 4), (0, 0)))
-    x_all, attn_weights, small_all = front(
-        jnp.concatenate([tokens[0], own_assigned], axis=1), qkv_weight, out_weight, small
     )
-    x_all = x_all.reshape(seq_len, D + LANE)
-    x_all, assigned = x_all[:, :D], x_all[:, D:]
-    attn_weights = attn_weights.reshape(D, 4 * width)
-    small_all = small_all.reshape(n_shard, -1)
-    gains = small_all[:, : 2 * LANE].reshape(n_shard, 2, LANE).transpose(1, 0, 2).reshape(2, D)
-    first_gain, second_gain = gains[0].astype(f32), gains[1].astype(f32)
-    logit_weights = (
-        small_all[:, 2 * LANE : 9 * LANE]
-        .reshape(n_shard, EXPERTS + 1, LANE)
-        .transpose(0, 2, 1)
-        .reshape(D, EXPERTS + 1)
+    cosines, sines = rope_tables(pos)
+    key_pos = jnp.where(valid, pos, 2 * seq_len)[:, None]
+    (
+        residual,
+        second_all,
+        g_all,
+        attn_weights,
+        small_all,
+        first_all,
+        ffn_weights,
+        qkv,
+        mixed,
+        assigned,
+    ) = front(
+        jnp.concatenate([tokens[0], own_assigned], axis=1),
+        own_grad,
+        qkv_weight,
+        out_weight,
+        ffn_in,
+        ffn_out,
+        small,
+        cosines,
+        sines,
+        key_pos,
+        pos[None],
     )
-    bias = small_all[:, 9 * LANE : 12 * LANE].reshape(3 * D)
-    own_bias = jnp.concatenate(
-        [lax.dynamic_slice_in_dim(bias, D * i + width * place, width) for i in range(3)]
-    ).astype(f32)
-    w_qkv, w_out = attn_weights[:, : 3 * width], attn_weights[:, 3 * width :]
-
-    first_normed_all, _ = normalize(x_all.astype(f32))
-    first_all = (first_normed_all * first_gain).astype(bf16)
-    projected = dot(first_all, w_qkv) + own_bias
-    cosines, sines = rope_tables(pos)
-    query = rotate(projected[:, :width].reshape(seq_len, heads, HEAD), cosines, sines).astype(bf16)
-    key = rotate(
-        projected[:, width : 2 * width].reshape(seq_len, heads, HEAD), cosines, sines
-    ).astype(bf16)
-    value = projected[:, 2 * width :].astype(bf16).reshape(seq_len, heads, HEAD)
-    allowed = ((pos[None, :] <= pos[:, None]) & valid[None, :])[None]
-    scores = jnp.einsum("qhd,khd->hqk", query, key, preferred_element_type=f32) * scale
-    masked = jnp.where(allowed, scores, -1e30)
-    peak = jnp.max(masked, axis=-1, keepdims=True)
-    log_total = peak + jnp.log(jnp.sum(jnp.exp(masked - peak), axis=-1, keepdims=True))
-    probs = jnp.exp(masked - log_total)
-    probs_low = probs.astype(bf16)
-    mixed = jnp.einsum("hqk,khd->qhd", probs_low, value, preferred_element_type=f32)
-    mixed = mixed.reshape(seq_len, width).astype(bf16)
-    residual, second_all = middle(
-        contract_last(mixed, w_out).astype(bf16).reshape(n_ctx, rows_dev, D),
-        tokens[0],
-        second_gain[None],
-    )
-
-    block_ids = jnp.stack(blocks)
+
+    block_ids = hidden_blocks * place + jnp.arange(hidden_blocks, dtype=jnp.int32)
     branch_of = jnp.where(
         block_ids < SHARED_BLOCKS, EXPERTS, (block_ids - SHARED_BLOCKS) // EXPERT_BLOCKS
     )
@@ -1357,43 +1567,35 @@
         & (block_ids < HIDDEN_BLOCKS)[None, :]
     ).astype(f32)
     member = jnp.repeat(member, LANE, axis=1)
-    logit_weights = jnp.pad(logit_weights, ((0, 0), (0, LANE - EXPERTS - 1)))
-    grad_residual, output, grad_second_gain, grad_both, act_low, grad_gu = feed_forward(
+    grad_residual, grad_low, output, grad_second_gain, grad_both, act_low, grad_gu = feed_forward(
         second_all,
-        g_all.reshape(blocked),
+        g_all,
         assigned,
-        w_in,
-        w_down,
-        logit_weights,
-        logit_weights.T.astype(f32),
+        ffn_weights.reshape(D, -1),
+        small_all,
         member,
         residual,
         own_grad,
         own_valid,
-        second_gain[None],
     )
-    lane = jnp.arange(HEAD, dtype=jnp.int32)
-    turned_sines = jnp.where(lane < HEAD // 2, sines[:, 0, :], -sines[:, 0, :])
-    qkv_low = jnp.concatenate(
-        [part.reshape(seq_len, width) for part in (query, key, value)], axis=1
-    )
+    first_gain = small_all[:, 0, :].reshape(1, D).astype(f32)
     input_grad, own_small, _, out_share, gate_share, up_share, mixed_share, qkv_share = backward(
-        grad_residual.astype(bf16),
+        grad_low,
         second_all,
-        g_all.reshape(blocked),
+        g_all,
         grad_gu,
         act_low,
-        qkv_low,
+        qkv,
         mixed,
-        attn_weights,
-        first_all.reshape(blocked),
-        cosines[:, 0, :],
-        turned_sines,
-        jnp.where(valid, pos, 2 * seq_len)[:, None],
+        attn_weights.reshape(D, -1),
+        first_all,
+        cosines,
+        sines,
+        key_pos,
         pos[None],
         tokens[0],
         grad_residual,
-        first_gain[None],
+        first_gain,
         grad_second_gain,
         grad_both,
     )
@@ -1403,37 +1605,9 @@
     grad_shared_gate = own_small[8 * LANE : 9 * LANE]
     grad_bias_out = own_small[9 * LANE : 12 * LANE]
 
-    grad_qkv = jnp.concatenate(
-        [
-            qkv_share[p, :, width * i : width * (i + 1)]
-            for i in range(3)
-            for p in range(n_ctx)
-        ],
-        axis=1,
-    ).astype(f32)
-    grad_out = jnp.concatenate(
-        [mixed_share[p] for p in range(n_ctx)], axis=1
-    ).astype(f32)
-
-    def piece(share, first, count):
-        parts = []
-        while count:
-            p, j = first // hidden_blocks, first % hidden_blocks
-            take = min(count, hidden_blocks - j)
-            parts.append(share[p, :, LANE * j : LANE * (j + take)])
-            first, count = first + take, count - take
-        return parts
-
-    spans = [(0, SHARED_BLOCKS)] + [
-        (SHARED_BLOCKS + EXPERT_BLOCKS * e, EXPERT_BLOCKS) for e in range(EXPERTS)
-    ]
-    grad_ffn_in = jnp.concatenate(
-        [part for f, n in spans for share in (gate_share, up_share) for part in piece(share, f, n)],
-        axis=1,
-    ).astype(f32)
-    grad_ffn_out = jnp.concatenate(
-        [part for f, n in spans for part in piece(out_share, f, n)], axis=1
-    ).astype(f32)
+    grad_ffn_out, grad_ffn_in, grad_out, grad_qkv = assemble(
+        out_share, gate_share, up_share, mixed_share, qkv_share
+    )
     return (
         output[None],
         input_grad[None],

time: 701 us -> 576 us (0.82); the launches traced: 691 us -> 575 us
  local copies, waits for them, and re-layouts: 72.9 us -> 11.6 us
  other arithmetic: 38.8 us -> 11.6 us
  between operations: 16.7 us -> 1.4 us
  waiting for transfers between devices: 14.1 us -> 0 us
  Pallas kernels: 537 us -> 551 us
  matrix products: 12 us -> 0 us
    unnamed x181 -> x6, local copies, waits for them, and re-layouts: 55.1 us -> 1.77 us
    pallas_call x2, Pallas kernels: 166 us -> 202 us  [the longest x1 186 us: front(): pl.pallas_call(kernel, out_shape=(shape(rows, width, kind=f32), shape(N_C...]
    convert_element_type x10 -> x1, other arithmetic: 21.4 us -> 1.36 us  [local(): first_gain = small_all[:, 0, :].reshape(1, D).astype(f32)]
    pallas_call x1, Pallas kernels: 243 us -> 224 us  [backward(): pl.pallas_call(kernel, out_shape=(jax.ShapeDtypeStruct((rows, width), f32...]
    all_gather x3 -> x0, waiting for transfers between devices: 14 us -> none  [the longest x2 14 us: ag_shard(): return lax.all_gather(value, 'shard', axis=0, tiled=True)]
    dot_general x4 -> x0, matrix products: 12 us -> none  [the longest x1 3.48 us: dot(): return jnp.dot(left, right, preferred_element_type=jnp.float32)]
  transfers between devices with their start and end apart: 3 -> 0, of which waited for: 1 -> 0; matrix products, arithmetic and copies ran while one was open for 11% -> 0% of each run, Pallas kernels for 24% -> 0%
where the time goes in v3:
time: 576 us; the launch traced here: 575 us
  Pallas kernels  551 us (96%)
  other arithmetic  11.6 us (2%)
  local copies, waits for them, and re-layouts  11.6 us (2%)
    pallas_call x1, Pallas kernels, backward(): pl.pallas_call(kernel, out_shape=(jax.ShapeDtypeStruct((rows, width), f32...  224 us
    pallas_call x1, Pallas kernels, front(): pl.pallas_call(kernel, out_shape=(shape(rows, width, kind=f32), shape(N_C...  186 us
    pallas_call x1, Pallas kernels, feed_forward(): pl.pallas_call(kernel, out_shape=(jax.ShapeDtypeStruct((rows, width), f32...  125 us
    pallas_call x1, Pallas kernels, assemble(): pl.pallas_call(kernel, out_shape=(jax.ShapeDtypeStruct((rows, FOUT), f32)...  16.1 us

profile of v3, /device:TPU:2, one launch (start us, length us, event | category | flops | bytes accessed | tf_op | source)
XLA Modules:
  0.0 575.2 jit_solution(11214754764663080571)
XLA Ops:
  1.4 2.6 concatenate.13.small
  3.9 0.7 select_reduce_fusion
  4.7 0.1 dynamic-slice_bitcast_fusion
  4.8 0.1 broadcast_compare_fusion
  4.9 0.6 fusion.13.query_pos
  5.4 0.1 fusion.10
  5.5 0.8 convert_reduce_fusion
  6.3 0.7 copy.31.own_valid
  7.1 1.9 bitcast_select_fusion.own_grad
  9.0 1.9 pad_maximum_fusion.block
  10.9 0.2 copy.29
  11.1 0.9 compare_select_fusion.key_pos
  12.0 0.1 broadcast_in_dim.64
  12.1 1.2 copy.30.member
  13.3 1.9 fusion.4
  15.2 1.3 pad_maximum_fusion.1
  16.5 185.9 %front.1 = (f32[128,2048]{1,0:T(8,128)}, bf16[8,128,2048]{2,1,0:T(8,128)(2,1)}, bf16[8,128,2048]{2,1,0:T(8,128)(2,1)}, bf16[16,128,1024]{2,1,0:T(8,128)(2,1)}, b...) custom-call(bf16[128,2176]{1,0:T(8,128)(2,1)} %pad_maximum_fusion.bl, ...), custom_call_target="tpu_custom_call" | custom-call | tf_op jit(solution)/shard_map/front/pallas_call | solution.py:702
  202.4 124.7 %feed_forward.1 = (f32[128,2048]{1,0:T(8,128)}, bf16[128,2048]{1,0:T(8,128)(2,1)}, bf16[128,2048]{1,0:T(8,128)(2,1)}, f32[1,2048]{1,0:T(1,128)}, f32[128,128]{1,...) custom-call(bf16[8,128,2048]{2,1,0:T(8,128)(2,1)} %get-tuple-element.38.second, ...), custom_call_target="tpu_custom_call" | custom-call | tf_op jit(solution)/shard_map/feed_forward/pallas_call | solution.py:961
  327.1 1.4 bitcast_convert_fusion.gain
  328.5 223.9 %backward.1 = (f32[128,2048]{1,0:T(8,128)}, f32[16,128]{1,0:T(8,128)}, bf16[8,128,2048]{2,1,0:T(8,128)(2,1)}, bf16[8,128,1792]{2,1,0:T(8,128)(2,1)}, bf16[8,128,...) custom-call(bf16[128,2048]{1,0:T(8,128)(2,1)} %get-tuple-element.45., ...), custom_call_target="tpu_custom_call" | custom-call | tf_op jit(solution)/shard_map/backward/pallas_call | solution.py:1445
  552.3 1.2 slice_bitcast_fusion.2
  553.5 1.2 slice.24
  554.8 1.3 slice_bitcast_fusion.1
  556.0 1.3 slice_bitcast_fusion
  557.3 0.0 copy-start.1
  557.3 0.0 copy-start
  557.3 16.1 %assemble.1 = (f32[128,14080]{1,0:T(8,128)}, f32[128,28160]{1,0:T(8,128)}, f32[128,2048]{1,0:T(8,128)}, f32[128,6144]{1,0:T(8,128)}) custom-call(bf16[8,128,1792]{2,1,0:T(8,128)(2,1)} %get-tuple-element.57.refs_0_, bf16[8,128,1792]{2,1,0:T(8,128)(2,1)} %get-tuple-element.58.refs_1_, bf16[8,128,1792]{2,1,0:T(8,128)(2,1)} %get-tuple-element.59.refs_2_, ...), custom_call_target="tpu_custom_call" | custom-call | tf_op jit(solution)/shard_map/assemble/pallas_call | solution.py:477
  573.4 0.0 copy-done.1
  573.4 0.8 copy.35
  574.2 0.0 copy-done
  574.2 1.0 copy.36
  (7 shorter events, 0.1 us)
Async XLA Ops:
  557.3 16.1 %copy-start.1 = (bf16[128,2048]{1,0:T(8,128)(2,1)S(1)}, bf16[128,2048]{1,0:T(8,128)(2,1)}, u32[]{:S(2)}) copy-start(bf16[128,2048]{1,0:T(8,128)(2,1)} %get-tuple-element.44) | copy-start | bytes 1572868
  557.3 16.9 %copy-start = (f32[128,2048]{1,0:T(8,128)S(1)}, f32[128,2048]{1,0:T(8,128)}, u32[]{:S(2)}) copy-start(f32[128,2048]{1,0:T(8,128)} %get-tuple-element.55) | copy-start | bytes 3145732

commit v4 on v3

--- a/solution.py
+++ b/solution.py
@@ -64,6 +64,7 @@
 VMEM = pl.BlockSpec(memory_space=pltpu.VMEM)
 N_CTX = 8
 CHIPS = 8
+AFTER = 512
 
 
 def params(number, limit=None):
@@ -116,8 +117,9 @@
     SEMAPHORES = 9
     PAIRED = 9 + CHIPS
 
-    def __init__(self, own, out, sends, arrivals, axis="ctx"):
-        self.own, self.out, self.sends, self.arrivals = own, out, sends, arrivals
+    def __init__(self, own, out, sends, arrivals, axis="ctx", columns=None, offset=0):
+        self.block, self.out, self.sends, self.arrivals = own, out, sends, arrivals
+        self.columns, self.offset = columns, offset
         self.places, self.peer = places_of(axis)
         (self.me, self.up, self.down, self.far), other = self.places
         self.other = other[0]
@@ -132,27 +134,48 @@
     def at(self, place, *half):
         if self.paired:
             return self.out.at[(place, self.core) + half]
-        return self.out.at[(place,) + half]
+        if self.columns is None:
+            return self.out.at[(place,) + half]
+        rows = half[0] if half else pl.ds(0, self.out.shape[1])
+        return self.out.at[place, rows, pl.ds(*self.columns)]
+
+    def own(self):
+        if self.columns is None:
+            return self.block
+        return self.block.at[:, pl.ds(*self.columns)]
 
     def _send(self, slot, source, target, peer):
         def copy():
-            return remote(source(), target(), self.sends, self.arrivals, slot, peer())
+            return remote(
+                source(), target(), self.sends, self.arrivals, slot + self.offset, peer()
+            )
 
         copy().start()
         self.started.append(copy)
 
     def _await(self, slot, ref):
-        remote(ref, ref, self.sends, self.arrivals, slot, self.peer(self.other)).wait_recv()
+        peer = self.peer(self.other)
+        remote(ref, ref, self.sends, self.arrivals, slot + self.offset, peer).wait_recv()
 
     def _hand(self, number, place, source=None):
         if self.paired:
             block = lambda: self.at(place)
             self._send(9 + number, source or block, block, lambda: self.mate)
 
+    def _begin(self, slot, place):
+        self._send(slot, self.own, lambda: self.at(self.me), lambda: self.peer(place))
+
+    def begin_other(self):
+        self._begin(0, self.other)
+        self._hand(0, self.me, self.own)
+
+    def begin_ring(self):
+        self._begin(1, self.up)
+        self._begin(2, self.down)
+
     def begin(self):
-        for slot, place in ((0, self.other), (1, self.up), (2, self.down)):
-            self._send(slot, lambda: self.own, lambda: self.at(self.me), lambda place=place: self.peer(place))
-        self._hand(0, self.me, lambda: self.own)
+        self.begin_other()
+        self.begin_ring()
 
     def pass_other(self):
         block = lambda: self.at(self.other)
@@ -189,6 +212,74 @@
                 self._await(9 + number, self.out.at[place, 1 - self.core])
         for copy in self.started:
             copy().wait_send()
+
+
+class RingFirst(Gather):
+    def _across(self, slot, block):
+        self._send(slot, block, block, lambda: self.peer(self.other))
+
+    def pass_other(self):
+        pass
+
+    def pass_ring(self, column):
+        _, up, down, far = self.places[0]
+        low, high = pl.ds(0, self.half), pl.ds(self.half, self.half)
+        if column:
+            for slot, half in ((5, low), (6, high)):
+                self._await(slot, self.at(far, half))
+                self._across(slot + 2, lambda half=half: self.at(far, half))
+            return
+        for slot, place, half, toward in ((1, down, low, self.up), (2, up, high, self.down)):
+            self._await(slot, self.at(place))
+            self._on(slot + 4, place, half, toward)
+            self._across(slot + 2, lambda place=place: self.at(place))
+
+    def _on(self, slot, place, half, toward):
+        block = lambda: self.at(place, half)
+        self._send(slot, block, block, lambda: self.peer(toward))
+
+    def end(self):
+        low, high = pl.ds(0, self.half), pl.ds(self.half, self.half)
+        other, up, down, far = self.places[1]
+        for slot, block in (
+            (0, self.at(other)),
+            (3, self.at(down)),
+            (4, self.at(up)),
+            (7, self.at(far, low)),
+            (8, self.at(far, high)),
+        ):
+            self._await(slot, block)
+        for copy in self.started:
+            copy().wait_send()
+
+
+class Both:
+    SEMAPHORES = 2 * Gather.SEMAPHORES
+
+    def __init__(self, own, out, sends, arrivals, after):
+        width = out.shape[-1]
+        first = Gather(own, out, sends, arrivals, columns=(0, width - after))
+        last = RingFirst(
+            own, out, sends, arrivals, columns=(width - after, after), offset=Gather.SEMAPHORES
+        )
+        self.parts, self.out = (first, last), out
+        self.me, self.up, self.down, self.other = first.me, first.up, first.down, first.other
+
+    def begin(self):
+        for part in self.parts:
+            part.begin()
+
+    def pass_other(self):
+        for part in self.parts:
+            part.pass_other()
+
+    def pass_ring(self, column):
+        for part in self.parts:
+            part.pass_ring(column)
+
+    def end(self):
+        for part in self.parts:
+            part.end()
 
 
 class Reduce:
@@ -510,16 +601,24 @@
     def kernel(
         block, own_grad, qkv_weight, out_weight, ffn_in, ffn_out, small, cosines, sines, key_pos,
         query_pos,
-        residual, second_all, g_all, weights_out, small_all, first_out, ffn_weights, qkv, mixed, assigned,
-        x_all, weights, first, staged, picked, params_all, parts, own, loads, picks, local, *scratch,
+        residual, second_all, g_all, weights_out, small_all, first_out, w_gate, w_up, w_down, qkv,
+        mixed_own, assigned,
+        x_all, weights, first, staged, picked, params_all, mixed, own, parts, loads, picks, local,
+        mixed_sends, mixed_arrivals, *scratch,
     ):
         gather = Gather(block, x_all, *scratch[0:2])
-        spread = Spread(staged, weights, *scratch[2:4])
+        gather_qkv = Gather(staged, weights, *scratch[2:4], axis="shard")
         spread_small = Spread(small, small_all, *scratch[4:6])
-        gather_grad = Gather(own_grad, g_all, *scratch[6:8])
-        gather_second = Gather(own, second_all, *scratch[8:10])
-        gather_ffn = Gather(picked, ffn_weights, *scratch[10:12], axis="shard")
-        reduce = Reduce(parts, parts, *scratch[12:17])
+        gather_grad = Both(own_grad, g_all, *scratch[6:8], AFTER)
+        gather_second = Both(own, second_all, *scratch[8:10], AFTER)
+        w_outs = (w_gate, w_up, w_down)
+        ffn = [
+            Gather(
+                picked.at[:, pl.ds(hidden * k, hidden)], out, *scratch[10 + 2 * k : 12 + 2 * k], axis="shard"
+            )
+            for k, out in enumerate(w_outs)
+        ]
+        reduce = Reduce(parts, parts, *scratch[16:21])
         me = gather.me
         loaded = [
             pltpu.make_async_copy(
@@ -536,41 +635,47 @@
         picking = pick_copies(ffn_in, ffn_out, picked, picks)
         for copy in picking:
             copy.start()
-        greet([{"ctx": p} for p in (gather.other, gather.up, gather.down)] + spread.peers())
+        places = [lax.rem(me + k, N_CTX) for k in range(1, N_CTX)]
+        greet([{"ctx": p} for p in places] + spread_small.peers())
         gather.begin()
         spread_small.begin()
         for copy in loaded:
             copy.wait()
-        spread.begin()
+        gather_qkv.begin()
         for copy in picking:
             copy.wait()
-        gather_ffn.begin()
+        ffn[0].begin()
         kept = [
             pltpu.make_async_copy(source, target, local.at[k])
             for k, (source, target) in enumerate(
                 (
                     (block, x_all.at[me]),
-                    (staged, weights.at[spread.me]),
-                    (small, small_all.at[spread.me]),
+                    (staged, weights.at[spread_small.chip, spread_small.core]),
+                    (small, small_all.at[spread_small.me]),
                     (own_grad, g_all.at[me]),
-                    (picked, ffn_weights.at[spread.chip, spread.core]),
                 )
             )
+        ] + [
+            pltpu.make_async_copy(gather_w.block, gather_w.at(gather_w.me), local.at[4 + k])
+            for k, gather_w in enumerate(ffn)
         ]
         for copy in kept:
             copy.start()
         gather.pass_other()
+        gather_qkv.pass_other()
+        gather_qkv.pass_ring(0)
         spread_small.hand_on()
         gather.pass_ring(0)
-        spread.hand_on()
+        gather_qkv.pass_ring(1)
+        ffn[0].pass_other()
         gather.pass_ring(1)
+        spread_small.end()
+        gather_qkv.end()
+        gather.end()
         gather_grad.begin()
-        spread_small.end()
-        spread.end()
-        gather.end()
+        ffn[1].begin()
         for copy in kept:
             copy.wait()
-        gather_ffn.pass_other()
         weights_kept = pltpu.make_async_copy(weights, weights_out, local.at[0])
         weights_kept.start()
         assigned[...] = x_all[:, :, width:].reshape(seq, extra)
@@ -606,7 +711,7 @@
                 columns = slice(heads_width * i, heads_width * (i + 1))
                 made = biases[i] + jnp.dot(
                     left,
-                    weights[:, :, columns].reshape(width, heads_width),
+                    weights[:, :, :, columns].reshape(width, heads_width),
                     preferred_element_type=f32,
                 )
                 if i == 2:
@@ -618,9 +723,18 @@
                     start = heads_width * i + HEAD * h
                     qkv[there, start : start + HEAD] = turned.astype(bf16)
 
+            @pl.when(n == 0)
+            def _():
+                ffn[0].pass_ring(0)
+
             @pl.when(n == 1)
             def _():
+                ffn[0].pass_ring(1)
+
+            @pl.when(n == 2)
+            def _():
                 gather_grad.pass_other()
+                ffn[1].pass_other()
 
             return carry
 
@@ -628,10 +742,10 @@
         first_kept = pltpu.make_async_copy(first, first_out, local.at[1])
         first_kept.start()
         events = {
-            0: lambda: gather_grad.pass_ring(0),
-            1: lambda: gather_ffn.pass_ring(0),
-            3: lambda: gather_grad.pass_ring(1),
-            7: lambda: gather_ffn.pass_ring(1),
+            0: [lambda: gather_grad.pass_ring(0)],
+            2: [lambda: ffn[1].pass_ring(0)],
+            3: [lambda: gather_grad.pass_ring(1)],
+            5: [lambda: ffn[1].pass_ring(1)],
         }
 
         def attend(n, carry):
@@ -648,19 +762,41 @@
             mixed[there, lanes_of(0)] = contract_first(
                 probs, qkv[:, lanes_of(2 * heads_width)]
             ).astype(bf16)
-            for at, event in events.items():
-                pl.when(n == at)(event)
+            for at, todo in events.items():
+
+                @pl.when(n == at)
+                def _(todo=todo):
+                    for event in todo:
+                        event()
+
             return carry
 
         lax.fori_loop(0, heads * (seq // tile), attend, 0)
+
+        def columns_of(place):
+            return pl.ds(pl.multiple_of(heads_width * place, heads_width), heads_width)
+
+        def rows_of(place):
+            return pl.ds(pl.multiple_of(rows * place, rows), rows)
+
+        to_rows = [
+            remote(
+                mixed.at[rows_of(p), :],
+                mixed_own.at[:, columns_of(me)],
+                mixed_sends,
+                mixed_arrivals,
+                k,
+                {"ctx": p},
+            )
+            for k, p in enumerate(places)
+        ]
 
         def attended(k, carry):
             ahead = 2 - k + 3 * (k // 2) - 2 * (k // 3)
             at = lax.rem(me // 2 + ahead, N_CTX // 2) * 2
             left = mixed[pl.ds(pl.multiple_of(at * rows, tile), tile), :]
-            blocks = 512 // rows
             for t in range(width // 512):
-                right = weights[blocks * t : blocks * (t + 1), :, 3 * heads_width :]
+                right = weights[2 * t : 2 * (t + 1), :, :, 3 * heads_width :]
                 made = contract_last(left, right.reshape(512, heads_width)).astype(bf16)
                 parts[pl.ds(at, 2), :, 512 * t : 512 * (t + 1)] = made.reshape(2, rows, 512)
             pl.when(k == 0)(reduce.send_far)
@@ -669,9 +805,15 @@
             return carry
 
         lax.fori_loop(0, 4, attended, 0)
+        for copy in to_rows:
+            copy.start()
+        ffn[2].begin()
+        mixed_own[:, columns_of(me)] = mixed[rows_of(me), :]
         reduce.pass_side(0)
         reduce.pass_side(1)
         reduce.cross()
+        ffn[2].pass_other()
+        ffn[0].end()
         reduce.ready()
 
         def norm_second(there):
@@ -685,78 +827,189 @@
         second_kept = pltpu.make_async_copy(own, second_all.at[me], local.at[2])
         second_kept.start()
         gather_second.pass_other()
+        ffn[2].pass_ring(0)
         gather_second.pass_ring(0)
+        ffn[2].pass_ring(1)
+        ffn[1].end()
         gather_second.pass_ring(1)
         gather_grad.end()
-        gather_ffn.end()
+        for k, p in enumerate(places):
+            ref = mixed_own.at[:, columns_of(lax.rem(me + N_CTX - 1 - k, N_CTX))]
+            remote(ref, ref, mixed_sends, mixed_arrivals, k, {"ctx": p}).wait_recv()
+        for copy in to_rows:
+            copy.wait_send()
         reduce.end()
         for copy in (weights_kept, first_kept, second_kept):
             copy.wait()
         gather_second.end()
+        ffn[2].end()
 
     def shape(*dims, kind=bf16):
         return jax.ShapeDtypeStruct(dims, kind)
 
-    pair = [pltpu.SemaphoreType.DMA((Gather.SEMAPHORES,))] * 2
-    spread_pair = [pltpu.SemaphoreType.DMA((Spread.SEMAPHORES,))] * 2
+    pair = [pltpu.SemaphoreType.DMA((Both.SEMAPHORES,))] * 2
+    paired = [pltpu.SemaphoreType.DMA((Gather.PAIRED,))] * 2
     return pl.pallas_call(
         kernel,
         out_shape=(
             shape(rows, width, kind=f32),
             shape(N_CTX, rows, width),
             shape(N_CTX, rows, width),
-            shape(n_shard, rows, 4 * heads_width),
+            shape(CHIPS, 2, rows, 4 * heads_width),
             shape(n_shard, 16, 128),
             shape(N_CTX, rows, width),
-            shape(CHIPS, 2, rows, 3 * hidden),
+            shape(CHIPS, 2, rows, hidden),
+            shape(CHIPS, 2, rows, hidden),
+            shape(CHIPS, 2, rows, hidden),
             shape(seq, 3 * heads_width),
-            shape(seq, heads_width),
+            shape(rows, width),
             shape(seq, extra),
         ),
         in_specs=[ANY, VMEM] + [ANY] * 5 + [VMEM] * 4,
-        out_specs=(VMEM, ANY, ANY, ANY, VMEM, ANY, ANY, VMEM, VMEM, VMEM),
+        out_specs=(VMEM, ANY, ANY, ANY, VMEM, ANY, ANY, ANY, ANY, VMEM, VMEM, VMEM),
         scratch_shapes=[
             pltpu.VMEM((N_CTX,) + block.shape, bf16),
-            pltpu.VMEM((n_shard, rows, 4 * heads_width), bf16),
+            pltpu.VMEM((CHIPS, 2, rows, 4 * heads_width), bf16),
             pltpu.VMEM((N_CTX, rows, width), bf16),
             pltpu.VMEM((rows, 4 * heads_width), bf16),
             pltpu.VMEM((rows, 3 * hidden), bf16),
             pltpu.VMEM((n_shard, 16, 128), f32),
+            pltpu.VMEM((seq, heads_width), bf16),
+            pltpu.VMEM((rows, width), bf16),
             pltpu.VMEM((N_CTX, rows, width), bf16),
-            pltpu.VMEM((rows, width), bf16),
             pltpu.SemaphoreType.DMA((4,)),
             pltpu.SemaphoreType.DMA((3 * hidden // LANE,)),
-            pltpu.SemaphoreType.DMA((5,)),
+            pltpu.SemaphoreType.DMA((7,)),
+            pltpu.SemaphoreType.DMA((N_CTX - 1,)),
+            pltpu.SemaphoreType.DMA((N_CTX - 1,)),
         ]
         + pair
-        + spread_pair * 2
+        + paired
+        + [pltpu.SemaphoreType.DMA((Spread.SEMAPHORES,))] * 2
         + pair * 2
-        + [pltpu.SemaphoreType.DMA((Gather.PAIRED,))] * 2
+        + paired * 3
         + Reduce.scratch(rows, width, 1),
         compiler_params=params(0, 56 << 20),
         name="front",
     )(block, own_grad, qkv_weight, out_weight, ffn_in, ffn_out, small, cosines, sines, key_pos, query_pos)
 
 
-def feed_forward(second, grad_out, assigned, ffn_weights, small, member, residual, own_grad, own_valid):
+class Exchange:
+    @staticmethod
+    def scratch():
+        return [pltpu.SemaphoreType.DMA((CHIPS,)), pltpu.SemaphoreType.DMA((CHIPS,))]
+
+    def __init__(self, parts, staged, sends, arrivals):
+        self.parts, self.staged = parts, staged
+        self.sems = (sends, arrivals)
+        self.width = parts.shape[2]
+        me = lax.axis_index("shard")
+        self.core, self.chip = lax.rem(me, 2), me // 2
+        self.mate = {"shard": me + 1 - 2 * self.core}
+
+    def chip_at(self, step):
+        base = self.chip + (1 - lax.rem(step, 2)) * (1 - 2 * lax.rem(self.chip, 2))
+        b = step // 2
+        ahead = 2 - b + 3 * (b // 2) - 2 * (b // 3)
+        return 2 * lax.rem(base // 2 + ahead, 4) + lax.rem(base, 2)
+
+    def stage(self, slot, core):
+        if len(self.staged.shape) == 2:
+            return self.staged.at[pl.ds(pl.multiple_of((2 * slot + core) * 128, 128), 128), :]
+        return self.staged.at[slot, core]
+
+    def columns_at(self, step):
+        return pl.ds(pl.multiple_of(self.chip_at(step) * 256, 256), 256)
+
+    def _pair(self, step):
+        return remote(
+            self.stage(lax.rem(step, 3), 1 - self.core).at[:, pl.ds(0, self.width)],
+            self.parts.at[self.chip_at(step)],
+            *self.sems,
+            step,
+            self.mate,
+        )
+
+    def finish(self, step):
+        chip, slot, width = self.chip_at(step), lax.rem(step, 3), self.width
+        ref = self.parts.at[chip]
+        remote(ref, ref, *self.sems, step, self.mate).wait_recv()
+
+        def add(there):
+            total = self.parts[chip, there, :].astype(jnp.float32)
+            total = total + self.stage(slot, self.core)[there, 0:width].astype(jnp.float32)
+            self.parts[chip, there, :] = total.astype(jnp.bfloat16)
+
+        by_rows(128, add)
+
+    def run(self, left, right, turned, between):
+        width = self.width
+        tile = 896 if width % 896 == 0 else min(width, 1024)
+
+        def step_of(step, carry):
+            @pl.when(step >= 3)
+            def _():
+                self._pair(step - 3).wait_send()
+
+            slot = lax.rem(step, 3)
+            rows = left(step)
+            depth = rows.shape[0]
+            turned[:, 0:depth] = rows.T
+            for start in range(0, width, tile):
+                made = jnp.dot(
+                    turned[:, 0:depth], right(start, tile), preferred_element_type=jnp.float32
+                ).astype(jnp.bfloat16)
+                self.stage(slot, 0)[:, start : start + tile] = made[:128]
+                self.stage(slot, 1)[:, start : start + tile] = made[128:]
+            self._pair(step).start()
+
+            @pl.when(step >= 2)
+            def _():
+                self.finish(step - 2)
+
+            for at, events in between.items():
+
+                @pl.when(step == at)
+                def _(events=events):
+                    for event in events:
+                        event()
+
+            return carry
+
+        lax.fori_loop(0, CHIPS, step_of, 0)
+        self.finish(CHIPS - 2)
+        self.finish(CHIPS - 1)
+        for step in range(CHIPS - 3, CHIPS):
+            self._pair(step).wait_send()
+
+
+def feed_forward(second, grad_out, assigned, w_gate, w_up, w_down, out_weight, small, residual, own_grad, own_valid):
     _, rows, width = second.shape
     seq = rows * N_CTX
-    hidden = ffn_weights.shape[1] // 3
+    hidden = w_gate.shape[1]
     lanes = 128
     n_shard = small.shape[0]
     pair = 2 * rows
-    tile = 256
+    tile = 896
     f32, bf16 = jnp.float32, jnp.bfloat16
 
     def kernel(
-        second, grad_out, assigned, ffn_weights, small, member, residual, own_grad, own_valid,
-        grad_residual, grad_low, output, grad_gain, grad_logits, act_out, grad_gu_out,
+        second, grad_out, assigned, w_gate, w_up, w_down, out_weight, small, residual, own_grad, own_valid,
+        grad_residual, grad_low, grad_mixed, output, grad_gain, grad_logits, act_out, grad_gu_out,
+        out_weights, out_owned,
         second_held, grad_held, in_held, down_held, act, grad_gu, weights, dots, dots_in, gain_sum,
-        logit_rows, logit_low,
+        logit_low, out_sems,
         back_parts, ffn_parts, dot_sends, dot_arrivals, loads, weight_loads, stores, *scratch,
     ):
         back = Reduce(back_parts, back_parts, *scratch[:5])
-        ahead = Reduce(ffn_parts, ffn_parts, *scratch[5:])
+        ahead = Reduce(ffn_parts, ffn_parts, *scratch[5:10])
+        gather_out = Gather(out_weight, out_weights, *scratch[10:12], axis="shard")
+        share, act_held = down_held.at[pl.ds(0, CHIPS)], down_held.at[pl.ds(CHIPS, N_CTX)]
+        staged = in_held.at[pl.ds(0, 768), pl.ds(0, hidden)]
+        turned = in_held.at[pl.ds(768, 256), pl.ds(0, seq)]
+        exchange = Exchange(share, staged, *scratch[12:14])
+        sums = Reduce(share, share, *scratch[14:19], axis="shard")
+        free = scratch[19]
         own, other = back.places
         me = own[0]
         peers = [lax.rem(me + k, N_CTX) for k in range(1, N_CTX)]
@@ -769,11 +1022,12 @@
 
         def weight_copies(t):
             copies = []
-            for k, (target, there, here) in enumerate(
-                ((in_held, 0, 0), (in_held, hidden, hidden), (down_held, 2 * hidden, 0))
+            for k, (source, target, here) in enumerate(
+                ((w_gate, in_held, 0), (w_up, in_held, hidden), (w_down, down_held, 0))
             ):
-                source = ffn_weights.at[:, pl.ds(pl.multiple_of(there + tile * t, tile), tile)]
-                target = target.at[:, pl.ds(pl.multiple_of(here + tile * t, tile), tile)]
+                every = (slice(None),) * (len(target.shape) - 1)
+                source = source.at[every + (pl.ds(pl.multiple_of(tile * t, tile), tile),)]
+                target = target.at[every + (pl.ds(pl.multiple_of(here + tile * t, tile), tile),)]
                 copies.append(pltpu.make_async_copy(source, target, weight_loads.at[3 * t + k]))
             return copies
 
@@ -783,23 +1037,33 @@
             return carry
 
         lax.fori_loop(0, hidden // tile, start_weights, 0)
-        greet([{"ctx": p} for p in peers])
-        logit_rows[...] = jnp.zeros_like(logit_rows)
+        shard_peers = [gather_out.peer(p) for p in (gather_out.up, gather_out.down, gather_out.other)]
+        greet([{"ctx": p} for p in peers] + shard_peers + [gather_out.mate])
+        gather_out.begin()
+        out_kept = pltpu.make_async_copy(
+            out_weight, out_weights.at[gather_out.me, gather_out.core], loads.at[2]
+        )
+        out_kept.start()
+        logit_low[...] = jnp.zeros_like(logit_low)
         gains = []
         for s in range(n_shard):
             held = small[s].astype(f32)
             gains.append(held[1:2])
-            logit_rows[0 : EXPERTS + 1, 128 * s : 128 * (s + 1)] = held[2 : 3 + EXPERTS]
+            part = jnp.concatenate([held[2 : 3 + EXPERTS], jnp.zeros((15 - EXPERTS, 128), f32)], axis=0)
+            logit_low[0:16, 128 * s : 128 * (s + 1)] = part.astype(bf16)
         gain = jnp.concatenate(gains, axis=1)
-        logit_low[...] = logit_rows[...].astype(bf16)
         for copy in copies:
             copy.wait()
 
         def stored(slot, start):
             there = pl.ds(start, pair)
             return [
-                pltpu.make_async_copy(act.at[slot], act_out.at[there, :], stores.at[slot, 0]),
-                pltpu.make_async_copy(grad_gu.at[slot], grad_gu_out.at[there, :], stores.at[slot, 1]),
+                pltpu.make_async_copy(
+                    act.at[slot, pl.ds(rows * k, rows)], act_out.at[start // rows + k], stores.at[slot, 1 + k]
+                )
+                for k in range(2)
+            ] + [
+                pltpu.make_async_copy(grad_gu.at[slot], grad_gu_out.at[there, :], stores.at[slot, 0]),
             ]
 
         def dot_copy(slot, place):
@@ -811,14 +1075,20 @@
             ahead = 2 - b + 3 * (b // 2) - 2 * (b // 3)
             return pl.multiple_of(lax.rem(me // 2 + ahead, N_CTX // 2) * pair, pair)
 
+        def branch_of(j):
+            at = me * (hidden // LANE) + j
+            routed = (at // SHARED_BLOCKS + 1) // 2
+            expert = (at - SHARED_BLOCKS) // EXPERT_BLOCKS
+            return (1 - routed) * EXPERTS + routed * expert + 100 * (at // HIDDEN_BLOCKS)
+
         def block(b, carry):
             start = start_of(b)
-            slot = lax.rem(b, 2)
+            slot = 0
             first = pl.multiple_of(start // rows, 2)
 
-            @pl.when(b >= 2)
+            @pl.when(b >= 1)
             def _():
-                for copy in stored(slot, start_of(b - 2)):
+                for copy in stored(slot, start_of(b - 1)):
                     copy.wait()
 
             def rows_of(ref):
@@ -846,25 +1116,34 @@
                 rows_in = rows_of(second_held)
                 gate = jnp.dot(rows_in, in_held[:, low], preferred_element_type=f32)
                 upward = jnp.dot(rows_in, in_held[:, high], preferred_element_type=f32)
-                raw = jnp.dot(rows_of(grad_held), down_held[:, low], preferred_element_type=f32)
-                held = jnp.dot(
-                    weights[pl.ds(start, pair), :],
-                    member[:, low],
-                    precision=highest,
+                raw = jnp.dot(
+                    rows_of(grad_held),
+                    down_held[:, :, low].reshape(width, tile),
                     preferred_element_type=f32,
+                )
+                gates = weights[pl.ds(start, pair), :]
+                lane = lax.broadcasted_iota(jnp.int32, gates.shape, 1)
+                branches = [branch_of(tile // LANE * t + j) for j in range(tile // LANE)]
+                held = jnp.concatenate(
+                    [
+                        jnp.broadcast_to(
+                            jnp.sum(jnp.where(lane == n, gates, 0.0), axis=1, keepdims=True),
+                            (pair, LANE),
+                        )
+                        for n in branches
+                    ],
+                    axis=1,
                 )
                 squashed = jax.nn.sigmoid(gate)
                 swished = gate * squashed
                 value = swished * upward
                 act[slot, :, low] = (value * held).astype(bf16)
-                part = lax.dot_general(
-                    raw * value,
-                    member[:, low],
-                    (((1,), (1,)), ((), ())),
-                    precision=highest,
-                    preferred_element_type=f32,
-                )
-                dots[pl.ds(first, 2)] += part.reshape(2, rows, lanes)
+                products = raw * value
+                part = dots[pl.ds(first, 2)].reshape(pair, lanes)
+                for j, n in enumerate(branches):
+                    inner = jnp.sum(products[:, LANE * j : LANE * (j + 1)], axis=1, keepdims=True)
+                    part = part + jnp.where(lane == n, inner, 0.0)
+                dots[pl.ds(first, 2)] = part.reshape(2, rows, lanes)
                 grad = raw * held
                 grad_gu[slot, :, low] = (
                     grad * upward * squashed * (1.0 + gate * (1.0 - squashed))
@@ -879,10 +1158,10 @@
             def out_tile(t, carry):
                 there = pl.ds(pl.multiple_of(512 * t, 512), 512)
                 for parts, left, right in (
-                    (back_parts, grad_gu, in_held),
-                    (ffn_parts, act, down_held),
+                    (back_parts, grad_gu, lambda: in_held[there, :]),
+                    (ffn_parts, act, lambda: down_held[pl.ds(4 * t, 4)].reshape(512, hidden)),
                 ):
-                    made = contract_last(left[slot], right[there, :])
+                    made = contract_last(left[slot], right())
                     parts[pl.ds(first, 2), :, there] = made.astype(bf16).reshape(2, rows, 512)
                 return carry
 
@@ -905,12 +1184,44 @@
             pl.when(b == 0)(far)
             pl.when(b == 1)(lambda: near(0))
             pl.when(b == 2)(lambda: near(1))
+            pl.when(b == 0)(gather_out.pass_other)
+            pl.when(b == 1)(lambda: gather_out.pass_ring(0))
+            pl.when(b == 2)(lambda: gather_out.pass_ring(1))
             return carry
 
         lax.fori_loop(0, 4, block, 0)
         dot_copy(6, other[0]).start()
-        back.cross()
+        for copy in stored(0, start_of(3)):
+            copy.wait()
+        act_load = pltpu.make_async_copy(act_out, act_held, loads.at[0])
+        act_load.start()
+        pl.semaphore_signal(free, inc=1, device_id=gather_out.mate, device_id_type=MESH)
+        out_kept.wait()
+        gather_out.end()
+        pl.semaphore_wait(free, 1)
+        act_load.wait()
+        exchange.run(
+            lambda step: grad_held[:, :, exchange.columns_at(step)].reshape(seq, 256),
+            lambda start, count: down_held[CHIPS:, :, start : start + count].reshape(seq, count),
+            turned,
+            {
+                2: [back.cross],
+                3: [sums.send_far],
+                5: [lambda: sums.send_near(0)],
+                7: [lambda: sums.send_near(1)],
+            },
+        )
+        out_loads = [
+            pltpu.make_async_copy(
+                out_weights.at[n // 2, n % 2], in_held.at[128 * n : 128 * (n + 1), 0:width], out_sems.at[n]
+            )
+            for n in range(n_shard)
+        ]
+        for copy in out_loads:
+            copy.start()
         ahead.cross()
+        sums.pass_side(0)
+        sums.pass_side(1)
         back.ready()
         for k in range(7):
             ref = dots_in.at[k]
@@ -927,10 +1238,18 @@
             held * (total_dots - centre),
             jnp.where(lane == EXPERTS, total_dots * held * (1.0 - held), 0.0),
         )
-        grad_logits[...] = both
-        grad_residual[...] = jnp.dot(
-            both, logit_rows[...], precision=highest, preferred_element_type=f32
-        )
+        grad_logits[...] = lax.dot_general(
+            both,
+            second_held[me].astype(f32),
+            (((0,), (0,)), ((), ())),
+            precision=highest,
+            preferred_element_type=f32,
+        )[0:8]
+        for t in range(width // 512):
+            there = slice(512 * t, 512 * (t + 1))
+            grad_residual[:, there] = jnp.dot(
+                both, logit_low[:, there].astype(f32), precision=highest, preferred_element_type=f32
+            )
         gain_sum[...] = jnp.zeros_like(gain_sum)
 
         def norm(there):
@@ -943,6 +1262,13 @@
 
         by_rows(rows, norm)
         grad_gain[...] = jnp.sum(gain_sum[...], axis=0, keepdims=True)
+        for copy in out_loads:
+            copy.wait()
+        for t in range(width // 512):
+            there = slice(512 * t, 512 * (t + 1))
+            grad_mixed[:, there] = jnp.dot(
+                grad_low[...], in_held[:, there], preferred_element_type=f32
+            ).astype(bf16)
         ahead.ready()
 
         def finish(there):
@@ -950,9 +1276,14 @@
             output[there, :] = (total * own_valid[there, :]).astype(bf16)
 
         by_rows(rows, finish)
-        for b in (2, 3):
-            for copy in stored(b % 2, start_of(b)):
-                copy.wait()
+        sums.cross()
+        sums.ready()
+
+        def keep(there):
+            out_owned[there, :] = sums.total(there).astype(bf16)
+
+        by_rows(128, keep)
+        sums.end()
         back.end()
         ahead.end()
         for slot, place in enumerate((own[3], other[3], own[1], other[1], own[2], other[2], other[0])):
@@ -964,127 +1295,56 @@
             jax.ShapeDtypeStruct((rows, width), f32),
             jax.ShapeDtypeStruct((rows, width), bf16),
             jax.ShapeDtypeStruct((rows, width), bf16),
+            jax.ShapeDtypeStruct((rows, width), bf16),
             jax.ShapeDtypeStruct((1, width), f32),
-            jax.ShapeDtypeStruct((rows, lanes), f32),
-            jax.ShapeDtypeStruct((seq, hidden), bf16),
+            jax.ShapeDtypeStruct((8, width), f32),
+            jax.ShapeDtypeStruct((N_CTX, rows, hidden), bf16),
             jax.ShapeDtypeStruct((seq, 2 * hidden), bf16),
+            jax.ShapeDtypeStruct((CHIPS, 2, rows, width), bf16),
+            jax.ShapeDtypeStruct((128, hidden), bf16),
         ),
-        in_specs=[ANY, ANY, VMEM, ANY] + [VMEM] * 5,
-        out_specs=(VMEM,) * 5 + (ANY, ANY),
+        in_specs=[ANY, ANY, VMEM] + [ANY] * 4 + [VMEM] * 4,
+        out_specs=(VMEM,) * 6 + (ANY,) * 3 + (VMEM,),
         scratch_shapes=[
             pltpu.VMEM(second.shape, bf16),
             pltpu.VMEM(grad_out.shape, bf16),
             pltpu.VMEM((width, 2 * hidden), bf16),
-            pltpu.VMEM((width, hidden), bf16),
-            pltpu.VMEM((2, pair, hidden), bf16),
-            pltpu.VMEM((2, pair, 2 * hidden), bf16),
+            pltpu.VMEM((width // 128, 128, hidden), bf16),
+            pltpu.VMEM((1, pair, hidden), bf16),
+            pltpu.VMEM((1, pair, 2 * hidden), bf16),
             pltpu.VMEM((seq, lanes), f32),
             pltpu.VMEM((N_CTX, rows, lanes), f32),
             pltpu.VMEM((N_CTX - 1, rows, lanes), f32),
             pltpu.VMEM((16, width), f32),
-            pltpu.VMEM((lanes, width), f32),
             pltpu.VMEM((lanes, width), bf16),
+            pltpu.SemaphoreType.DMA((n_shard,)),
             pltpu.VMEM(second.shape, bf16),
             pltpu.VMEM(second.shape, bf16),
             pltpu.SemaphoreType.DMA((N_CTX - 1,)),
             pltpu.SemaphoreType.DMA((N_CTX - 1,)),
-            pltpu.SemaphoreType.DMA((2,)),
+            pltpu.SemaphoreType.DMA((3,)),
             pltpu.SemaphoreType.DMA((3 * hidden // tile,)),
-            pltpu.SemaphoreType.DMA((2, 2)),
+            pltpu.SemaphoreType.DMA((1, 3)),
         ]
-        + Reduce.scratch(rows, width, 1) * 2,
+        + Reduce.scratch(rows, width, 1) * 2
+        + [pltpu.SemaphoreType.DMA((Gather.PAIRED,))] * 2
+        + Exchange.scratch()
+        + Reduce.scratch(128, hidden, 1)
+        + [pltpu.SemaphoreType.REGULAR],
         compiler_params=params(2, 64 << 20),
         name="feed_forward",
-    )(second, grad_out, assigned, ffn_weights, small, member, residual, own_grad, own_valid)
-
-
-class Exchange:
-    @staticmethod
-    def scratch():
-        return [pltpu.SemaphoreType.DMA((CHIPS,)), pltpu.SemaphoreType.DMA((CHIPS,))]
-
-    def __init__(self, parts, staged, sends, arrivals):
-        self.parts, self.staged = parts, staged
-        self.sems = (sends, arrivals)
-        self.width = parts.shape[2]
-        me = lax.axis_index("shard")
-        self.core, self.chip = lax.rem(me, 2), me // 2
-        self.mate = {"shard": me + 1 - 2 * self.core}
-
-    def chip_at(self, step):
-        base = self.chip + (1 - lax.rem(step, 2)) * (1 - 2 * lax.rem(self.chip, 2))
-        b = step // 2
-        ahead = 2 - b + 3 * (b // 2) - 2 * (b // 3)
-        return 2 * lax.rem(base // 2 + ahead, 4) + lax.rem(base, 2)
-
-    def _pair(self, step):
-        return remote(
-            self.staged.at[lax.rem(step, 2), 1 - self.core, :, pl.ds(0, self.width)],
-            self.parts.at[self.chip_at(step)],
-            *self.sems,
-            step,
-            self.mate,
-        )
-
-    def finish(self, step):
-        chip, slot, width = self.chip_at(step), lax.rem(step, 2), self.width
-        ref = self.parts.at[chip]
-        remote(ref, ref, *self.sems, step, self.mate).wait_recv()
-
-        def add(there):
-            total = self.parts[chip, there, :].astype(jnp.float32)
-            total = total + self.staged[slot, self.core, there, 0:width].astype(jnp.float32)
-            self.parts[chip, there, :] = total.astype(jnp.bfloat16)
-
-        by_rows(128, add)
-
-    def run(self, left, right, turned, between):
-        width = self.width
-        tile = 896 if width % 896 == 0 else width
-
-        def step_of(step, carry):
-            @pl.when(step >= 2)
-            def _():
-                self._pair(step - 2).wait_send()
-
-            slot = lax.rem(step, 2)
-            columns = pl.ds(pl.multiple_of(self.chip_at(step) * 256, 256), 256)
-            turned[...] = left[:, :, columns].reshape(turned.shape[1], 256).T
-            for start in range(0, width, tile):
-                made = jnp.dot(
-                    turned[...], right(start, tile), preferred_element_type=jnp.float32
-                ).astype(jnp.bfloat16)
-                self.staged[slot, 0, :, start : start + tile] = made[:128]
-                self.staged[slot, 1, :, start : start + tile] = made[128:]
-            self._pair(step).start()
-
-            @pl.when(step >= 1)
-            def _():
-                self.finish(step - 1)
-
-            for at, events in between.items():
-
-                @pl.when(step == at)
-                def _(events=events):
-                    for event in events:
-                        event()
-
-            return carry
-
-        lax.fori_loop(0, CHIPS, step_of, 0)
-        self.finish(CHIPS - 1)
-        for step in (CHIPS - 2, CHIPS - 1):
-            self._pair(step).wait_send()
+    )(second, grad_out, assigned, w_gate, w_up, w_down.reshape(width // 128, 128, hidden), out_weight, small, residual, own_grad, own_valid)
 
 
 class Share:
     @staticmethod
-    def scratch(width):
+    def scratch(width, split=1):
+        own = width // split
         return (
-            [pltpu.VMEM((CHIPS, 128, width), jnp.bfloat16), pltpu.VMEM((128, width), jnp.bfloat16)]
+            [pltpu.VMEM((CHIPS, 128, width), jnp.bfloat16), pltpu.VMEM((128, own), jnp.bfloat16)]
             + Exchange.scratch()
             + Reduce.scratch(128, width, 1)
-            + [pltpu.SemaphoreType.DMA((Gather.SEMAPHORES,))] * 2
+            + [pltpu.SemaphoreType.DMA((Both.SEMAPHORES,))] * 2
             + [pltpu.SemaphoreType.DMA]
         )
 
@@ -1094,7 +1354,10 @@
         parts, self.owned = scratch[0:2]
         self.exchange = Exchange(parts, staged, *scratch[2:4])
         self.reduce = Reduce(parts, parts, *scratch[4:9], axis="shard")
-        self.gather = Gather(self.owned, out, *scratch[9:11])
+        if out.shape[-1] > 2 * AFTER:
+            self.gather = Both(self.owned, out, *scratch[9:11], AFTER)
+        else:
+            self.gather = Gather(self.owned, out, *scratch[9:11])
         self.local = scratch[11]
 
     def near(self, side):
@@ -1107,12 +1370,18 @@
         return lambda: self.gather.pass_ring(column)
 
     def own(self):
+        self.sum_into(self.owned)
+        self.pass_own()
+
+    def sum_into(self, ref):
         self.reduce.ready()
 
         def keep(there):
-            self.owned[there, :] = self.reduce.total(there).astype(jnp.bfloat16)
+            ref[there, :] = self.reduce.total(there).astype(jnp.bfloat16)
 
         by_rows(128, keep)
+
+    def pass_own(self):
         self.gather.begin()
         self._kept().start()
 
@@ -1127,35 +1396,37 @@
         self.reduce.end()
 
 
-def backward(own, second, grad_out, grad_gu, act, qkv, mixed, weights, first, cosines, sines, key_pos, query_pos, inputs, grad_residual, gain, second_gain_grad, grad_logits):
+def backward(own, grad_mixed, mixed, out_own, second, grad_gu, qkv, weights, first, cosines, sines, key_pos, query_pos, inputs, grad_residual, gain, second_gain_grad, logits_grad):
     rows, width = own.shape
     seq = rows * N_CTX
-    hidden = act.shape[1]
-    heads_width = mixed.shape[1]
+    hidden = out_own.shape[1]
+    heads_width = width // N_CTX
     heads = heads_width // HEAD
-    lanes = grad_logits.shape[1]
     n_shard = width // 128
     f32, bf16 = jnp.float32, jnp.bfloat16
     scale = HEAD ** (-0.5)
     tile = 256
     half = width // 2
+    columns_grad = 3 * heads_width
 
     def kernel(
-        own, second, grad_out, grad_gu, act, qkv, mixed, weights, first, cosines, sines, key_pos,
-        query_pos, inputs, grad_residual, gain, second_gain_grad, grad_logits,
-        input_grad, small_out, grad_attended, out_share, gate_share, up_share, mixed_share, qkv_share,
-        second_held, g_held, gu_held, act_held, turned, staged, key_sum, value_sum, gain_sum,
-        small, small_in, small_kept, small_across,
-        loads, local, small_sends, small_arrivals, across_sends, across_arrivals, *scratch,
+        own, grad_mixed, mixed, out_own, second, grad_gu, qkv, weights, first,
+        cosines, sines, key_pos, query_pos, inputs, grad_residual, gain, second_gain_grad, logits_grad,
+        input_grad, small_out, out_share, gate_share, up_share, mixed_share, qkv_share,
+        grad_held, parts, left_held, gu_held, w_held, turned, staged, key_sum, value_sum, gain_sum,
+        small, small_in, small_kept, small_across, mixed_in,
+        loads, left_loads, grad_sends, grad_arrivals, mixed_sends, mixed_arrivals,
+        small_sends, small_arrivals, across_sends, across_arrivals, *scratch,
     ):
-        gather = Gather(own, grad_attended, *scratch[0:2])
-        reduce = Reduce(g_held, g_held, *scratch[2:7])
+        reduce = Reduce(parts, parts, *scratch[0:5])
         shares = []
-        for k, out in enumerate((out_share, gate_share, up_share, mixed_share, qkv_share)):
-            start = 7 + Share.COUNT * k
+        for k, out in enumerate((gate_share, up_share, mixed_share, qkv_share)):
+            start = 8 + Share.COUNT * k
             shares.append(Share(staged, out, scratch[start : start + Share.COUNT]))
-        a, b, c, d, e = shares
-        me = gather.me
+        b, c, d, e = shares
+        gather = Both(out_own, out_share, *scratch[5:7], AFTER)
+        local = scratch[7]
+        me = reduce.places[0][0]
         shard = lax.axis_index("shard")
         owners = [lax.rem(shard + k, n_shard) for k in range(1, n_shard)]
         places = [lax.rem(me + k, N_CTX) for k in range(1, N_CTX)]
@@ -1163,130 +1434,99 @@
         def load(k, source, target):
             return pltpu.make_async_copy(source, target, loads.at[k])
 
-        early = [
-            load(0, grad_out, g_held),
-            load(1, act, act_held),
-            load(2, second, second_held),
-            load(3, grad_gu, gu_held),
-        ]
+        def columns_of(place):
+            return pl.ds(pl.multiple_of(heads_width * place, heads_width), heads_width)
+
+        def left_copy(source, step):
+            slot = lax.rem(step, 2)
+            return pltpu.make_async_copy(
+                source.at[:, :, b.exchange.columns_at(step)], left_held.at[slot], left_loads.at[slot]
+            )
+
+        def streamed(source):
+            left_copy(source, 0).start()
+
+            def left(step):
+                @pl.when(step < CHIPS - 1)
+                def _():
+                    left_copy(source, step + 1).start()
+
+                left_copy(source, step).wait()
+                return left_held[lax.rem(step, 2)].reshape(seq, 256)
+
+            return left
+
+        early = [load(1, grad_gu, gu_held), load(3, grad_residual, input_grad)]
         for copy in early:
             copy.start()
+        left = streamed(second)
         greet([{"ctx": p} for p in places] + [{"shard": s} for s in owners])
+        to_heads = [
+            remote(
+                grad_mixed.at[:, columns_of(p)], grad_held.at[me], grad_sends, grad_arrivals, k, {"ctx": p}
+            )
+            for k, p in enumerate(places)
+        ]
+        for copy in to_heads:
+            copy.start()
+        grad_held[me] = grad_mixed[:, columns_of(me)]
         gather.begin()
-        kept = pltpu.make_async_copy(own, grad_attended.at[me], local)
+        kept = pltpu.make_async_copy(out_own, out_share.at[me], local)
         kept.start()
+        late = [
+            load(
+                2 * k,
+                weights.at[pl.ds(half * k, half), pl.ds(0, columns_grad)],
+                w_held.at[:, columns_grad * k : columns_grad * (k + 1)],
+            )
+            for k in range(2)
+        ]
+        for copy in late:
+            copy.start()
         early[0].wait()
-        early[1].wait()
-        a.exchange.run(
-            g_held,
-            lambda start, count: act_held[:, start : start + count],
-            turned,
-            {
-                2: [a.reduce.send_far],
-                4: [a.near(0)],
-                6: [a.near(1), gather.pass_other],
-            },
-        )
-        early[2].wait()
-        early[3].wait()
         b.exchange.run(
-            second_held,
+            left,
             lambda start, count: gu_held[:, start : start + count],
             turned,
             {
-                0: [a.side(0)],
-                1: [a.side(1)],
-                2: [b.reduce.send_far],
-                3: [lambda: gather.pass_ring(0)],
-                4: [b.near(0)],
-                6: [b.near(1), lambda: gather.pass_ring(1)],
+                3: [b.reduce.send_far],
+                4: [gather.pass_other],
+                5: [b.near(0)],
+                7: [b.near(1)],
             },
         )
         c.exchange.run(
-            second_held,
+            streamed(second),
             lambda start, count: gu_held[:, hidden + start : hidden + start + count],
             turned,
             {
-                2: [c.reduce.send_far],
-                4: [c.near(0)],
-                5: [a.reduce.cross],
-                6: [c.near(1)],
-                7: [b.side(0)],
+                0: [lambda: gather.pass_ring(0)],
+                1: [b.side(0)],
+                2: [b.side(1)],
+                3: [c.reduce.send_far],
+                4: [lambda: gather.pass_ring(1)],
+                5: [c.near(0)],
+                7: [c.near(1)],
             },
         )
-        logits_grad = lax.dot_general(
-            grad_logits[...],
-            second_held[me].astype(f32),
-            (((0,), (0,)), ((), ())),
-            precision=highest,
-            preferred_element_type=f32,
-        )
+        late.append(load(1, qkv, gu_held.at[:, 0:columns_grad]))
+        late[-1].start()
         small[...] = jnp.zeros_like(small)
         for s in range(n_shard):
             there = slice(128 * s, 128 * (s + 1))
             small[s, 1:2, :] = second_gain_grad[:, there]
             small[s, 2 : 3 + EXPERTS, :] = logits_grad[: EXPERTS + 1, there]
-        kept.wait()
-        gather.end()
-        late = [
-            load(0, grad_attended, g_held),
-            load(1, weights.at[pl.ds(0, half), :], gu_held.at[:, 0:half]),
-            load(2, weights.at[pl.ds(half, half), :], gu_held.at[:, half : 2 * half]),
-            load(3, qkv, gu_held.at[:, 2 * half : 2 * half + 3 * heads_width]),
-            load(
-                4,
-                mixed,
-                gu_held.at[:, 2 * half + 3 * heads_width : 2 * half + 4 * heads_width],
-            ),
-            load(5, first, second_held),
-        ]
-        for copy in late:
-            copy.start()
-        b.side(1)()
-        a.own()
+        for k, p in enumerate(places):
+            place = lax.rem(me + N_CTX - 1 - k, N_CTX)
+            ref = grad_held.at[place]
+            remote(ref, ref, grad_sends, grad_arrivals, k, {"ctx": p}).wait_recv()
         for copy in late:
             copy.wait()
-        columns_qkv = 2 * half
-        columns_mixed = columns_qkv + 3 * heads_width
-        columns_grad = columns_mixed + heads_width
-        w_out = [3 * heads_width, half + 3 * heads_width]
-
-        def grad_mixed(i, carry):
-            first_block = 2 * i
-            there = pl.ds(pl.multiple_of(i * tile, tile), tile)
-            left = g_held[pl.ds(first_block, 2)].reshape(tile, width)
-            made = jnp.dot(
-                left[:, :half],
-                gu_held[:, w_out[0] : w_out[0] + heads_width],
-                preferred_element_type=f32,
-            ) + jnp.dot(
-                left[:, half:],
-                gu_held[:, w_out[1] : w_out[1] + heads_width],
-                preferred_element_type=f32,
-            )
-            gu_held[there, columns_grad : columns_grad + heads_width] = made.astype(bf16)
-            return carry
-
-        lax.fori_loop(0, seq // tile, grad_mixed, 0)
-        d.exchange.run(
-            g_held,
-            lambda start, count: gu_held[:, columns_mixed + start : columns_mixed + start + count],
-            turned,
-            {
-                2: [d.reduce.send_far],
-                4: [d.near(0)],
-                6: [d.near(1)],
-            },
-        )
         events = {
-            0: [a.gather.pass_other],
             1: [b.reduce.cross],
-            2: [a.ring(0)],
-            3: [d.side(0), d.side(1)],
-            4: [b.own],
-            5: [a.ring(1), c.side(0)],
-            6: [c.side(1)],
-            7: [d.reduce.cross],
+            3: [c.side(0)],
+            4: [c.side(1)],
+            5: [b.own],
         }
 
         def attend(n, carry):
@@ -1296,10 +1536,10 @@
             def lanes_of(start):
                 return pl.ds(pl.multiple_of(start + HEAD * head, HEAD), HEAD)
 
-            query = gu_held[there, lanes_of(columns_qkv)]
-            key = gu_held[:, lanes_of(columns_qkv + heads_width)]
-            value = gu_held[:, lanes_of(columns_qkv + 2 * heads_width)]
-            grad = gu_held[there, lanes_of(columns_grad)]
+            query = gu_held[there, lanes_of(0)]
+            key = gu_held[:, lanes_of(heads_width)]
+            value = gu_held[:, lanes_of(2 * heads_width)]
+            grad = grad_held[pl.ds(2 * i, 2), :, lanes_of(0)].reshape(tile, HEAD)
             scores = contract_last(key, query) * scale
             scores = jnp.where(key_pos[...] <= query_pos[:, there], scores, -1e30)
             raised = jnp.exp(scores - jnp.max(scores, axis=0, keepdims=True))
@@ -1320,16 +1560,16 @@
             def turn_back(values, cosines, sines):
                 return (values * cosines - pltpu.roll(values, HEAD // 2, 1) * sines).astype(bf16)
 
-            act_held[there, lanes_of(0)] = turn_back(
+            gu_held[there, lanes_of(columns_grad)] = turn_back(
                 grad_query, cosines[there, :], sines[there, :]
             )
 
             @pl.when(i == seq // tile - 1)
             def _():
-                act_held[:, lanes_of(heads_width)] = turn_back(
+                gu_held[:, lanes_of(columns_grad + heads_width)] = turn_back(
                     key_sum[...] * scale, cosines[...], sines[...]
                 )
-                act_held[:, lanes_of(2 * heads_width)] = value_sum[...].astype(bf16)
+                gu_held[:, lanes_of(columns_grad + 2 * heads_width)] = value_sum[...].astype(bf16)
 
             for at, todo in events.items():
 
@@ -1348,12 +1588,13 @@
 
         def grad_first(k, carry):
             block = start_of(k)
-            left = act_held[pl.ds(pl.multiple_of(block * rows, tile), tile), 0 : 3 * heads_width]
+            left = gu_held[
+                pl.ds(pl.multiple_of(block * rows, tile), tile), columns_grad : 2 * columns_grad
+            ]
             for t in range(4):
-                low = 512 * (t % 2)
-                start = half * (t // 2)
-                made = contract_last(left, gu_held[low : low + 512, start : start + 3 * heads_width])
-                g_held[pl.ds(block, 2), :, 512 * t : 512 * (t + 1)] = made.astype(bf16).reshape(
+                low, start = 512 * (t % 2), columns_grad * (t // 2)
+                made = contract_last(left, w_held[low : low + 512, start : start + columns_grad])
+                parts[pl.ds(block, 2), :, 512 * t : 512 * (t + 1)] = made.astype(bf16).reshape(
                     2, rows, 512
                 )
             pl.when(k == 0)(reduce.send_far)
@@ -1362,24 +1603,39 @@
             return carry
 
         lax.fori_loop(0, 4, grad_first, 0)
-        b.gather.pass_other()
         e.exchange.run(
-            second_held,
-            lambda start, count: act_held[:, start : start + count],
+            streamed(first),
+            lambda start, count: gu_held[:, columns_grad + start : columns_grad + start + count],
             turned,
             {
-                1: [lambda: reduce.pass_side(0)],
-                2: [e.reduce.send_far, lambda: reduce.pass_side(1)],
-                3: [b.ring(0)],
-                4: [e.near(0), c.reduce.cross],
-                6: [e.near(1), c.own],
-                7: [b.ring(1), reduce.cross],
+                0: [c.reduce.cross],
+                2: [b.gather.pass_other],
+                3: [e.reduce.send_far],
+                5: [e.near(0), b.ring(0)],
+                7: [e.near(1), c.own],
             },
         )
-        e.side(0)()
-        e.side(1)()
-        d.own()
-        bias = jnp.sum(act_held[:, 0 : 3 * heads_width].astype(f32), axis=0, keepdims=True)
+        d.exchange.run(
+            lambda step: own[:, b.exchange.columns_at(step)],
+            lambda start, count: mixed[:, start : start + count],
+            turned,
+            {
+                0: [lambda: reduce.pass_side(0)],
+                1: [lambda: reduce.pass_side(1)],
+                3: [d.reduce.send_far],
+                4: [b.ring(1)],
+                5: [d.near(0)],
+                6: [e.side(0), e.side(1)],
+                7: [d.near(1), reduce.cross],
+            },
+        )
+        mixed_sum = staged.at[0, 0]
+        own_inputs = staged.at[1, 0]
+        inputs_load = load(1, inputs, own_inputs)
+        inputs_load.start()
+        bias = jnp.sum(
+            gu_held[:, columns_grad : 2 * columns_grad].astype(f32), axis=0, keepdims=True
+        )
         per = heads_width // 128
         for i in range(3):
             for j in range(per):
@@ -1387,18 +1643,16 @@
                 there = slice(heads_width * i + 128 * j, heads_width * i + 128 * (j + 1))
                 small[block // 3, pl.ds(3 + EXPERTS + lax.rem(block, 3), 1), :] = bias[:, there]
         e.reduce.cross()
-        c.gather.pass_other()
-        d.gather.pass_other()
         reduce.ready()
+        early[1].wait()
+        inputs_load.wait()
         gain_sum[...] = jnp.zeros_like(gain_sum)
 
         def norm(there):
-            normed, factor = normalize(inputs[there, :].astype(f32))
+            normed, factor = normalize(own_inputs[there, :].astype(f32))
             grad = reduce.total(there)
             gain_sum[...] += grad * normed
-            input_grad[there, :] = grad_residual[there, :] + norm_back(
-                grad, normed, factor, gain[...]
-            )
+            input_grad[there, :] += norm_back(grad, normed, factor, gain[...])
 
         by_rows(rows, norm)
         first_gain_grad = jnp.sum(gain_sum[...], axis=0, keepdims=True)
@@ -1410,9 +1664,13 @@
         ]
         for copy in to_owners:
             copy.start()
+        d.side(0)()
+        d.side(1)()
+        c.gather.pass_other()
         e.own()
         c.ring(0)()
-        d.ring(0)()
+        d.reduce.cross()
+        e.gather.pass_other()
         total = small[shard]
         for k, copy in enumerate(to_owners):
             copy.wait_recv()
@@ -1424,19 +1682,38 @@
         ]
         for copy in to_places:
             copy.start()
-        e.gather.pass_other()
         c.ring(1)()
-        d.ring(1)()
         e.ring(0)()
+        d.sum_into(mixed_sum)
+        to_columns = [
+            remote(
+                mixed_sum.at[:, columns_of(p)], mixed_in.at[k], mixed_sends, mixed_arrivals, k, {"ctx": p}
+            )
+            for k, p in enumerate(places)
+        ]
+        for copy in to_columns:
+            copy.start()
         e.ring(1)()
+        for k, copy in enumerate(to_columns):
+            copy.wait_recv()
+        part = mixed_sum[:, columns_of(me)].astype(f32)
+        for k in range(N_CTX - 1):
+            part = part + mixed_in[k].astype(f32)
+        d.owned[...] = part.astype(bf16)
+        d.pass_own()
         for k, copy in enumerate(to_places):
             copy.wait_recv()
             total = total + small_across[k]
         small_out[...] = total
-        for copy in to_owners + to_places:
+        d.gather.pass_other()
+        d.ring(0)()
+        d.ring(1)()
+        for copy in to_heads + to_owners + to_places + to_columns:
             copy.wait_send()
         reduce.end()
-        for share in shares:
+        kept.wait()
+        gather.end()
+        for share in (b, c, e, d):
             share.end()
 
     def shared(count):
@@ -1447,22 +1724,22 @@
         out_shape=(
             jax.ShapeDtypeStruct((rows, width), f32),
             jax.ShapeDtypeStruct((16, 128), f32),
-            jax.ShapeDtypeStruct((N_CTX, rows, width), bf16),
             shared(hidden),
             shared(hidden),
             shared(hidden),
             shared(heads_width),
             shared(3 * heads_width),
         ),
-        in_specs=[VMEM] + [ANY] * 8 + [VMEM] * 9,
-        out_specs=(VMEM, VMEM) + (ANY,) * 6,
+        in_specs=[VMEM] * 4 + [ANY] * 5 + [VMEM] * 4 + [ANY] * 2 + [VMEM] * 3,
+        out_specs=(VMEM, VMEM) + (ANY,) * 5,
         scratch_shapes=[
-            pltpu.VMEM(second.shape, bf16),
-            pltpu.VMEM(grad_out.shape, bf16),
+            pltpu.VMEM((N_CTX, rows, heads_width), bf16),
+            pltpu.VMEM((N_CTX, rows, width), bf16),
+            pltpu.VMEM((2, N_CTX, rows, 256), bf16),
             pltpu.VMEM(grad_gu.shape, bf16),
-            pltpu.VMEM(act.shape, bf16),
+            pltpu.VMEM((half, 2 * columns_grad), bf16),
             pltpu.VMEM((256, seq), bf16),
-            pltpu.VMEM((2, 2, 128, hidden), bf16),
+            pltpu.VMEM((3, 2, 128, width), bf16),
             pltpu.VMEM((seq, HEAD), f32),
             pltpu.VMEM((seq, HEAD), f32),
             pltpu.VMEM((16, width), f32),
@@ -1470,21 +1747,22 @@
             pltpu.VMEM((n_shard - 1, 16, 128), f32),
             pltpu.VMEM((16, 128), f32),
             pltpu.VMEM((N_CTX - 1, 16, 128), f32),
-            pltpu.SemaphoreType.DMA((6,)),
-            pltpu.SemaphoreType.DMA,
-            pltpu.SemaphoreType.DMA((n_shard - 1,)),
-            pltpu.SemaphoreType.DMA((n_shard - 1,)),
-            pltpu.SemaphoreType.DMA((N_CTX - 1,)),
-            pltpu.SemaphoreType.DMA((N_CTX - 1,)),
+            pltpu.VMEM((N_CTX - 1, 128, heads_width), bf16),
+            pltpu.SemaphoreType.DMA((4,)),
+            pltpu.SemaphoreType.DMA((2,)),
         ]
-        + [pltpu.SemaphoreType.DMA((Gather.SEMAPHORES,))] * 2
+        + [pltpu.SemaphoreType.DMA((N_CTX - 1,))] * 4
+        + [pltpu.SemaphoreType.DMA((n_shard - 1,))] * 2
+        + [pltpu.SemaphoreType.DMA((N_CTX - 1,))] * 2
         + Reduce.scratch(rows, width, 1)
-        + Share.scratch(hidden) * 3
-        + Share.scratch(heads_width)
+        + [pltpu.SemaphoreType.DMA((Both.SEMAPHORES,))] * 2
+        + [pltpu.SemaphoreType.DMA]
+        + Share.scratch(hidden) * 2
+        + Share.scratch(width, N_CTX)
         + Share.scratch(3 * heads_width),
         compiler_params=params(3, 64 << 20),
         name="backward",
-    )(own, second, grad_out, grad_gu, act, qkv, mixed, weights, first, cosines, sines, key_pos, query_pos, inputs, grad_residual, gain, second_gain_grad, grad_logits)
+    )(own, grad_mixed, mixed, out_own, second, grad_gu, qkv, weights, first, cosines, sines, key_pos, query_pos, inputs, grad_residual, gain, second_gain_grad, logits_grad)
 
 
 def local(
@@ -1509,7 +1787,6 @@
     seq_len = rows_dev * n_ctx
     n_blocks = block_order.shape[0]
     block = seq_len // n_blocks
-    hidden_blocks = -(-HIDDEN_BLOCKS // n_ctx)
     place = lax.axis_index("ctx")
 
     every = jnp.arange(seq_len, dtype=jnp.int32)
@@ -1540,7 +1817,9 @@
         attn_weights,
         small_all,
         first_all,
-        ffn_weights,
+        w_gate,
+        w_up,
+        w_down,
         qkv,
         mixed,
         assigned,
@@ -1558,35 +1837,39 @@
         pos[None],
     )
 
-    block_ids = hidden_blocks * place + jnp.arange(hidden_blocks, dtype=jnp.int32)
-    branch_of = jnp.where(
-        block_ids < SHARED_BLOCKS, EXPERTS, (block_ids - SHARED_BLOCKS) // EXPERT_BLOCKS
-    )
-    member = (
-        (branch_of[None, :] == jnp.arange(LANE, dtype=jnp.int32)[:, None])
-        & (block_ids < HIDDEN_BLOCKS)[None, :]
-    ).astype(f32)
-    member = jnp.repeat(member, LANE, axis=1)
-    grad_residual, grad_low, output, grad_second_gain, grad_both, act_low, grad_gu = feed_forward(
+    (
+        grad_residual,
+        grad_low,
+        grad_mixed,
+        output,
+        grad_second_gain,
+        grad_both,
+        _,
+        grad_gu,
+        _,
+        out_own,
+    ) = feed_forward(
         second_all,
         g_all,
         assigned,
-        ffn_weights.reshape(D, -1),
+        w_gate.reshape(D, -1),
+        w_up.reshape(D, -1),
+        w_down.reshape(D, -1),
+        out_weight,
         small_all,
-        member,
         residual,
         own_grad,
         own_valid,
     )
     first_gain = small_all[:, 0, :].reshape(1, D).astype(f32)
-    input_grad, own_small, _, out_share, gate_share, up_share, mixed_share, qkv_share = backward(
+    input_grad, own_small, out_share, gate_share, up_share, mixed_share, qkv_share = backward(
         grad_low,
+        grad_mixed,
+        mixed,
+        out_own,
         second_all,
-        g_all,
         grad_gu,
-        act_low,
         qkv,
-        mixed,
         attn_weights.reshape(D, -1),
         first_all,
         cosines,

time: 576 us -> 538 us (0.934)
  Pallas kernels: 551 us -> 512 us
    pallas_call x1, Pallas kernels: 224 us -> 194 us  [backward(): pl.pallas_call(kernel, out_shape=(jax.ShapeDtypeStruct((rows, width), f32...]
    pallas_call x1, Pallas kernels: 186 us -> 170 us  [front(): pl.pallas_call(kernel, out_shape=(shape(rows, width, kind=f32), shape(N_C...]
    pallas_call x1, Pallas kernels: 125 us -> 131 us  [feed_forward(): pl.pallas_call(kernel, out_shape=(jax.ShapeDtypeStruct((rows, width), f32...]
where the time goes in v4:
time: 538 us; the launch traced here: 535 us
  Pallas kernels  512 us (95%)
  other arithmetic  11.5 us (2%)
  local copies, waits for them, and re-layouts  10.4 us (2%)
    pallas_call x1, Pallas kernels, backward(): pl.pallas_call(kernel, out_shape=(jax.ShapeDtypeStruct((rows, width), f32...  194 us
    pallas_call x1, Pallas kernels, front(): pl.pallas_call(kernel, out_shape=(shape(rows, width, kind=f32), shape(N_C...  170 us
    pallas_call x1, Pallas kernels, feed_forward(): pl.pallas_call(kernel, out_shape=(jax.ShapeDtypeStruct((rows, width), f32...  131 us
    pallas_call x1, Pallas kernels, assemble(): pl.pallas_call(kernel, out_shape=(jax.ShapeDtypeStruct((rows, FOUT), f32)...  16.1 us

profile of v4, /device:TPU:2, one launch (start us, length us, event | category | flops | bytes accessed | tf_op | source)
XLA Modules:
  0.0 535.0 jit_solution(8598374399000655040)
XLA Ops:
  1.3 2.6 concatenate.13.small
  3.9 0.7 select_reduce_fusion
  4.7 0.1 dynamic-slice_bitcast_fusion
  4.7 0.1 broadcast_compare_fusion
  4.8 0.6 fusion.11.query_pos
  5.4 0.8 convert_reduce_fusion
  6.2 0.7 copy.29.own_valid
  7.0 1.9 bitcast_select_fusion.own_grad
  8.9 1.9 pad_maximum_fusion.block
  10.8 0.2 copy.28
  11.0 0.9 compare_select_fusion.key_pos
  11.9 1.9 fusion.4
  13.8 1.3 pad_maximum_fusion.1
  15.1 169.9 %front.1 = (f32[128,2048]{1,0:T(8,128)}, bf16[8,128,2048]{2,1,0:T(8,128)(2,1)}, bf16[8,128,2048]{2,1,0:T(8,128)(2,1)}, bf16[8,2,128,1024]{3,2,1,0:T(8,128)(2,1)}...) custom-call(bf16[128,2176]{1,0:T(8,128)(2,1)} %pad_maximum_fusion.bl, ...), custom_call_target="tpu_custom_call" | custom-call | tf_op jit(solution)/shard_map/front/pallas_call | solution.py:852
  185.0 131.2 %feed_forward.1 = (f32[128,2048]{1,0:T(8,128)}, bf16[128,2048]{1,0:T(8,128)(2,1)}, bf16[128,2048]{1,0:T(8,128)(2,1)}, bf16[128,2048]{1,0:T(8,128)(2,1)}, f32[1,2...) custom-call(bf16[8,128,2048]{2,1,0:T(8,128)(2,1)} %get-tuple-element, ...), custom_call_target="tpu_custom_call" | custom-call | tf_op jit(solution)/shard_map/feed_forward/pallas_call | solution.py:1292
  316.2 1.4 bitcast_convert_fusion.gain
  317.6 194.5 %backward.1 = (f32[128,2048]{1,0:T(8,128)}, f32[16,128]{1,0:T(8,128)}, bf16[8,128,1792]{2,1,0:T(8,128)(2,1)}, bf16[8,128,1792]{2,1,0:T(8,128)(2,1)}, bf16[8,128,...) custom-call(bf16[128,2048]{1,0:T(8,128)(2,1)} %get-tuple-element.50.own, ...), custom_call_target="tpu_custom_call" | custom-call | tf_op jit(solution)/shard_map/backward/pallas_call | solution.py:1722
  512.1 1.2 slice_bitcast_fusion.2
  513.3 1.2 slice.24
  514.5 1.3 slice_bitcast_fusion.1
  515.8 1.3 slice_bitcast_fusion
  517.0 0.0 copy-start.1
  517.0 0.0 copy-start
  517.0 16.1 %assemble.1 = (f32[128,14080]{1,0:T(8,128)}, f32[128,28160]{1,0:T(8,128)}, f32[128,2048]{1,0:T(8,128)}, f32[128,6144]{1,0:T(8,128)}) custom-call(bf16[8,128,1792]{2,1,0:T(8,128)(2,1)} %get-tuple-element.63.refs_0_, bf16[8,128,1792]{2,1,0:T(8,128)(2,1)} %get-tuple-element.64.refs_1_, bf16[8,128,1792]{2,1,0:T(8,128)(2,1)} %get-tuple-element.65.refs_2_, ...), custom_call_target="tpu_custom_call" | custom-call | tf_op jit(solution)/shard_map/assemble/pallas_call | solution.py:568
  533.2 0.0 copy-done.1
  533.2 0.8 copy.33
  534.0 0.0 copy-done
  534.0 1.0 copy.34
  (5 shorter events, 0.0 us)
Async XLA Ops:
  517.0 16.1 %copy-start.1 = (bf16[128,2048]{1,0:T(8,128)(2,1)S(1)}, bf16[128,2048]{1,0:T(8,128)(2,1)}, u32[]{:S(2)}) copy-start(bf16[128,2048]{1,0:T(8,128)(2,1)} %get-tuple-element.49) | copy-start | bytes 1572868
  517.0 16.9 %copy-start = (f32[128,2048]{1,0:T(8,128)S(1)}, f32[128,2048]{1,0:T(8,128)}, u32[]{:S(2)}) copy-start(f32[128,2048]{1,0:T(8,128)} %get-tuple-element.61) | copy-start | bytes 3145732

commit v5 on v4

--- a/solution.py
+++ b/solution.py
@@ -40,13 +40,10 @@
 
 def rope_tables(positions):
     half = HEAD // 2
-    freqs = rope_base ** (-jnp.arange(half, dtype=jnp.float32) * 2.0 / HEAD)
+    lane = jnp.arange(HEAD, dtype=jnp.int32)
+    freqs = rope_base ** (-(lane % half).astype(jnp.float32) * 2.0 / HEAD)
     phase = positions.astype(jnp.float32)[:, None] * freqs[None, :]
-    cosines, sines = jnp.cos(phase), jnp.sin(phase)
-    return (
-        jnp.concatenate([cosines, cosines], axis=1),
-        jnp.concatenate([-sines, sines], axis=1),
-    )
+    return jnp.cos(phase), jnp.where(lane < half, -1.0, 1.0) * jnp.sin(phase)
 
 
 def normalize(values):
@@ -519,7 +516,7 @@
         jobs.append(
             (4, place, 3 * width, 3, [(width * i, D * i + width * place, width) for i in range(3)])
         )
-    depth = 4
+    depth = 6
     most = max(len(job[4]) for job in jobs)
 
     def kernel(*refs):
@@ -586,7 +583,7 @@
     )(out_share, gate_share, up_share, mixed_share, qkv_share)
 
 
-def front(block, own_grad, qkv_weight, out_weight, ffn_in, ffn_out, small, cosines, sines, key_pos, query_pos):
+def front(block, grad_out, own_valid, qkv_weight, out_weight, ffn_in, ffn_out, small, cosines, sines, key_pos, query_pos):
     rows, width = qkv_weight.shape[0], out_weight.shape[1]
     n_shard = width // rows
     heads_width = width // N_CTX
@@ -599,18 +596,18 @@
     f32, bf16 = jnp.float32, jnp.bfloat16
 
     def kernel(
-        block, own_grad, qkv_weight, out_weight, ffn_in, ffn_out, small, cosines, sines, key_pos,
-        query_pos,
-        residual, second_all, g_all, weights_out, small_all, first_out, w_gate, w_up, w_down, qkv,
-        mixed_own, assigned,
-        x_all, weights, first, staged, picked, params_all, mixed, own, parts, loads, picks, local,
+        block, grad_out, own_valid, qkv_weight, out_weight, ffn_in, ffn_out, small, cosines, sines,
+        key_pos, query_pos,
+        residual, second_all, g_all, weights_out, out_out, small_all, first_out, w_gate, w_up, w_down,
+        qkv, mixed_own, assigned,
+        own_grad, x_all, weights, out_all, first, staged, picked, params_all, mixed, own, loads, picks, local,
         mixed_sends, mixed_arrivals, *scratch,
     ):
         gather = Gather(block, x_all, *scratch[0:2])
         gather_qkv = Gather(staged, weights, *scratch[2:4], axis="shard")
         spread_small = Spread(small, small_all, *scratch[4:6])
-        gather_grad = Both(own_grad, g_all, *scratch[6:8], AFTER)
-        gather_second = Both(own, second_all, *scratch[8:10], AFTER)
+        gather_grad = Both(own_grad, g_all, *scratch[6:8], 768)
+        gather_second = Both(own, second_all, *scratch[8:10], 768)
         w_outs = (w_gate, w_up, w_down)
         ffn = [
             Gather(
@@ -618,7 +615,7 @@
             )
             for k, out in enumerate(w_outs)
         ]
-        reduce = Reduce(parts, parts, *scratch[16:21])
+        gather_out = Gather(out_weight, out_all, *scratch[16:18], axis="shard")
         me = gather.me
         loaded = [
             pltpu.make_async_copy(
@@ -627,7 +624,7 @@
                 loads.at[i],
             )
             for i, (source, start) in enumerate(
-                ((qkv_weight, 0), (qkv_weight, width), (qkv_weight, 2 * width), (out_weight, 0))
+                ((qkv_weight, 0), (qkv_weight, width), (qkv_weight, 2 * width))
             )
         ]
         for copy in loaded:
@@ -642,9 +639,10 @@
         for copy in loaded:
             copy.wait()
         gather_qkv.begin()
+        gather_out.begin()
+        own_grad[...] = (grad_out[...].astype(f32) * own_valid[...]).astype(bf16)
         for copy in picking:
             copy.wait()
-        ffn[0].begin()
         kept = [
             pltpu.make_async_copy(source, target, local.at[k])
             for k, (source, target) in enumerate(
@@ -652,11 +650,12 @@
                     (block, x_all.at[me]),
                     (staged, weights.at[spread_small.chip, spread_small.core]),
                     (small, small_all.at[spread_small.me]),
+                    (out_weight, gather_out.at(gather_out.me)),
                     (own_grad, g_all.at[me]),
                 )
             )
         ] + [
-            pltpu.make_async_copy(gather_w.block, gather_w.at(gather_w.me), local.at[4 + k])
+            pltpu.make_async_copy(gather_w.block, gather_w.at(gather_w.me), local.at[5 + k])
             for k, gather_w in enumerate(ffn)
         ]
         for copy in kept:
@@ -667,13 +666,14 @@
         spread_small.hand_on()
         gather.pass_ring(0)
         gather_qkv.pass_ring(1)
-        ffn[0].pass_other()
+        gather_out.pass_other()
         gather.pass_ring(1)
+        gather_out.pass_ring(0)
         spread_small.end()
         gather_qkv.end()
         gather.end()
         gather_grad.begin()
-        ffn[1].begin()
+        ffn[0].begin()
         for copy in kept:
             copy.wait()
         weights_kept = pltpu.make_async_copy(weights, weights_out, local.at[0])
@@ -725,16 +725,15 @@
 
             @pl.when(n == 0)
             def _():
-                ffn[0].pass_ring(0)
+                gather_out.pass_ring(1)
 
             @pl.when(n == 1)
             def _():
-                ffn[0].pass_ring(1)
+                ffn[0].pass_other()
 
             @pl.when(n == 2)
             def _():
                 gather_grad.pass_other()
-                ffn[1].pass_other()
 
             return carry
 
@@ -743,9 +742,11 @@
         first_kept.start()
         events = {
             0: [lambda: gather_grad.pass_ring(0)],
-            2: [lambda: ffn[1].pass_ring(0)],
+            1: [lambda: ffn[0].pass_ring(0)],
+            2: [lambda: ffn[0].pass_ring(1), ffn[1].begin],
             3: [lambda: gather_grad.pass_ring(1)],
-            5: [lambda: ffn[1].pass_ring(1)],
+            4: [gather_out.end],
+            6: [ffn[1].pass_other],
         }
 
         def attend(n, carry):
@@ -791,33 +792,21 @@
             for k, p in enumerate(places)
         ]
 
-        def attended(k, carry):
-            ahead = 2 - k + 3 * (k // 2) - 2 * (k // 3)
-            at = lax.rem(me // 2 + ahead, N_CTX // 2) * 2
-            left = mixed[pl.ds(pl.multiple_of(at * rows, tile), tile), :]
-            for t in range(width // 512):
-                right = weights[2 * t : 2 * (t + 1), :, :, 3 * heads_width :]
-                made = contract_last(left, right.reshape(512, heads_width)).astype(bf16)
-                parts[pl.ds(at, 2), :, 512 * t : 512 * (t + 1)] = made.reshape(2, rows, 512)
-            pl.when(k == 0)(reduce.send_far)
-            pl.when(k == 1)(lambda: reduce.send_near(0))
-            pl.when(k == 2)(lambda: reduce.send_near(1))
-            return carry
-
-        lax.fori_loop(0, 4, attended, 0)
         for copy in to_rows:
             copy.start()
-        ffn[2].begin()
         mixed_own[:, columns_of(me)] = mixed[rows_of(me), :]
-        reduce.pass_side(0)
-        reduce.pass_side(1)
-        reduce.cross()
-        ffn[2].pass_other()
-        ffn[0].end()
-        reduce.ready()
+        out_kept = pltpu.make_async_copy(out_all, out_out, local.at[3])
+        out_kept.start()
+        ffn[1].pass_ring(0)
+        for k, p in enumerate(places):
+            ref = mixed_own.at[:, columns_of(lax.rem(me + N_CTX - 1 - k, N_CTX))]
+            remote(ref, ref, mixed_sends, mixed_arrivals, k, {"ctx": p}).wait_recv()
+        for t in range(width // 512):
+            right = out_all[2 * t : 2 * (t + 1)].reshape(512, width)
+            residual[:, 512 * t : 512 * (t + 1)] = contract_last(mixed_own[...], right)
 
         def norm_second(there):
-            total = x_all[me, there, 0:width].astype(f32) + reduce.total(there)
+            total = x_all[me, there, 0:width].astype(f32) + residual[there, :]
             residual[there, :] = total
             normed, _ = normalize(total)
             own[there, :] = (normed * gains[1]).astype(bf16)
@@ -826,20 +815,20 @@
         gather_second.begin()
         second_kept = pltpu.make_async_copy(own, second_all.at[me], local.at[2])
         second_kept.start()
+        ffn[2].begin()
         gather_second.pass_other()
+        ffn[1].pass_ring(1)
+        ffn[0].end()
+        gather_second.pass_ring(0)
+        ffn[2].pass_other()
+        gather_second.pass_ring(1)
         ffn[2].pass_ring(0)
-        gather_second.pass_ring(0)
+        ffn[1].end()
         ffn[2].pass_ring(1)
-        ffn[1].end()
-        gather_second.pass_ring(1)
         gather_grad.end()
-        for k, p in enumerate(places):
-            ref = mixed_own.at[:, columns_of(lax.rem(me + N_CTX - 1 - k, N_CTX))]
-            remote(ref, ref, mixed_sends, mixed_arrivals, k, {"ctx": p}).wait_recv()
         for copy in to_rows:
             copy.wait_send()
-        reduce.end()
-        for copy in (weights_kept, first_kept, second_kept):
+        for copy in (weights_kept, first_kept, second_kept, out_kept):
             copy.wait()
         gather_second.end()
         ffn[2].end()
@@ -855,7 +844,8 @@
             shape(rows, width, kind=f32),
             shape(N_CTX, rows, width),
             shape(N_CTX, rows, width),
-            shape(CHIPS, 2, rows, 4 * heads_width),
+            shape(CHIPS, 2, rows, 3 * heads_width),
+            shape(CHIPS, 2, rows, width),
             shape(n_shard, 16, 128),
             shape(N_CTX, rows, width),
             shape(CHIPS, 2, rows, hidden),
@@ -865,21 +855,22 @@
             shape(rows, width),
             shape(seq, extra),
         ),
-        in_specs=[ANY, VMEM] + [ANY] * 5 + [VMEM] * 4,
-        out_specs=(VMEM, ANY, ANY, ANY, VMEM, ANY, ANY, ANY, ANY, VMEM, VMEM, VMEM),
+        in_specs=[ANY, VMEM, VMEM] + [ANY] * 5 + [VMEM] * 4,
+        out_specs=(VMEM, ANY, ANY, ANY, ANY, VMEM, ANY, ANY, ANY, ANY, VMEM, VMEM, VMEM),
         scratch_shapes=[
+            pltpu.VMEM((rows, width), bf16),
             pltpu.VMEM((N_CTX,) + block.shape, bf16),
-            pltpu.VMEM((CHIPS, 2, rows, 4 * heads_width), bf16),
+            pltpu.VMEM((CHIPS, 2, rows, 3 * heads_width), bf16),
+            pltpu.VMEM((CHIPS, 2, rows, width), bf16),
             pltpu.VMEM((N_CTX, rows, width), bf16),
-            pltpu.VMEM((rows, 4 * heads_width), bf16),
+            pltpu.VMEM((rows, 3 * heads_width), bf16),
             pltpu.VMEM((rows, 3 * hidden), bf16),
             pltpu.VMEM((n_shard, 16, 128), f32),
             pltpu.VMEM((seq, heads_width), bf16),
             pltpu.VMEM((rows, width), bf16),
-            pltpu.VMEM((N_CTX, rows, width), bf16),
-            pltpu.SemaphoreType.DMA((4,)),
+            pltpu.SemaphoreType.DMA((3,)),
             pltpu.SemaphoreType.DMA((3 * hidden // LANE,)),
-            pltpu.SemaphoreType.DMA((7,)),
+            pltpu.SemaphoreType.DMA((8,)),
             pltpu.SemaphoreType.DMA((N_CTX - 1,)),
             pltpu.SemaphoreType.DMA((N_CTX - 1,)),
         ]
@@ -887,11 +878,10 @@
         + paired
         + [pltpu.SemaphoreType.DMA((Spread.SEMAPHORES,))] * 2
         + pair * 2
-        + paired * 3
-        + Reduce.scratch(rows, width, 1),
+        + paired * 4,
         compiler_params=params(0, 56 << 20),
         name="front",
-    )(block, own_grad, qkv_weight, out_weight, ffn_in, ffn_out, small, cosines, sines, key_pos, query_pos)
+    )(block, grad_out, own_valid, qkv_weight, out_weight, ffn_in, ffn_out, small, cosines, sines, key_pos, query_pos)
 
 
 class Exchange:
@@ -983,7 +973,7 @@
             self._pair(step).wait_send()
 
 
-def feed_forward(second, grad_out, assigned, w_gate, w_up, w_down, out_weight, small, residual, own_grad, own_valid):
+def feed_forward(second, grad_out, assigned, w_gate, w_up, w_down, out_weights, small, residual, own_grad, own_valid):
     _, rows, width = second.shape
     seq = rows * N_CTX
     hidden = w_gate.shape[1]
@@ -994,22 +984,21 @@
     f32, bf16 = jnp.float32, jnp.bfloat16
 
     def kernel(
-        second, grad_out, assigned, w_gate, w_up, w_down, out_weight, small, residual, own_grad, own_valid,
+        second, grad_out, assigned, w_gate, w_up, w_down, out_weights, small, residual, own_grad, own_valid,
         grad_residual, grad_low, grad_mixed, output, grad_gain, grad_logits, act_out, grad_gu_out,
-        out_weights, out_owned,
+        out_owned,
         second_held, grad_held, in_held, down_held, act, grad_gu, weights, dots, dots_in, gain_sum,
-        logit_low, out_sems,
+        logit_low,
         back_parts, ffn_parts, dot_sends, dot_arrivals, loads, weight_loads, stores, *scratch,
     ):
         back = Reduce(back_parts, back_parts, *scratch[:5])
         ahead = Reduce(ffn_parts, ffn_parts, *scratch[5:10])
-        gather_out = Gather(out_weight, out_weights, *scratch[10:12], axis="shard")
         share, act_held = down_held.at[pl.ds(0, CHIPS)], down_held.at[pl.ds(CHIPS, N_CTX)]
         staged = in_held.at[pl.ds(0, 768), pl.ds(0, hidden)]
         turned = in_held.at[pl.ds(768, 256), pl.ds(0, seq)]
-        exchange = Exchange(share, staged, *scratch[12:14])
-        sums = Reduce(share, share, *scratch[14:19], axis="shard")
-        free = scratch[19]
+        exchange = Exchange(share, staged, *scratch[10:12])
+        sums = Reduce(share, share, *scratch[12:17], axis="shard")
+        free = scratch[17]
         own, other = back.places
         me = own[0]
         peers = [lax.rem(me + k, N_CTX) for k in range(1, N_CTX)]
@@ -1037,13 +1026,8 @@
             return carry
 
         lax.fori_loop(0, hidden // tile, start_weights, 0)
-        shard_peers = [gather_out.peer(p) for p in (gather_out.up, gather_out.down, gather_out.other)]
-        greet([{"ctx": p} for p in peers] + shard_peers + [gather_out.mate])
-        gather_out.begin()
-        out_kept = pltpu.make_async_copy(
-            out_weight, out_weights.at[gather_out.me, gather_out.core], loads.at[2]
-        )
-        out_kept.start()
+        plane_peers = [sums.peer(p) for p in (sums.up, sums.down, sums.other)]
+        greet([{"ctx": p} for p in peers] + plane_peers + [exchange.mate])
         logit_low[...] = jnp.zeros_like(logit_low)
         gains = []
         for s in range(n_shard):
@@ -1156,16 +1140,16 @@
                 copy.start()
 
             def out_tile(t, carry):
-                there = pl.ds(pl.multiple_of(512 * t, 512), 512)
+                there = pl.ds(pl.multiple_of(1024 * t, 1024), 1024)
                 for parts, left, right in (
                     (back_parts, grad_gu, lambda: in_held[there, :]),
-                    (ffn_parts, act, lambda: down_held[pl.ds(4 * t, 4)].reshape(512, hidden)),
+                    (ffn_parts, act, lambda: down_held[pl.ds(8 * t, 8)].reshape(1024, hidden)),
                 ):
                     made = contract_last(left[slot], right())
-                    parts[pl.ds(first, 2), :, there] = made.astype(bf16).reshape(2, rows, 512)
+                    parts[pl.ds(first, 2), :, there] = made.astype(bf16).reshape(2, rows, 1024)
                 return carry
 
-            lax.fori_loop(0, width // 512, out_tile, 0)
+            lax.fori_loop(0, width // 1024, out_tile, 0)
 
             def far():
                 back.send_far()
@@ -1184,9 +1168,6 @@
             pl.when(b == 0)(far)
             pl.when(b == 1)(lambda: near(0))
             pl.when(b == 2)(lambda: near(1))
-            pl.when(b == 0)(gather_out.pass_other)
-            pl.when(b == 1)(lambda: gather_out.pass_ring(0))
-            pl.when(b == 2)(lambda: gather_out.pass_ring(1))
             return carry
 
         lax.fori_loop(0, 4, block, 0)
@@ -1195,9 +1176,7 @@
             copy.wait()
         act_load = pltpu.make_async_copy(act_out, act_held, loads.at[0])
         act_load.start()
-        pl.semaphore_signal(free, inc=1, device_id=gather_out.mate, device_id_type=MESH)
-        out_kept.wait()
-        gather_out.end()
+        pl.semaphore_signal(free, inc=1, device_id=exchange.mate, device_id_type=MESH)
         pl.semaphore_wait(free, 1)
         act_load.wait()
         exchange.run(
@@ -1211,14 +1190,8 @@
                 7: [lambda: sums.send_near(1)],
             },
         )
-        out_loads = [
-            pltpu.make_async_copy(
-                out_weights.at[n // 2, n % 2], in_held.at[128 * n : 128 * (n + 1), 0:width], out_sems.at[n]
-            )
-            for n in range(n_shard)
-        ]
-        for copy in out_loads:
-            copy.start()
+        out_load = pltpu.make_async_copy(out_weights, in_held.at[:, 0:width], loads.at[1])
+        out_load.start()
         ahead.cross()
         sums.pass_side(0)
         sums.pass_side(1)
@@ -1256,14 +1229,14 @@
             normed, factor = normalize(residual[there, :])
             grad = back.total(there) + grad_residual[there, :]
             gain_sum[...] += grad * normed
-            grad = own_grad[there, :].astype(f32) + norm_back(grad, normed, factor, gain)
+            grad = norm_back(grad, normed, factor, gain)
+            grad = grad + own_grad[there, :].astype(f32) * own_valid[there, :]
             grad_residual[there, :] = grad
             grad_low[there, :] = grad.astype(bf16)
 
         by_rows(rows, norm)
         grad_gain[...] = jnp.sum(gain_sum[...], axis=0, keepdims=True)
-        for copy in out_loads:
-            copy.wait()
+        out_load.wait()
         for t in range(width // 512):
             there = slice(512 * t, 512 * (t + 1))
             grad_mixed[:, there] = jnp.dot(
@@ -1300,11 +1273,10 @@
             jax.ShapeDtypeStruct((8, width), f32),
             jax.ShapeDtypeStruct((N_CTX, rows, hidden), bf16),
             jax.ShapeDtypeStruct((seq, 2 * hidden), bf16),
-            jax.ShapeDtypeStruct((CHIPS, 2, rows, width), bf16),
             jax.ShapeDtypeStruct((128, hidden), bf16),
         ),
         in_specs=[ANY, ANY, VMEM] + [ANY] * 4 + [VMEM] * 4,
-        out_specs=(VMEM,) * 6 + (ANY,) * 3 + (VMEM,),
+        out_specs=(VMEM,) * 6 + (ANY,) * 2 + (VMEM,),
         scratch_shapes=[
             pltpu.VMEM(second.shape, bf16),
             pltpu.VMEM(grad_out.shape, bf16),
@@ -1317,7 +1289,6 @@
             pltpu.VMEM((N_CTX - 1, rows, lanes), f32),
             pltpu.VMEM((16, width), f32),
             pltpu.VMEM((lanes, width), bf16),
-            pltpu.SemaphoreType.DMA((n_shard,)),
             pltpu.VMEM(second.shape, bf16),
             pltpu.VMEM(second.shape, bf16),
             pltpu.SemaphoreType.DMA((N_CTX - 1,)),
@@ -1327,13 +1298,12 @@
             pltpu.SemaphoreType.DMA((1, 3)),
         ]
         + Reduce.scratch(rows, width, 1) * 2
-        + [pltpu.SemaphoreType.DMA((Gather.PAIRED,))] * 2
         + Exchange.scratch()
         + Reduce.scratch(128, hidden, 1)
         + [pltpu.SemaphoreType.REGULAR],
         compiler_params=params(2, 64 << 20),
         name="feed_forward",
-    )(second, grad_out, assigned, w_gate, w_up, w_down.reshape(width // 128, 128, hidden), out_weight, small, residual, own_grad, own_valid)
+    )(second, grad_out, assigned, w_gate, w_up, w_down.reshape(width // 128, 128, hidden), out_weights, small, residual, own_grad, own_valid)
 
 
 class Share:
@@ -1796,7 +1766,6 @@
     valid_rows = valid.astype(f32)[:, None]
 
     own_valid = lax.dynamic_slice_in_dim(valid_rows, place * rows_dev, rows_dev)
-    own_grad = jnp.where(own_valid > 0, cotangent[0], 0).astype(bf16)
     picks = routes[0][:, :, None] == jnp.arange(LANE, dtype=jnp.int32)[None, None, :]
     own_assigned = jnp.sum(picks.astype(f32), axis=1).astype(bf16)
     small = jnp.concatenate(
@@ -1815,6 +1784,7 @@
         second_all,
         g_all,
         attn_weights,
+        out_weights,
         small_all,
         first_all,
         w_gate,
@@ -1825,7 +1795,8 @@
         assigned,
     ) = front(
         jnp.concatenate([tokens[0], own_assigned], axis=1),
-        own_grad,
+        cotangent[0],
+        own_valid,
         qkv_weight,
         out_weight,
         ffn_in,
@@ -1846,7 +1817,6 @@
         grad_both,
         _,
         grad_gu,
-        _,
         out_own,
     ) = feed_forward(
         second_all,
@@ -1855,10 +1825,10 @@
         w_gate.reshape(D, -1),
         w_up.reshape(D, -1),
         w_down.reshape(D, -1),
-        out_weight,
+        out_weights.reshape(D, D),
         small_all,
         residual,
-        own_grad,
+        cotangent[0],
         own_valid,
     )
     first_gain = small_all[:, 0, :].reshape(1, D).astype(f32)

time: 538 us -> 520 us (0.967)
  Pallas kernels: 512 us -> 498 us
    pallas_call x1, Pallas kernels: 170 us -> 157 us  [front(): pl.pallas_call(kernel, out_shape=(shape(rows, width, kind=f32), shape(N_C...]
where the time goes in v5:
time: 520 us; the launch traced here: 519 us
  Pallas kernels  498 us (96%)
  local copies, waits for them, and re-layouts  10.4 us (2%)
  other arithmetic  9.35 us (2%)
    pallas_call x1, Pallas kernels, backward(): pl.pallas_call(kernel, out_shape=(jax.ShapeDtypeStruct((rows, width), f32...  196 us
    pallas_call x1, Pallas kernels, front(): pl.pallas_call(kernel, out_shape=(shape(rows, width, kind=f32), shape(N_C...  157 us
    pallas_call x1, Pallas kernels, feed_forward(): pl.pallas_call(kernel, out_shape=(jax.ShapeDtypeStruct((rows, width), f32...  130 us
    pallas_call x1, Pallas kernels, assemble(): pl.pallas_call(kernel, out_shape=(jax.ShapeDtypeStruct((rows, FOUT), f32)...  14.3 us

profile of v5, /device:TPU:2, one launch (start us, length us, event | category | flops | bytes accessed | tf_op | source)
XLA Modules:
  0.0 518.7 jit_solution(16520153352197473072)
XLA Ops:
  1.3 2.6 concatenate.7.small
  3.9 0.7 select_reduce_fusion
  4.7 0.1 dynamic-slice_bitcast_fusion
  4.7 0.6 fusion.11.query_pos
  5.3 0.8 convert_reduce_fusion
  6.2 0.7 copy.31.own_valid
  6.9 1.9 pad_maximum_fusion.block
  8.8 0.2 copy.30
  9.0 0.9 compare_select_fusion.key_pos
  9.9 3.0 fusion
  13.0 157.2 %front.1 = (f32[128,2048]{1,0:T(8,128)}, bf16[8,128,2048]{2,1,0:T(8,128)(2,1)}, bf16[8,128,2048]{2,1,0:T(8,128)(2,1)}, bf16[8,2,128,768]{3,2,1,0:T(8,128)(2,1)},...) custom-call(bf16[128,2176]{1,0:T(8,128)(2,1)} %pad_maximum_fusion.bl, ...), custom_call_target="tpu_custom_call" | custom-call | tf_op jit(solution)/shard_map/front/pallas_call | solution.py:841
  170.2 129.8 %feed_forward.1 = (f32[128,2048]{1,0:T(8,128)}, bf16[128,2048]{1,0:T(8,128)(2,1)}, bf16[128,2048]{1,0:T(8,128)(2,1)}, bf16[128,2048]{1,0:T(8,128)(2,1)}, f32[1,2...) custom-call(bf16[8,128,2048]{2,1,0:T(8,128)(2,1)} %get-tuple-element, ...), custom_call_target="tpu_custom_call" | custom-call | tf_op jit(solution)/shard_map/feed_forward/pallas_call | solution.py:1265
  300.0 1.4 bitcast_convert_fusion.gain
  301.3 196.4 %backward.1 = (f32[128,2048]{1,0:T(8,128)}, f32[16,128]{1,0:T(8,128)}, bf16[8,128,1792]{2,1,0:T(8,128)(2,1)}, bf16[8,128,1792]{2,1,0:T(8,128)(2,1)}, bf16[8,128,...) custom-call(bf16[128,2048]{1,0:T(8,128)(2,1)} %get-tuple-element.52.own, ...), custom_call_target="tpu_custom_call" | custom-call | tf_op jit(solution)/shard_map/backward/pallas_call | solution.py:1692
  497.7 1.2 slice_bitcast_fusion.2
  498.9 1.2 slice.24
  500.2 1.3 slice_bitcast_fusion.1
  501.4 1.3 slice_bitcast_fusion
  502.7 0.0 copy-start.1
  502.7 0.0 copy-start
  502.7 14.3 %assemble.1 = (f32[128,14080]{1,0:T(8,128)}, f32[128,28160]{1,0:T(8,128)}, f32[128,2048]{1,0:T(8,128)}, f32[128,6144]{1,0:T(8,128)}) custom-call(bf16[8,128,1792]{2,1,0:T(8,128)(2,1)} %get-tuple-element.65.refs_0_, bf16[8,128,1792]{2,1,0:T(8,128)(2,1)} %get-tuple-element.66.refs_1_, bf16[8,128,1792]{2,1,0:T(8,128)(2,1)} %get-tuple-element.67.refs_2_, ...), custom_call_target="tpu_custom_call" | custom-call | tf_op jit(solution)/shard_map/assemble/pallas_call | solution.py:565
  517.0 0.0 copy-done.1
  517.0 0.8 copy.36
  517.8 0.0 copy-done
  517.8 1.0 copy.37
  (5 shorter events, 0.0 us)
Async XLA Ops:
  502.7 14.3 %copy-start.1 = (bf16[128,2048]{1,0:T(8,128)(2,1)S(1)}, bf16[128,2048]{1,0:T(8,128)(2,1)}, u32[]{:S(2)}) copy-start(bf16[128,2048]{1,0:T(8,128)(2,1)} %get-tuple-element.51) | copy-start | bytes 1572868
  502.7 15.1 %copy-start = (f32[128,2048]{1,0:T(8,128)S(1)}, f32[128,2048]{1,0:T(8,128)}, u32[]{:S(2)}) copy-start(f32[128,2048]{1,0:T(8,128)} %get-tuple-element.63) | copy-start | bytes 3145732

commit v6 on v5

--- a/solution.py
+++ b/solution.py
@@ -989,7 +989,7 @@
         out_owned,
         second_held, grad_held, in_held, down_held, act, grad_gu, weights, dots, dots_in, gain_sum,
         logit_low,
-        back_parts, ffn_parts, dot_sends, dot_arrivals, loads, weight_loads, stores, *scratch,
+        back_parts, ffn_parts, dot_sends, dot_arrivals, loads, row_loads, weight_loads, stores, *scratch,
     ):
         back = Reduce(back_parts, back_parts, *scratch[:5])
         ahead = Reduce(ffn_parts, ffn_parts, *scratch[5:10])
@@ -1002,12 +1002,22 @@
         own, other = back.places
         me = own[0]
         peers = [lax.rem(me + k, N_CTX) for k in range(1, N_CTX)]
-        copies = [
-            pltpu.make_async_copy(source, target, loads.at[k])
-            for k, (source, target) in enumerate(((second, second_held), (grad_out, grad_held)))
-        ]
-        for copy in copies:
-            copy.start()
+
+        def start_of(b):
+            ahead = 2 - b + 3 * (b // 2) - 2 * (b // 3)
+            return pl.multiple_of(lax.rem(me // 2 + ahead, N_CTX // 2) * pair, pair)
+
+        def row_copies(b):
+            there = pl.ds(start_of(b) // rows, 2)
+            return [
+                pltpu.make_async_copy(source.at[there], target.at[there], row_loads.at[2 * b + k])
+                for k, (source, target) in enumerate(((second, second_held), (grad_out, grad_held)))
+            ]
+
+        def start_rows(b, carry):
+            for copy in row_copies(b):
+                copy.start()
+            return carry
 
         def weight_copies(t):
             copies = []
@@ -1025,7 +1035,10 @@
                 copy.start()
             return carry
 
-        lax.fori_loop(0, hidden // tile, start_weights, 0)
+        start_rows(0, 0)
+        start_weights(0, 0)
+        lax.fori_loop(1, N_CTX // 2, start_rows, 0)
+        lax.fori_loop(1, hidden // tile, start_weights, 0)
         plane_peers = [sums.peer(p) for p in (sums.up, sums.down, sums.other)]
         greet([{"ctx": p} for p in peers] + plane_peers + [exchange.mate])
         logit_low[...] = jnp.zeros_like(logit_low)
@@ -1036,9 +1049,6 @@
             part = jnp.concatenate([held[2 : 3 + EXPERTS], jnp.zeros((15 - EXPERTS, 128), f32)], axis=0)
             logit_low[0:16, 128 * s : 128 * (s + 1)] = part.astype(bf16)
         gain = jnp.concatenate(gains, axis=1)
-        for copy in copies:
-            copy.wait()
-
         def stored(slot, start):
             there = pl.ds(start, pair)
             return [
@@ -1055,10 +1065,6 @@
                 dots.at[place], dots_in.at[slot], dot_sends, dot_arrivals, slot, {"ctx": place}
             )
 
-        def start_of(b):
-            ahead = 2 - b + 3 * (b // 2) - 2 * (b // 3)
-            return pl.multiple_of(lax.rem(me // 2 + ahead, N_CTX // 2) * pair, pair)
-
         def branch_of(j):
             at = me * (hidden // LANE) + j
             routed = (at // SHARED_BLOCKS + 1) // 2
@@ -1069,6 +1075,8 @@
             start = start_of(b)
             slot = 0
             first = pl.multiple_of(start // rows, 2)
+            for copy in row_copies(b):
+                copy.wait()
 
             @pl.when(b >= 1)
             def _():
@@ -1294,6 +1302,7 @@
             pltpu.SemaphoreType.DMA((N_CTX - 1,)),
             pltpu.SemaphoreType.DMA((N_CTX - 1,)),
             pltpu.SemaphoreType.DMA((3,)),
+            pltpu.SemaphoreType.DMA((N_CTX,)),
             pltpu.SemaphoreType.DMA((3 * hidden // tile,)),
             pltpu.SemaphoreType.DMA((1, 3)),
         ]

time: 520 us -> 519 us (level)
  no operation moved by 1% of the time
where the time goes in v6:
time: 519 us; the launch traced here: 518 us
  Pallas kernels  497 us (96%)
  local copies, waits for them, and re-layouts  10.4 us (2%)
  other arithmetic  9.35 us (2%)
    pallas_call x1, Pallas kernels, backward(): pl.pallas_call(kernel, out_shape=(jax.ShapeDtypeStruct((rows, width), f32...  196 us
    pallas_call x1, Pallas kernels, front(): pl.pallas_call(kernel, out_shape=(shape(rows, width, kind=f32), shape(N_C...  157 us
    pallas_call x1, Pallas kernels, feed_forward(): pl.pallas_call(kernel, out_shape=(jax.ShapeDtypeStruct((rows, width), f32...  129 us
    pallas_call x1, Pallas kernels, assemble(): pl.pallas_call(kernel, out_shape=(jax.ShapeDtypeStruct((rows, FOUT), f32)...  14.3 us

profile of v6, /device:TPU:2, one launch (start us, length us, event | category | flops | bytes accessed | tf_op | source)
XLA Modules:
  0.0 517.9 jit_solution(10238125822237330250)
XLA Ops:
  1.3 2.6 concatenate.7.small
  3.9 0.7 select_reduce_fusion
  4.7 0.1 dynamic-slice_bitcast_fusion
  4.7 0.6 fusion.11.query_pos
  5.3 0.8 convert_reduce_fusion
  6.2 0.7 copy.31.own_valid
  6.9 1.9 pad_maximum_fusion.block
  8.8 0.2 copy.30
  9.0 0.9 compare_select_fusion.key_pos
  9.9 3.0 fusion
  13.0 157.2 %front.1 = (f32[128,2048]{1,0:T(8,128)}, bf16[8,128,2048]{2,1,0:T(8,128)(2,1)}, bf16[8,128,2048]{2,1,0:T(8,128)(2,1)}, bf16[8,2,128,768]{3,2,1,0:T(8,128)(2,1)},...) custom-call(bf16[128,2176]{1,0:T(8,128)(2,1)} %pad_maximum_fusion.bl, ...), custom_call_target="tpu_custom_call" | custom-call | tf_op jit(solution)/shard_map/front/pallas_call | solution.py:841
  170.2 128.9 %feed_forward.1 = (f32[128,2048]{1,0:T(8,128)}, bf16[128,2048]{1,0:T(8,128)(2,1)}, bf16[128,2048]{1,0:T(8,128)(2,1)}, bf16[128,2048]{1,0:T(8,128)(2,1)}, f32[1,2...) custom-call(bf16[8,128,2048]{2,1,0:T(8,128)(2,1)} %get-tuple-element, ...), custom_call_target="tpu_custom_call" | custom-call | tf_op jit(solution)/shard_map/feed_forward/pallas_call | solution.py:1273
  299.1 1.4 bitcast_convert_fusion.gain
  300.4 196.5 %backward.1 = (f32[128,2048]{1,0:T(8,128)}, f32[16,128]{1,0:T(8,128)}, bf16[8,128,1792]{2,1,0:T(8,128)(2,1)}, bf16[8,128,1792]{2,1,0:T(8,128)(2,1)}, bf16[8,128,...) custom-call(bf16[128,2048]{1,0:T(8,128)(2,1)} %get-tuple-element.52.own, ...), custom_call_target="tpu_custom_call" | custom-call | tf_op jit(solution)/shard_map/backward/pallas_call | solution.py:1701
  496.9 1.2 slice_bitcast_fusion.2
  498.1 1.2 slice.24
  499.3 1.3 slice_bitcast_fusion.1
  500.6 1.3 slice_bitcast_fusion
  501.8 0.0 copy-start.1
  501.8 0.0 copy-start
  501.8 14.3 %assemble.1 = (f32[128,14080]{1,0:T(8,128)}, f32[128,28160]{1,0:T(8,128)}, f32[128,2048]{1,0:T(8,128)}, f32[128,6144]{1,0:T(8,128)}) custom-call(bf16[8,128,1792]{2,1,0:T(8,128)(2,1)} %get-tuple-element.65.refs_0_, bf16[8,128,1792]{2,1,0:T(8,128)(2,1)} %get-tuple-element.66.refs_1_, bf16[8,128,1792]{2,1,0:T(8,128)(2,1)} %get-tuple-element.67.refs_2_, ...), custom_call_target="tpu_custom_call" | custom-call | tf_op jit(solution)/shard_map/assemble/pallas_call | solution.py:565
  516.1 0.0 copy-done.1
  516.1 0.8 copy.36
  516.9 0.0 copy-done
  516.9 1.0 copy.37
  (5 shorter events, 0.0 us)
Async XLA Ops:
  501.8 14.3 %copy-start.1 = (bf16[128,2048]{1,0:T(8,128)(2,1)S(1)}, bf16[128,2048]{1,0:T(8,128)(2,1)}, u32[]{:S(2)}) copy-start(bf16[128,2048]{1,0:T(8,128)(2,1)} %get-tuple-element.51) | copy-start | bytes 1572868
  501.8 15.1 %copy-start = (f32[128,2048]{1,0:T(8,128)S(1)}, f32[128,2048]{1,0:T(8,128)}, u32[]{:S(2)}) copy-start(f32[128,2048]{1,0:T(8,128)} %get-tuple-element.63) | copy-start | bytes 3145732
